TPU v7x, 128 devices: a whole 4x4x4 slice. The times are simulated.
128 devices in a mesh: rep: 4 (over x), ten: 32 (over y, z, core).
Axes of the slice: x: 4, y: 4, z: 4, core: 2. Of those that a mesh axis runs over, the one named last changes fastest.
Arguments:
- amplitudes: bfloat16 [32, 32, 1024, 128], P('ten', 'rep'), may hold values from -6 to 6
- integrals: bfloat16 [32, 1024, 32, 128], P('rep', 'ten'), may hold values from -0.125 to 0.125
- pair_irreps: int32 [2], replicated, may hold values from 0 to 7
Outputs:
- cycle: bfloat16 [32, 32, 1024, 128], P('ten', 'rep')
All inputs are finite; a program needn't handle non-finite values.
Results may differ from a plain program's by a relative error of at most 0.001.
Values may be sent and summed in bfloat16 or wider, within the bound.
No kernel may reach another device: no remote copies, remote signals or barrier semaphores. Data moves between devices by JAX's collectives and lax.ppermute only.
A program may use at most 192 MiB of HBM per device.

v0:
```python
import jax
import jax.numpy as jnp
from jax import lax
from jax.sharding import PartitionSpec as P


def partner(array, axis, distance):
    return lax.ppermute(array, axis, [(i, i ^ 1 << distance) for i in range(lax.axis_size(axis))])


def cycle_block(amp_rows, chosen):
    return jnp.einsum("ikac,kcjb->ijab", amp_rows, chosen, preferred_element_type=jnp.float32)


def fetch_block(held_rows, pair_xor, block_rows):
    rows_here = held_rows.shape[1]
    position = lax.axis_index("ten")
    devices_per_irrep = block_rows // rows_here
    low_bits = devices_per_irrep.bit_length() - 1
    for bit_index in range(3):
        crossed = partner(held_rows, "ten", low_bits + bit_index)
        flipped = jnp.bitwise_and(jnp.right_shift(pair_xor, bit_index), 1) == 1
        held_rows = jnp.where(flipped, crossed, held_rows)
    for bit_index in range(low_bits):
        partner_rows = partner(held_rows, "ten", bit_index)
        upper_half = jnp.bitwise_and(jnp.right_shift(position, bit_index), 1) == 1
        held_rows = jnp.where(
            upper_half,
            jnp.concatenate([partner_rows, held_rows], axis=1),
            jnp.concatenate([held_rows, partner_rows], axis=1),
        )
    return held_rows


def per_device(amplitudes, integrals, pair_irreps):
    pair_xor = jnp.bitwise_xor(pair_irreps[0], pair_irreps[1])
    block_rows = amplitudes.shape[3]
    moved_amps = lax.all_to_all(amplitudes, "ten", split_axis=2, concat_axis=0, tiled=True)
    chosen = fetch_block(integrals, pair_xor, block_rows)
    partial_value = cycle_block(moved_amps, chosen)
    summed = lax.psum_scatter(partial_value, "rep", scatter_dimension=1, tiled=True).astype(
        jnp.bfloat16
    )
    return lax.all_to_all(summed, "ten", split_axis=0, concat_axis=2, tiled=True)


def solution(mesh):
    in_specs = (P("ten", "rep", None, None), P("rep", "ten", None, None), P())
    out_specs = P("ten", "rep", None, None)
    return jax.shard_map(
        per_device, mesh=mesh, in_specs=in_specs, out_specs=out_specs, check_vma=False
    )
```

profile of v0, /device:TPU:0, one launch (start us, length us, event | category | flops | bytes accessed | tf_op | source)
XLA Modules:
  0.0 491.2 jit_solution(10126267153176389665)
XLA Ops:
  6.5 4.0 collective-permute-start
  10.5 1.3 fusion.4
  13.1 43.2 %collective-permute-done = bf16[8,32,32,128]{3,2,1,0:T(8,128)(2,1)S(1)} collective-permute-done((bf16[8,32,32,128]{3,2,1,0:T(8,128)(2,1)}, bf16[8,32,32,128]{3,2,1,0:T(8,128)(2,1)S(1)}, u32[]{:S(2)}, u32[]{:S(2)}) %collective-permute-start) | collective-permute-done | bytes 2097184 | tf_op jit(solution)/shard_map/ppermute | solution.py:8
  56.3 0.2 broadcast_select_fusion
  56.6 1.7 collective-permute-start.1
  58.2 45.2 %collective-permute-done.1 = bf16[8,32,32,128]{3,2,1,0:T(8,128)(2,1)S(1)} collective-permute-done((bf16[8,32,32,128]{3,2,1,0:T(8,128)(2,1)S(1)}, bf16[8,32,32,128]{3,2,1,0:T(8,128)(2,1)S(1)}, u32[]{:S(2)}, u32[]{:S(2)}) %collective-permute-start.1) | collective-permute-done | bytes 2097184 | tf_op jit(solution)/shard_map/ppermute | solution.py:8
  103.5 0.2 broadcast_select_fusion.1
  103.7 3.3 collective-permute-start.2
  106.9 44.2 %collective-permute-done.2 = bf16[8,32,32,128]{3,2,1,0:T(8,128)(2,1)S(1)} collective-permute-done((bf16[8,32,32,128]{3,2,1,0:T(8,128)(2,1)S(1)}, bf16[8,32,32,128]{3,2,1,0:T(8,128)(2,1)S(1)}, u32[]{:S(2)}, u32[]{:S(2)}) %collective-permute-start.2) | collective-permute-done | bytes 2097184 | tf_op jit(solution)/shard_map/ppermute | solution.py:8
  151.2 0.2 broadcast_select_fusion.2
  151.4 0.1 collective-permute-start.3
  151.5 4.3 collective-permute-done.3
  155.7 4.4 maximum_select_fusion.1
  160.1 0.7 collective-permute-start.4
  160.8 2.7 copy.12
  163.4 7.9 %all-to-all-start = ((bf16[1,8,1024,128]{3,1,0,2:T(8,128)(2,1)}), bf16[1,8,1024,128]{3,1,0,2:T(8,128)(2,1)S(1)}, u32[]{:S(2)}, u32[]{:S(2)}) async-start(bf16[1,8,1024,128]{3,1,0,2:T(8,128)(2,1)} %copy.12), calls=%async_computation | async-start | bytes 4194304 | tf_op jit(solution)/shard_map/all_to_all | solution.py:38
  171.4 99.3 %collective-permute-done.4 = bf16[8,64,32,128]{3,2,1,0:T(8,128)(2,1)} collective-permute-done((bf16[8,64,32,128]{3,2,1,0:T(8,128)(2,1)}, bf16[8,64,32,128]{3,2,1,0:T(8,128)(2,1)}, u32[]{:S(2)}, u32[]{:S(2)}) %collective-permute-start.4) | collective-permute-done | bytes 4194336 | tf_op jit(solution)/shard_map/ppermute | solution.py:8
  270.7 10.4 %fusion = bf16[8,128,32,128,1]{3,2,1,0,4:T(8,128)(2,1)} fusion(bf16[8,64,32,128]{3,2,1,0:T(8,128)(2,1)} %maximum_select_fusion.1, bf16[8,64,32,128]{3,2,1,0:T(8,128)(2,1)} %collective-permute-done.4, pred[]{:T(512)S(6)} %eq.24), kind=kLoop, calls=%fused_computation.2 | loop fusion | flops 12582912 | bytes 16777216 | tf_op jit(solution)/shard_map/jit(_where)/select_n | solution.py:27
  281.1 13.9 %convolution_bitcast_fusion = f32[32,32,32,128]{3,2,0,1:T(8,128)} fusion(bf16[8,128,32,128,1]{3,2,1,0,4:T(8,128)(2,1)} %fusion, bf16[1,8,32,32,128]{4,1,3,2,0:T(8,128)(2,1)S(1)} %bitcast.23), kind=kOutput, calls=%fused_computation | convolution fusion | flops 8589934592 | bytes 27262976 | tf_op jit(solution)/shard_map/ikac,kcjb->ijab/dot_general | solution.py:12
  295.0 149.1 %reduce-scatter.2.cloned.1.call-done = f32[32,8,32,128]{3,2,0,1:T(8,128)} async-done(((f32[32,32,32,128]{3,2,0,1:T(8,128)}), f32[32,8,32,128]{3,2,0,1:T(8,128)}) %reduce-scatter.2.cloned.1.call-update) | async-done | bytes 4194320 | tf_op jit(solution)/shard_map/reduce_scatter | solution.py:41
  444.2 2.7 convert_element_type.3
  446.9 0.6 copy.16
  447.5 35.1 %all_to_all.36 = bf16[32,8,32,128]{3,2,1,0:T(8,128)(2,1)S(1)} all-to-all(bf16[32,8,32,128]{3,2,1,0:T(8,128)(2,1)S(1)} %copy.16), channel_id=1, replica_groups=mesh['rep'=4,'ten'=32] {'ten'}, dimensions={0} | all-to-all | bytes 4194304 | tf_op jit(solution)/shard_map/all_to_all | solution.py:44
  482.6 1.8 copy.17
  (5 shorter events, 0.1 us)
Async XLA Ops:
  6.5 49.8 %collective-permute-start = (bf16[8,32,32,128]{3,2,1,0:T(8,128)(2,1)}, bf16[8,32,32,128]{3,2,1,0:T(8,128)(2,1)S(1)}, u32[]{:S(2)}, u32[]{:S(2)}) collective-permute-start(bf16[8,32,32,128]{3,2,1,0:T(8,128)(2,1)} %param.4), channel_id=1, source_target_pairs={{0,4},{1,5},{2,6},{3,7},{4,0},{5,1},{6,2},{7,3},{8,12},{9,13},{10,... | collective-permute-start | bytes 6291464 | tf_op jit(solution)/shard_map/ppermute | solution.py:8
  56.6 46.9 %collective-permute-start.1 = (bf16[8,32,32,128]{3,2,1,0:T(8,128)(2,1)S(1)}, bf16[8,32,32,128]{3,2,1,0:T(8,128)(2,1)S(1)}, u32[]{:S(2)}, u32[]{:S(2)}) collective-permute-start(bf16[8,32,32,128]{3,2,1,0:T(8,128)(2,1)S(1)} %broadcast_select_fusion), channel_id=1, source_target_pairs={{0,8},{1,9},{2,10},{3,11},{4,12},{5,13},{6,14},{7,15},{8,0},{9,1},... | collective-permute-start | bytes 6291464 | tf_op jit(solution)/shard_map/ppermute | solution.py:8
  103.7 47.5 %collective-permute-start.2 = (bf16[8,32,32,128]{3,2,1,0:T(8,128)(2,1)S(1)}, bf16[8,32,32,128]{3,2,1,0:T(8,128)(2,1)S(1)}, u32[]{:S(2)}, u32[]{:S(2)}) collective-permute-start(bf16[8,32,32,128]{3,2,1,0:T(8,128)(2,1)S(1)} %broadcast_select_fusion.1), channel_id=1, source_target_pairs={{0,16},{1,17},{2,18},{3,19},{4,20},{5,21},{6,22},{7,23},{8,24},{9,... | collective-permute-start | bytes 6291464 | tf_op jit(solution)/shard_map/ppermute | solution.py:8
  151.4 4.4 collective-permute-start.3
  151.5 9.3 %copy-start = (bf16[1,8,1024,128]{3,2,1,0:T(8,128)(2,1)S(1)}, bf16[1,8,1024,128]{3,2,1,0:T(8,128)(2,1)}, u32[]{:S(2)}) copy-start(bf16[1,8,1024,128]{3,2,1,0:T(8,128)(2,1)} %param.3) | copy-start | bytes 6291460
  160.1 110.6 %collective-permute-start.4 = (bf16[8,64,32,128]{3,2,1,0:T(8,128)(2,1)}, bf16[8,64,32,128]{3,2,1,0:T(8,128)(2,1)}, u32[]{:S(2)}, u32[]{:S(2)}) collective-permute-start(bf16[8,64,32,128]{3,2,1,0:T(8,128)(2,1)} %maximum_select_fusion.1), channel_id=1, source_target_pairs={{0,2},{1,3},{2,0},{3,1},{4,6},{5,7},{6,4},{7,5},{8,10},{9,11},{10,... | collective-permute-start | bytes 12582920 | tf_op jit(solution)/shard_map/ppermute | solution.py:8
  163.4 117.6 %all-to-all-start = ((bf16[1,8,1024,128]{3,1,0,2:T(8,128)(2,1)}), bf16[1,8,1024,128]{3,1,0,2:T(8,128)(2,1)S(1)}, u32[]{:S(2)}, u32[]{:S(2)}) async-start(bf16[1,8,1024,128]{3,1,0,2:T(8,128)(2,1)} %copy.12), calls=%async_computation | async-start | bytes 4194304 | tf_op jit(solution)/shard_map/all_to_all | solution.py:38
  171.3 272.9 %reduce-scatter.2.cloned.1.call-start = ((), (), s32[]{:S(2)}) async-start(), calls=%async_computation.3 | async-start | bytes 20971520 | tf_op jit(solution)/shard_map/reduce_scatter | solution.py:41
Sparse Core Ops, SparseCore 0:
  295.2 148.9 reduce-scatter.1
where the time goes:
time: 493 us; the launch traced here: 491 us
  waiting for transfers between devices  385 us (78%)
  blocking collectives  35.1 us (7%)
  other arithmetic  18.1 us (4%)
  starting transfers between devices  17.5 us (4%)
  between operations  14.7 us (3%)
  matrix products  13.9 us (3%)
  local copies, waits for them, and re-layouts  6.37 us (1%)
    ppermute x5, waiting for transfers between devices, partner(): lax.ppermute(array, axis, [(i, i ^ 1 << distance) for i in range(lax.axis...  236 us
    reduce_scatter x1, waiting for transfers between devices, per_device(): lax.psum_scatter(partial_value, 'rep', scatter_dimension=1, tiled=True)  149 us
    all_to_all x1, blocking collectives, per_device(): lax.all_to_all(summed, 'ten', split_axis=0, concat_axis=2, tiled=True)  35.1 us
    select_n x2, other arithmetic, fetch_block(): jnp.where(upper_half, jnp.concatenate([partner_rows, held_rows], axis=1),...  14.7 us
    dot_general x1, matrix products, cycle_block(): jnp.einsum('ikac,kcjb->ijab', amp_rows, chosen, preferred_element_type=jn...  13.9 us
  transfers between devices with their start and end apart: 7, of which 6 were waited for; matrix products, arithmetic and copies ran while one was open for 3% of the time, Pallas kernels for 0%

commit v1 on v0

v1 whole, which is shorter than its diff:
```python
import jax
import jax.numpy as jnp
from jax import lax
from jax.sharding import PartitionSpec as P

IRREPS = 8
CHUNKS = 4


def shift_rep(array, distance):
    n = lax.axis_size("rep")
    return lax.ppermute(array, "rep", [(s, (s + distance) % n) for s in range(n)])


def flip_ten(array, mask):
    return lax.ppermute(array, "ten", [(s, s ^ mask) for s in range(lax.axis_size("ten"))])


def exchange_irreps(array, groups):
    return lax.all_to_all(
        array, "ten", split_axis=0, concat_axis=0, axis_index_groups=groups, tiled=True
    )


def gather_rep(block):
    half = block.shape[0] // 2
    from_left = shift_rep(block, 1)
    from_right = shift_rep(block, -1)
    far = jnp.concatenate([shift_rep(from_left[:half], 1), shift_rep(from_right[half:], -1)], axis=0)
    return jnp.concatenate([block, from_left, from_right, far], axis=1)


def per_device(amplitudes, integrals, pair_irreps):
    pair_xor = jnp.bitwise_xor(pair_irreps[0], pair_irreps[1])
    ten = lax.axis_size("ten")
    quarters = ten // IRREPS
    groups = [[g * quarters + q for g in range(IRREPS)] for q in range(quarters)]
    column = lax.axis_index("rep")
    ranks = lax.axis_size("rep")
    quarter = lax.axis_index("ten") % quarters

    nk, rows, js = amplitudes.shape[1], amplitudes.shape[3], integrals.shape[2] // ranks
    amps = amplitudes.reshape(nk, IRREPS, rows, rows)
    order = jnp.bitwise_xor(jnp.arange(IRREPS), pair_xor)
    by_group = jnp.take(amps.transpose(1, 0, 2, 3), order, axis=0)

    by_j = integrals.transpose(2, 0, 1, 3)

    def j_block(distance):
        return lax.dynamic_slice_in_dim(by_j, ((column + distance) % ranks) * js, js, 0)

    pieces = [j_block(0), shift_rep(j_block(1), 1), shift_rep(j_block(3), -1), shift_rep(j_block(2), 2)]
    held = jnp.concatenate(pieces, axis=1)
    other = flip_ten(held, 2)
    upper = (quarter // 2) == 1
    pair = jnp.stack([jnp.where(upper, other, held), jnp.where(upper, held, other)], axis=2)
    across = flip_ten(pair, 1)
    odd = (quarter % 2) == 1
    block = jnp.stack([jnp.where(odd, across, pair), jnp.where(odd, pair, across)], axis=3)
    chosen = block.reshape(js, nk * ranks, rows, rows)

    mine = exchange_irreps(by_group, groups)
    step = rows // CHUNKS
    outs = []
    for chunk in range(CHUNKS):
        part = gather_rep(mine[:, :, chunk * step:(chunk + 1) * step])
        sums = jnp.einsum("ikac,jkcb->ijab", part, chosen, preferred_element_type=jnp.float32)
        outs.append(exchange_irreps(sums.astype(jnp.bfloat16), groups))
    result = jnp.take(jnp.concatenate(outs, axis=2), order, axis=0)
    return result.transpose(1, 0, 2, 3).reshape(amplitudes.shape)


def solution(mesh):
    in_specs = (P("ten", "rep", None, None), P("rep", "ten", None, None), P())
    return jax.shard_map(
        per_device, mesh=mesh, in_specs=in_specs, out_specs=in_specs[0], check_vma=False
    )
```

time: 493 us -> 279 us (0.57)
  waiting for transfers between devices: 385 us -> 96.6 us
  starting transfers between devices: 17.5 us -> 48.6 us
  local copies, waits for them, and re-layouts: 6.37 us -> 34.7 us
  blocking collectives: 35.1 us -> 49.5 us
  between operations: 14.7 us -> 1.69 us
  matrix products: 13.9 us -> 23.9 us
    reduce_scatter x1 -> x0, waiting for transfers between devices: 149 us -> none  [per_device(): lax.psum_scatter(partial_value, 'rep', scatter_dimension=1, tiled=True)]
    ppermute x5 -> x21, waiting for transfers between devices: 236 us -> 90.5 us  [the longest x19 45.4 us: shift_rep(): lax.ppermute(array, 'rep', [(s, (s + distance) % n) for s in range(n)])]
    ppermute x5 -> x21, starting transfers between devices: 9.64 us -> 33.5 us  [the longest x19 31.5 us: shift_rep(): lax.ppermute(array, 'rep', [(s, (s + distance) % n) for s in range(n)])]
    another operation x0 -> x4, other arithmetic: none -> 16 us  [the longest x2 10.7 us: per_device(): jnp.stack([jnp.where(odd, across, pair), jnp.where(odd, pair, across)], a...]
    all_to_all x1 -> x2, blocking collectives: 35.1 us -> 49.5 us  [exchange_irreps(): lax.all_to_all(array, 'ten', split_axis=0, concat_axis=0, axis_index_grou...]
    select_n x5 -> x2, other arithmetic: 15.4 us -> 1.86 us  [the longest x1 1.85 us: per_device(): by_group = jnp.take(amps.transpose(1, 0, 2, 3), order, axis=0)]
    slice x0 -> x9, local copies, waits for them, and re-layouts: none -> 13.2 us  [the longest x4 6.7 us: gather_rep(): from_right[half:]]
    dot_general x1 -> x4, matrix products: 13.9 us -> 23.9 us  [per_device(): jnp.einsum('ikac,jkcb->ijab', part, chosen, preferred_element_type=jnp.fl...]
  transfers between devices with their start and end apart: 7 -> 24, of which waited for: 6 -> 10; matrix products, arithmetic and copies ran while one was open for 3% -> 23% of each run, Pallas kernels for 0% -> 0%
where the time goes in v1:
time: 279 us; the launch traced here: 278 us
  waiting for transfers between devices  96.6 us (35%)
  blocking collectives  49.5 us (18%)
  starting transfers between devices  48.6 us (17%)
  local copies, waits for them, and re-layouts  34.7 us (12%)
  matrix products  23.9 us (9%)
  other arithmetic  22.8 us (8%)
    all_to_all x2, blocking collectives, exchange_irreps(): lax.all_to_all(array, 'ten', split_axis=0, concat_axis=0, axis_index_grou...  49.5 us
    ppermute x19, waiting for transfers between devices, shift_rep(): lax.ppermute(array, 'rep', [(s, (s + distance) % n) for s in range(n)])  45.4 us
    ppermute x2, waiting for transfers between devices, flip_ten(): lax.ppermute(array, 'ten', [(s, s ^ mask) for s in range(lax.axis_size('t...  45.1 us
    ppermute x19, starting transfers between devices, shift_rep(): lax.ppermute(array, 'rep', [(s, (s + distance) % n) for s in range(n)])  31.5 us
    dot_general x4, matrix products, per_device(): jnp.einsum('ikac,jkcb->ijab', part, chosen, preferred_element_type=jnp.fl...  23.9 us
    all_to_all x3, starting transfers between devices, exchange_irreps(): lax.all_to_all(array, 'ten', split_axis=0, concat_axis=0, axis_index_grou...  15.2 us
    another operation x2, other arithmetic, per_device(): jnp.stack([jnp.where(odd, across, pair), jnp.where(odd, pair, across)], a...  10.7 us
    another operation x1, local copies, waits for them, and re-layouts, per_device(): jnp.stack([jnp.where(odd, across, pair), jnp.where(odd, pair, across)], a...  9.09 us
  transfers between devices with their start and end apart: 24, of which 10 were waited for; matrix products, arithmetic and copies ran while one was open for 23% of the time, Pallas kernels for 0%

profile of v1, /device:TPU:0, one launch (start us, length us, event | category | flops | bytes accessed | tf_op | source)
XLA Modules:
  0.0 277.8 jit_solution(10039982824615203665)
XLA Ops:
  7.1 9.6 %collective-permute-done = bf16[8,8,32,128]{3,0,2,1:T(8,128)(2,1)S(1)} collective-permute-done((bf16[8,8,32,128]{3,0,2,1:T(8,128)(2,1)S(1)}, bf16[8,8,32,128]{3,0,2,1:T(8,128)(2,1)S(1)}, u32[]{:S(2)}, u32[]{:S(2)}) %collective-permute-start) | collective-permute-done | bytes 524320 | tf_op jit(solution)/shard_map/ppermute | solution.py:12
  18.4 10.8 %collective-permute-done.2 = bf16[8,8,32,128]{3,0,2,1:T(8,128)(2,1)S(1)} collective-permute-done((bf16[8,8,32,128]{3,0,2,1:T(8,128)(2,1)S(1)}, bf16[8,8,32,128]{3,0,2,1:T(8,128)(2,1)S(1)}, u32[]{:S(2)}, u32[]{:S(2)}) %collective-permute-start.2) | collective-permute-done | bytes 524320 | tf_op jit(solution)/shard_map/ppermute | solution.py:12
  32.6 45.1 %collective-permute-done.3 = bf16[8,32,32,128]{3,0,2,1:T(8,128)(2,1)} collective-permute-done((bf16[8,32,32,128]{3,0,2,1:T(8,128)(2,1)}, bf16[8,32,32,128]{3,0,2,1:T(8,128)(2,1)}, u32[]{:S(2)}, u32[]{:S(2)}) %collective-permute-start.3) | collective-permute-done | bytes 2097184 | tf_op jit(solution)/shard_map/ppermute | solution.py:16
  89.6 36.2 %all_to_all.25 = bf16[8,8,128,128]{3,2,1,0:T(8,128)(2,1)S(1)} all-to-all(bf16[8,8,128,128]{3,2,1,0:T(8,128)(2,1)S(1)} %broadcast_select_fusion), channel_id=1, replica_groups={{0,4,8,12,16,20,24,28},{1,5,9,13,17,21,25,29},{2,6,10,14,18,22,26,30},{..., dimensions={0} | all-to-all | bytes 4194304 | tf_op jit(solution)/shard_map/all_to_all | solution.py:20
  129.5 3.2 %collective-permute-start.10 = (bf16[8,8,32,128]{3,2,1,0:T(8,128)(2,1)S(1)}, bf16[8,8,32,128]{3,2,1,0:T(8,128)(2,1)S(1)}, u32[]{:S(2)}, u32[]{:S(2)}) collective-permute-start(bf16[8,8,32,128]{3,2,1,0:T(8,128)(2,1)S(1)} %get-tuple-element.13), channel_id=1, source_target_pairs={{0,96},{32,0},{64,32},{96,64},{1,97},{33,1},{65,33},{97,65},{2,98}... | collective-permute-start | bytes 1572872 | tf_op jit(solution)/shard_map/ppermute | solution.py:12
  132.8 9.6 %collective-permute-done.5 = bf16[8,8,32,128]{3,2,1,0:T(8,128)(2,1)S(1)} collective-permute-done((bf16[8,8,32,128]{3,2,1,0:T(8,128)(2,1)S(1)}, bf16[8,8,32,128]{3,2,1,0:T(8,128)(2,1)S(1)}, u32[]{:S(2)}, u32[]{:S(2)}) %collective-permute-start.5) | collective-permute-done | bytes 524320 | tf_op jit(solution)/shard_map/ppermute | solution.py:12
  145.6 8.0 %collective-permute-done.9 = bf16[8,8,32,128]{3,2,1,0:T(8,128)(2,1)S(1)} collective-permute-done((bf16[8,8,32,128]{3,2,1,0:T(8,128)(2,1)S(1)}, bf16[8,8,32,128]{3,2,1,0:T(8,128)(2,1)S(1)}, u32[]{:S(2)}, u32[]{:S(2)}) %collective-permute-start.9) | collective-permute-done | bytes 524320 | tf_op jit(solution)/shard_map/ppermute | solution.py:12
  153.6 3.3 %collective-permute-start.18 = (bf16[8,8,32,128]{3,2,1,0:T(8,128)(2,1)S(1)}, bf16[8,8,32,128]{3,2,1,0:T(8,128)(2,1)}, u32[]{:S(2)}, u32[]{:S(2)}) collective-permute-start(bf16[8,8,32,128]{3,2,1,0:T(8,128)(2,1)S(1)} %get-tuple-element.11), channel_id=1, source_target_pairs={{0,96},{32,0},{64,32},{96,64},{1,97},{33,1},{65,33},{97,65},{2,98}... | collective-permute-start | bytes 1572872 | tf_op jit(solution)/shard_map/ppermute | solution.py:12
  166.6 3.2 %collective-permute-start.8 = (bf16[4,8,32,128]{3,2,1,0:T(8,128)(2,1)}, bf16[4,8,32,128]{3,2,1,0:T(8,128)(2,1)}, u32[]{:S(2)}, u32[]{:S(2)}) collective-permute-start(bf16[4,8,32,128]{3,2,1,0:T(8,128)(2,1)} %slice.62), channel_id=1, source_target_pairs={{0,96},{32,0},{64,32},{96,64},{1,97},{33,1},{65,33},{97,65},{2,98}... | collective-permute-start | bytes 786440 | tf_op jit(solution)/shard_map/ppermute | solution.py:12
  171.5 4.6 %collective-permute-done.17 = bf16[8,8,32,128]{3,2,1,0:T(8,128)(2,1)} collective-permute-done((bf16[8,8,32,128]{3,2,1,0:T(8,128)(2,1)S(1)}, bf16[8,8,32,128]{3,2,1,0:T(8,128)(2,1)}, u32[]{:S(2)}, u32[]{:S(2)}) %collective-permute-start.17) | collective-permute-done | bytes 524320 | tf_op jit(solution)/shard_map/ppermute | solution.py:12
  177.2 3.3 %collective-permute-start.12 = (bf16[4,8,32,128]{3,2,1,0:T(8,128)(2,1)}, bf16[4,8,32,128]{3,2,1,0:T(8,128)(2,1)}, u32[]{:S(2)}, u32[]{:S(2)}) collective-permute-start(bf16[4,8,32,128]{3,2,1,0:T(8,128)(2,1)} %slice.65), channel_id=1, source_target_pairs={{0,96},{32,0},{64,32},{96,64},{1,97},{33,1},{65,33},{97,65},{2,98}... | collective-permute-start | bytes 786440 | tf_op jit(solution)/shard_map/ppermute | solution.py:12
  182.4 4.5 %select_bitcast_fusion.1 = (bf16[8,32,2,1,32,128]{5,0,4,1,2,3:T(8,128)(2,1)S(1)}, bf16[8,32,2,1,32,128]{5,0,4,1,2,3:T(8,128)(2,1)}) fusion(bf16[8,32,2,32,128]{4,0,3,1,2:T(8,128)(2,1)} %collective-permute-done.4, pred[]{:T(512)S(6)} %eq.13, bf16[8,32,1,32,128]{4,0,3,1,2:T(8,128)(2,1)} %copy-done.4, bf16[8,32,1,32,128]{4,0,3,1,2:T(8,128)(2,1)S(1)} %copy-done.3), kind=kLoop, calls=%fused_computation.5 | loop fusion | flops 6291456 | bytes 16777216 | tf_op jit(solution)/shard_map/stack | solution.py:59
  186.9 6.2 %pad_maximum_fusion = bf16[8,32,2,2,32,128]{5,0,4,1,2,3:T(8,128)(2,1)} fusion(bf16[8,32,2,1,32,128]{5,0,4,1,2,3:T(8,128)(2,1)} %get-tuple-element.7, bf16[8,32,2,1,32,128]{5,0,4,1,2,3:T(8,128)(2,1)S(1)} %get-tuple-element.6), kind=kLoop, calls=%fused_computation.2 | loop fusion | flops 4194304 | bytes 16777216 | tf_op jit(solution)/shard_map/stack | solution.py:59
  193.1 9.1 %copy.12 = bf16[8,32,2,2,32,128]{5,4,3,2,1,0:T(8,128)(2,1)} copy(bf16[8,32,2,2,32,128]{5,0,4,1,2,3:T(8,128)(2,1)} %pad_maximum_fusion) | data formatting | bytes 16777216 | tf_op jit(solution)/shard_map/stack | solution.py:59
  205.5 5.9 %fusion.47 = bf16[8,8,32,128]{3,2,0,1:T(8,128)(2,1)S(1)} fusion(bf16[8,32,128,128,1]{3,2,1,4,0:T(8,128)(2,1)} %bitcast.105, bf16[4,8,32,128]{3,2,1,0:T(8,128)(2,1)} %collective-permute-done.8, bf16[4,8,32,128]{3,2,1,0:T(8,128)(2,1)} %collective-permute-done.7, bf16[8,8,32,128]{3,2,1,0:T(8,128)(2,1)S(1)} %copy-done.25, ...), kind=kOutput, calls=%fused_computation.63 | convolution fusion | flops 2158231552 | bytes 11010048 | tf_op jit(solution)/shard_map/ikac,jkcb->ijab/dot_general | solution.py:67
  212.2 3.5 %all-to-all-start.1 = ((bf16[8,8,32,128]{3,2,1,0:T(8,128)(2,1)}), bf16[8,8,32,128]{3,2,1,0:T(8,128)(2,1)S(1)}, u32[]{:S(2)}, u32[]{:S(2)}) async-start(bf16[8,8,32,128]{3,2,1,0:T(8,128)(2,1)} %copy.13), calls=%async_computation.1 | async-start | bytes 1048576 | tf_op jit(solution)/shard_map/all_to_all | solution.py:20
  215.8 3.3 %collective-permute-start.20 = (bf16[4,8,32,128]{3,2,1,0:T(8,128)(2,1)S(1)}, bf16[4,8,32,128]{3,2,1,0:T(8,128)(2,1)}, u32[]{:S(2)}, u32[]{:S(2)}) collective-permute-start(bf16[4,8,32,128]{3,2,1,0:T(8,128)(2,1)S(1)} %copy-done.16), channel_id=1, source_target_pairs={{0,96},{32,0},{64,32},{96,64},{1,97},{33,1},{65,33},{97,65},{2,98}... | collective-permute-start | bytes 786440 | tf_op jit(solution)/shard_map/ppermute | solution.py:12
  219.1 5.8 %fusion.46 = bf16[8,8,32,128]{3,2,0,1:T(8,128)(2,1)S(1)} fusion(bf16[8,32,128,128,1]{3,2,1,4,0:T(8,128)(2,1)} %bitcast.106, bf16[4,8,32,128]{3,2,1,0:T(8,128)(2,1)} %collective-permute-done.12, bf16[4,8,32,128]{3,2,1,0:T(8,128)(2,1)} %collective-permute-done.11, bf16[8,8,32,128]{3,2,1,0:T(8,128)(2,1)S(1)} %copy-done.21, ...), kind=kOutput, calls=%fused_computation.62 | convolution fusion | flops 2158231552 | bytes 11010048 | tf_op jit(solution)/shard_map/ikac,jkcb->ijab/dot_general | solution.py:67
  225.7 7.1 %all-to-all-start.2 = ((bf16[8,8,32,128]{3,2,1,0:T(8,128)(2,1)}), bf16[8,8,32,128]{3,2,1,0:T(8,128)(2,1)S(1)}, u32[]{:S(2)}, u32[]{:S(2)}) async-start(bf16[8,8,32,128]{3,2,1,0:T(8,128)(2,1)} %copy.14), calls=%async_computation.2 | async-start | bytes 1048576 | tf_op jit(solution)/shard_map/all_to_all | solution.py:20
  232.9 6.2 %fusion.45 = bf16[8,8,32,128]{3,2,0,1:T(8,128)(2,1)S(1)} fusion(bf16[8,32,128,128,1]{3,2,1,4,0:T(8,128)(2,1)} %bitcast.107, bf16[4,8,32,128]{3,2,1,0:T(8,128)(2,1)} %collective-permute-done.16, bf16[4,8,32,128]{3,2,1,0:T(8,128)(2,1)} %collective-permute-done.15, bf16[8,8,32,128]{3,2,1,0:T(8,128)(2,1)} %collective-permute-done.14, ...), kind=kOutput, calls=%fused_computation.61 | convolution fusion | flops 2158231552 | bytes 11010048 | tf_op jit(solution)/shard_map/ikac,jkcb->ijab/dot_general | solution.py:67
  242.5 4.6 %all-to-all-start.3 = ((bf16[8,8,32,128]{3,2,1,0:T(8,128)(2,1)}), bf16[8,8,32,128]{3,2,1,0:T(8,128)(2,1)S(1)}, u32[]{:S(2)}, u32[]{:S(2)}) async-start(bf16[8,8,32,128]{3,2,1,0:T(8,128)(2,1)} %copy.15), calls=%async_computation.3 | async-start | bytes 1048576 | tf_op jit(solution)/shard_map/all_to_all | solution.py:20
  247.1 6.1 %fusion.44 = bf16[8,8,32,128]{3,2,0,1:T(8,128)(2,1)S(1)} fusion(bf16[8,32,128,128,1]{3,2,1,4,0:T(8,128)(2,1)} %bitcast.108, bf16[4,8,32,128]{3,2,1,0:T(8,128)(2,1)} %collective-permute-done.20, bf16[4,8,32,128]{3,2,1,0:T(8,128)(2,1)} %collective-permute-done.19, bf16[8,8,32,128]{3,2,1,0:T(8,128)(2,1)} %collective-permute-done.18, ...), kind=kOutput, calls=%fused_computation.60 | convolution fusion | flops 2158231552 | bytes 11010048 | tf_op jit(solution)/shard_map/ikac,jkcb->ijab/dot_general | solution.py:67
  253.2 3.5 %all-to-all-done.3 = bf16[8,8,32,128]{3,2,1,0:T(8,128)(2,1)S(1)} async-done(((bf16[8,8,32,128]{3,2,1,0:T(8,128)(2,1)}), bf16[8,8,32,128]{3,2,1,0:T(8,128)(2,1)S(1)}, u32[]{:S(2)}, u32[]{:S(2)}) %all-to-all-start.3) | async-done | bytes 524320 | tf_op jit(solution)/shard_map/all_to_all | solution.py:20
  257.6 13.3 %all_to_all.26 = bf16[8,8,32,128]{3,2,1,0:T(8,128)(2,1)S(1)} all-to-all(bf16[8,8,32,128]{3,2,1,0:T(8,128)(2,1)S(1)} %copy.16), channel_id=1, replica_groups={{0,4,8,12,16,20,24,28},{1,5,9,13,17,21,25,29},{2,6,10,14,18,22,26,30},{..., dimensions={0} | all-to-all | bytes 1048576 | tf_op jit(solution)/shard_map/all_to_all | solution.py:20
  (114 shorter events, 60.2 us)
Async XLA Ops:
  1.9 14.8 %collective-permute-start = (bf16[8,8,32,128]{3,0,2,1:T(8,128)(2,1)S(1)}, bf16[8,8,32,128]{3,0,2,1:T(8,128)(2,1)S(1)}, u32[]{:S(2)}, u32[]{:S(2)}) collective-permute-start(bf16[8,8,32,128]{3,0,2,1:T(8,128)(2,1)S(1)} %get-tuple-element.15), channel_id=1, source_target_pairs={{0,32},{32,64},{64,96},{96,0},{1,33},{33,65},{65,97},{97,1},{2,34}... | collective-permute-start | bytes 1572872 | tf_op jit(solution)/shard_map/ppermute | solution.py:12
  3.5 14.8 %collective-permute-start.1 = (bf16[8,8,32,128]{3,0,2,1:T(8,128)(2,1)S(1)}, bf16[8,8,32,128]{3,0,2,1:T(8,128)(2,1)S(1)}, u32[]{:S(2)}, u32[]{:S(2)}) collective-permute-start(bf16[8,8,32,128]{3,0,2,1:T(8,128)(2,1)S(1)} %get-tuple-element.17), channel_id=1, source_target_pairs={{0,96},{32,0},{64,32},{96,64},{1,97},{33,1},{65,33},{97,65},{2,98}... | collective-permute-start | bytes 1572872 | tf_op jit(solution)/shard_map/ppermute | solution.py:12
  5.2 23.9 %collective-permute-start.2 = (bf16[8,8,32,128]{3,0,2,1:T(8,128)(2,1)S(1)}, bf16[8,8,32,128]{3,0,2,1:T(8,128)(2,1)S(1)}, u32[]{:S(2)}, u32[]{:S(2)}) collective-permute-start(bf16[8,8,32,128]{3,0,2,1:T(8,128)(2,1)S(1)} %get-tuple-element.16), channel_id=1, source_target_pairs={{0,64},{32,96},{64,0},{96,32},{1,65},{33,97},{65,1},{97,33},{2,66}... | collective-permute-start | bytes 1572872 | tf_op jit(solution)/shard_map/ppermute | solution.py:12
  30.7 47.0 %collective-permute-start.3 = (bf16[8,32,32,128]{3,0,2,1:T(8,128)(2,1)}, bf16[8,32,32,128]{3,0,2,1:T(8,128)(2,1)}, u32[]{:S(2)}, u32[]{:S(2)}) collective-permute-start(bf16[8,32,32,128]{3,0,2,1:T(8,128)(2,1)} %pad_maximum_fusion.2), channel_id=1, source_target_pairs={{0,2},{1,3},{2,0},{3,1},{4,6},{5,7},{6,4},{7,5},{8,10},{9,11},{10,... | collective-permute-start | bytes 6291464 | tf_op jit(solution)/shard_map/ppermute | solution.py:16
  83.6 98.5 %collective-permute-start.4 = (bf16[8,32,2,32,128]{4,0,3,1,2:T(8,128)(2,1)}, bf16[8,32,2,32,128]{4,0,3,1,2:T(8,128)(2,1)}, u32[]{:S(2)}, u32[]{:S(2)}) collective-permute-start(bf16[8,32,2,32,128]{4,0,3,1,2:T(8,128)(2,1)} %pad_maximum_fusion.1), channel_id=1, source_target_pairs={{0,1},{1,0},{2,3},{3,2},{4,5},{5,4},{6,7},{7,6},{8,9},{9,8},{10,11... | collective-permute-start | bytes 12582920 | tf_op jit(solution)/shard_map/ppermute | solution.py:16
  126.2 16.1 %collective-permute-start.5 = (bf16[8,8,32,128]{3,2,1,0:T(8,128)(2,1)S(1)}, bf16[8,8,32,128]{3,2,1,0:T(8,128)(2,1)S(1)}, u32[]{:S(2)}, u32[]{:S(2)}) collective-permute-start(bf16[8,8,32,128]{3,2,1,0:T(8,128)(2,1)S(1)} %get-tuple-element.10), channel_id=1, source_target_pairs={{0,32},{32,64},{64,96},{96,0},{1,33},{33,65},{65,97},{97,1},{2,34}... | collective-permute-start | bytes 1572872 | tf_op jit(solution)/shard_map/ppermute | solution.py:12
  127.1 15.3 %collective-permute-start.6 = (bf16[8,8,32,128]{3,2,1,0:T(8,128)(2,1)S(1)}, bf16[8,8,32,128]{3,2,1,0:T(8,128)(2,1)S(1)}, u32[]{:S(2)}, u32[]{:S(2)}) collective-permute-start(bf16[8,8,32,128]{3,2,1,0:T(8,128)(2,1)S(1)} %get-tuple-element.10), channel_id=1, source_target_pairs={{0,96},{32,0},{64,32},{96,64},{1,97},{33,1},{65,33},{97,65},{2,98}... | collective-permute-start | bytes 1572872 | tf_op jit(solution)/shard_map/ppermute | solution.py:12
  129.5 24.1 %collective-permute-start.9 = (bf16[8,8,32,128]{3,2,1,0:T(8,128)(2,1)S(1)}, bf16[8,8,32,128]{3,2,1,0:T(8,128)(2,1)S(1)}, u32[]{:S(2)}, u32[]{:S(2)}) collective-permute-start(bf16[8,8,32,128]{3,2,1,0:T(8,128)(2,1)S(1)} %get-tuple-element.13), channel_id=1, source_target_pairs={{0,32},{32,64},{64,96},{96,0},{1,33},{33,65},{65,97},{97,1},{2,34}... | collective-permute-start | bytes 1572872 | tf_op jit(solution)/shard_map/ppermute | solution.py:12
  129.5 24.1 %collective-permute-start.10 = (bf16[8,8,32,128]{3,2,1,0:T(8,128)(2,1)S(1)}, bf16[8,8,32,128]{3,2,1,0:T(8,128)(2,1)S(1)}, u32[]{:S(2)}, u32[]{:S(2)}) collective-permute-start(bf16[8,8,32,128]{3,2,1,0:T(8,128)(2,1)S(1)} %get-tuple-element.13), channel_id=1, source_target_pairs={{0,96},{32,0},{64,32},{96,64},{1,97},{33,1},{65,33},{97,65},{2,98}... | collective-permute-start | bytes 1572872 | tf_op jit(solution)/shard_map/ppermute | solution.py:12
  142.4 22.6 %collective-permute-start.13 = (bf16[8,8,32,128]{3,2,1,0:T(8,128)(2,1)S(1)}, bf16[8,8,32,128]{3,2,1,0:T(8,128)(2,1)}, u32[]{:S(2)}, u32[]{:S(2)}) collective-permute-start(bf16[8,8,32,128]{3,2,1,0:T(8,128)(2,1)S(1)} %get-tuple-element.12), channel_id=1, source_target_pairs={{0,32},{32,64},{64,96},{96,0},{1,33},{33,65},{65,97},{97,1},{2,34}... | collective-permute-start | bytes 1572872 | tf_op jit(solution)/shard_map/ppermute | solution.py:12
  142.4 24.2 %collective-permute-start.14 = (bf16[8,8,32,128]{3,2,1,0:T(8,128)(2,1)S(1)}, bf16[8,8,32,128]{3,2,1,0:T(8,128)(2,1)}, u32[]{:S(2)}, u32[]{:S(2)}) collective-permute-start(bf16[8,8,32,128]{3,2,1,0:T(8,128)(2,1)S(1)} %get-tuple-element.12), channel_id=1, source_target_pairs={{0,96},{32,0},{64,32},{96,64},{1,97},{33,1},{65,33},{97,65},{2,98}... | collective-permute-start | bytes 1572872 | tf_op jit(solution)/shard_map/ppermute | solution.py:12
  153.6 22.6 %collective-permute-start.17 = (bf16[8,8,32,128]{3,2,1,0:T(8,128)(2,1)S(1)}, bf16[8,8,32,128]{3,2,1,0:T(8,128)(2,1)}, u32[]{:S(2)}, u32[]{:S(2)}) collective-permute-start(bf16[8,8,32,128]{3,2,1,0:T(8,128)(2,1)S(1)} %get-tuple-element.11), channel_id=1, source_target_pairs={{0,32},{32,64},{64,96},{96,0},{1,33},{33,65},{65,97},{97,1},{2,34}... | collective-permute-start | bytes 1572872 | tf_op jit(solution)/shard_map/ppermute | solution.py:12
  153.6 23.5 %collective-permute-start.18 = (bf16[8,8,32,128]{3,2,1,0:T(8,128)(2,1)S(1)}, bf16[8,8,32,128]{3,2,1,0:T(8,128)(2,1)}, u32[]{:S(2)}, u32[]{:S(2)}) collective-permute-start(bf16[8,8,32,128]{3,2,1,0:T(8,128)(2,1)S(1)} %get-tuple-element.11), channel_id=1, source_target_pairs={{0,96},{32,0},{64,32},{96,64},{1,97},{33,1},{65,33},{97,65},{2,98}... | collective-permute-start | bytes 1572872 | tf_op jit(solution)/shard_map/ppermute | solution.py:12
  164.9 37.3 %collective-permute-start.7 = (bf16[4,8,32,128]{3,2,1,0:T(8,128)(2,1)}, bf16[4,8,32,128]{3,2,1,0:T(8,128)(2,1)}, u32[]{:S(2)}, u32[]{:S(2)}) collective-permute-start(bf16[4,8,32,128]{3,2,1,0:T(8,128)(2,1)} %slice.61), channel_id=1, source_target_pairs={{0,32},{32,64},{64,96},{96,0},{1,33},{33,65},{65,97},{97,1},{2,34}... | collective-permute-start | bytes 786440 | tf_op jit(solution)/shard_map/ppermute | solution.py:12
  166.6 38.8 %collective-permute-start.8 = (bf16[4,8,32,128]{3,2,1,0:T(8,128)(2,1)}, bf16[4,8,32,128]{3,2,1,0:T(8,128)(2,1)}, u32[]{:S(2)}, u32[]{:S(2)}) collective-permute-start(bf16[4,8,32,128]{3,2,1,0:T(8,128)(2,1)} %slice.62), channel_id=1, source_target_pairs={{0,96},{32,0},{64,32},{96,64},{1,97},{33,1},{65,33},{97,65},{2,98}... | collective-permute-start | bytes 786440 | tf_op jit(solution)/shard_map/ppermute | solution.py:12
  176.2 39.6 %collective-permute-start.11 = (bf16[4,8,32,128]{3,2,1,0:T(8,128)(2,1)}, bf16[4,8,32,128]{3,2,1,0:T(8,128)(2,1)}, u32[]{:S(2)}, u32[]{:S(2)}) collective-permute-start(bf16[4,8,32,128]{3,2,1,0:T(8,128)(2,1)} %slice.64), channel_id=1, source_target_pairs={{0,32},{32,64},{64,96},{96,0},{1,33},{33,65},{65,97},{97,1},{2,34}... | collective-permute-start | bytes 786440 | tf_op jit(solution)/shard_map/ppermute | solution.py:12
  177.2 41.9 %collective-permute-start.12 = (bf16[4,8,32,128]{3,2,1,0:T(8,128)(2,1)}, bf16[4,8,32,128]{3,2,1,0:T(8,128)(2,1)}, u32[]{:S(2)}, u32[]{:S(2)}) collective-permute-start(bf16[4,8,32,128]{3,2,1,0:T(8,128)(2,1)} %slice.65), channel_id=1, source_target_pairs={{0,96},{32,0},{64,32},{96,64},{1,97},{33,1},{65,33},{97,65},{2,98}... | collective-permute-start | bytes 786440 | tf_op jit(solution)/shard_map/ppermute | solution.py:12
  182.1 50.7 %collective-permute-start.15 = (bf16[4,8,32,128]{3,2,1,0:T(8,128)(2,1)}, bf16[4,8,32,128]{3,2,1,0:T(8,128)(2,1)}, u32[]{:S(2)}, u32[]{:S(2)}) collective-permute-start(bf16[4,8,32,128]{3,2,1,0:T(8,128)(2,1)} %slice.67), channel_id=1, source_target_pairs={{0,32},{32,64},{64,96},{96,0},{1,33},{33,65},{65,97},{97,1},{2,34}... | collective-permute-start | bytes 786440 | tf_op jit(solution)/shard_map/ppermute | solution.py:12
  202.2 30.6 %collective-permute-start.16 = (bf16[4,8,32,128]{3,2,1,0:T(8,128)(2,1)S(1)}, bf16[4,8,32,128]{3,2,1,0:T(8,128)(2,1)}, u32[]{:S(2)}, u32[]{:S(2)}) collective-permute-start(bf16[4,8,32,128]{3,2,1,0:T(8,128)(2,1)S(1)} %copy-done.17), channel_id=1, source_target_pairs={{0,96},{32,0},{64,32},{96,64},{1,97},{33,1},{65,33},{97,65},{2,98}... | collective-permute-start | bytes 786440 | tf_op jit(solution)/shard_map/ppermute | solution.py:12
  205.4 41.7 %collective-permute-start.19 = (bf16[4,8,32,128]{3,2,1,0:T(8,128)(2,1)S(1)}, bf16[4,8,32,128]{3,2,1,0:T(8,128)(2,1)}, u32[]{:S(2)}, u32[]{:S(2)}) collective-permute-start(bf16[4,8,32,128]{3,2,1,0:T(8,128)(2,1)S(1)} %slice.70), channel_id=1, source_target_pairs={{0,32},{32,64},{64,96},{96,0},{1,33},{33,65},{65,97},{97,1},{2,34}... | collective-permute-start | bytes 786440 | tf_op jit(solution)/shard_map/ppermute | solution.py:12
  212.2 13.5 %all-to-all-start.1 = ((bf16[8,8,32,128]{3,2,1,0:T(8,128)(2,1)}), bf16[8,8,32,128]{3,2,1,0:T(8,128)(2,1)S(1)}, u32[]{:S(2)}, u32[]{:S(2)}) async-start(bf16[8,8,32,128]{3,2,1,0:T(8,128)(2,1)} %copy.13), calls=%async_computation.1 | async-start | bytes 1048576 | tf_op jit(solution)/shard_map/all_to_all | solution.py:20
  215.8 31.4 %collective-permute-start.20 = (bf16[4,8,32,128]{3,2,1,0:T(8,128)(2,1)S(1)}, bf16[4,8,32,128]{3,2,1,0:T(8,128)(2,1)}, u32[]{:S(2)}, u32[]{:S(2)}) collective-permute-start(bf16[4,8,32,128]{3,2,1,0:T(8,128)(2,1)S(1)} %copy-done.16), channel_id=1, source_target_pairs={{0,96},{32,0},{64,32},{96,64},{1,97},{33,1},{65,33},{97,65},{2,98}... | collective-permute-start | bytes 786440 | tf_op jit(solution)/shard_map/ppermute | solution.py:12
  225.7 16.8 %all-to-all-start.2 = ((bf16[8,8,32,128]{3,2,1,0:T(8,128)(2,1)}), bf16[8,8,32,128]{3,2,1,0:T(8,128)(2,1)S(1)}, u32[]{:S(2)}, u32[]{:S(2)}) async-start(bf16[8,8,32,128]{3,2,1,0:T(8,128)(2,1)} %copy.14), calls=%async_computation.2 | async-start | bytes 1048576 | tf_op jit(solution)/shard_map/all_to_all | solution.py:20
  242.5 14.2 %all-to-all-start.3 = ((bf16[8,8,32,128]{3,2,1,0:T(8,128)(2,1)}), bf16[8,8,32,128]{3,2,1,0:T(8,128)(2,1)S(1)}, u32[]{:S(2)}, u32[]{:S(2)}) async-start(bf16[8,8,32,128]{3,2,1,0:T(8,128)(2,1)} %copy.15), calls=%async_computation.3 | async-start | bytes 1048576 | tf_op jit(solution)/shard_map/all_to_all | solution.py:20
  (27 other events, 430.4 us)

commit v2 on v1

v2 whole, which is shorter than its diff:
```python
import functools

import jax
import jax.numpy as jnp
from jax import lax
from jax.experimental import pallas as pl
from jax.experimental.pallas import tpu as pltpu
from jax.sharding import PartitionSpec as P

IRREPS = 8
STEPS = (64, 64)
VMEM_PRODUCT = 60
MIB = 1 << 20


def shift_rep(array, distance):
    n = lax.axis_size("rep")
    return lax.ppermute(array, "rep", [(s, (s + distance) % n) for s in range(n)])


def flip_ten(array, mask):
    return lax.ppermute(array, "ten", [(s, s ^ mask) for s in range(lax.axis_size("ten"))])


def exchange_irreps(array, groups):
    return lax.all_to_all(
        array, "ten", split_axis=0, concat_axis=0, axis_index_groups=groups, tiled=True
    )


def params(limit):
    return pltpu.CompilerParams(vmem_limit_bytes=limit * MIB)


def cost(flops, moved):
    return pl.CostEstimate(flops=0, bytes_accessed=0, transcendentals=0)


def order_body(xor_ref, amps_ref, *out_refs):
    place = 0
    for ref in out_refs:
        step = ref.shape[2]
        ref[0] = amps_ref[:, 0, place:place + step]
        place += step


def order_amps(amps, pair_xor, steps):
    nk, irreps, rows, cols = amps.shape
    return pl.pallas_call(
        order_body,
        out_shape=[jax.ShapeDtypeStruct((irreps, nk, step, cols), amps.dtype) for step in steps],
        grid_spec=pltpu.PrefetchScalarGridSpec(
            num_scalar_prefetch=1,
            grid=(irreps,),
            in_specs=[pl.BlockSpec((nk, 1, rows, cols), lambda g, px: (0, jnp.bitwise_xor(g, px[0]), 0, 0))],
            out_specs=[pl.BlockSpec((1, nk, step, cols), lambda g, px: (g, 0, 0, 0)) for step in steps],
        ),
        compiler_params=params(16),
        cost_estimate=cost(0, 2 * amps.size * 2),
        name="order_amps",
    )(pair_xor.reshape(1), amps)


def by_j_body(ranks, w_ref, out_ref):
    rows, js, cols = w_ref.shape[1:]
    share = js // ranks
    moved = jnp.swapaxes(w_ref[0].astype(jnp.float32), 0, 1).astype(w_ref.dtype)
    for j in range(js):
        place = (j % share) * cols
        out_ref[j // share, 0, :, place:place + cols] = moved[j]


def integrals_by_j(integrals, ranks):
    nk, rows, js, cols = integrals.shape
    share = js // ranks
    return pl.pallas_call(
        functools.partial(by_j_body, ranks),
        out_shape=jax.ShapeDtypeStruct((ranks, nk, rows, share * cols), integrals.dtype),
        grid=(nk,),
        in_specs=[pl.BlockSpec((1, rows, js, cols), lambda k: (k, 0, 0, 0))],
        out_specs=pl.BlockSpec((ranks, 1, rows, share * cols), lambda k: (0, k, 0, 0)),
        compiler_params=params(16),
        cost_estimate=cost(0, 2 * integrals.size * 2),
        name="integrals_by_j",
    )(integrals)


def product_body(plan, blocks, rows_of, has_sum, quarter_ref, *refs):
    count = len(plan)
    pieces, w_refs = refs[:count], refs[count:count + 4 * len(blocks)]
    sum_refs = refs[count + 4 * len(blocks):][:1] if has_sum else ()
    out_ref, lhs, chosen, total, piece_sems, w_sems = refs[-6:]
    nk, rows, width = w_refs[0].shape
    cols = lhs.shape[2] // nk
    quarter = quarter_ref[0]

    copies = {}
    for slot, block in enumerate(blocks):
        copies[block] = []
        for d in range(4):
            place = pl.multiple_of(jnp.bitwise_xor(quarter, d) * rows, rows)
            copies[block].append(
                pltpu.make_async_copy(
                    w_refs[4 * slot + d],
                    chosen.at[pl.ds(slot * nk, nk), pl.ds(place, rows), :],
                    w_sems.at[4 * slot + d],
                )
            )
    for n, ((row, block), ref) in enumerate(zip(plan, pieces)):
        slot = blocks.index(block)
        for k in range(nk):
            copies[block].append(
                pltpu.make_async_copy(
                    ref.at[:, k],
                    lhs.at[pl.ds(slot * rows_of + row, ref.shape[0]), :, pl.ds(k * cols, cols)],
                    piece_sems.at[n * nk + k],
                )
            )
    for block in blocks:
        for copy in copies[block]:
            copy.start()
    for slot, block in enumerate(blocks):
        for copy in copies[block]:
            copy.wait()
        left = lhs[slot * rows_of:(slot + 1) * rows_of].reshape(-1, nk * cols)
        right = chosen[slot * nk:(slot + 1) * nk].reshape(nk * 4 * rows, width)
        sums = jnp.dot(left, right, preferred_element_type=jnp.float32)
        if slot == 0:
            if has_sum:
                sums = sums + sum_refs[0][...]
        else:
            sums = sums + total[...]
        if slot < len(blocks) - 1:
            total[...] = sums
        elif out_ref.dtype == jnp.float32:
            out_ref[...] = sums
        else:
            ni, js, step, _ = out_ref.shape
            for j in range(js):
                out_ref[:, j] = sums[:, j * cols:(j + 1) * cols].astype(out_ref.dtype).reshape(ni, step, cols)


def product(pieces, plan, chosen, blocks, quarter, sums=None, last=True):
    nk, step, cols = pieces[0].shape[1:]
    ni = IRREPS
    rows, width = chosen[0][0].shape[1:]
    js = width // cols
    w_parts = [part for block in blocks for part in chosen[block]]
    operands = [quarter.reshape(1), *pieces, *w_parts]
    in_specs = [pl.BlockSpec(memory_space=pltpu.SMEM)]
    in_specs += [pl.BlockSpec(memory_space=pl.ANY)] * (len(operands) - 1)
    if sums is not None:
        in_specs.append(pl.BlockSpec(memory_space=pltpu.VMEM))
        operands.append(sums)
    if last:
        out_shape = jax.ShapeDtypeStruct((ni, js, step, cols), pieces[0].dtype)
    else:
        out_shape = jax.ShapeDtypeStruct((ni * step, width), jnp.float32)
    depth = nk * 4 * rows * len(blocks)
    return pl.pallas_call(
        functools.partial(product_body, plan, blocks, ni, sums is not None),
        out_shape=out_shape,
        in_specs=in_specs,
        out_specs=pl.BlockSpec(memory_space=pltpu.VMEM),
        scratch_shapes=[
            pltpu.VMEM((ni * len(blocks), step, nk * cols), pieces[0].dtype),
            pltpu.VMEM((nk * len(blocks), 4 * rows, width), pieces[0].dtype),
            pltpu.VMEM((ni * step, width), jnp.float32),
            pltpu.SemaphoreType.DMA((len(pieces) * nk,)),
            pltpu.SemaphoreType.DMA((len(w_parts),)),
        ],
        compiler_params=params(VMEM_PRODUCT),
        cost_estimate=cost(2 * ni * step * depth * width, 2 * depth * width + 2 * ni * step * depth),
        name="product",
    )(*operands)


def place_body(offset, xor_ref, part_ref, *refs):
    out_ref, sems = refs[-2:]
    irreps, _, step, _ = part_ref.shape
    copies = [
        pltpu.make_async_copy(
            part_ref.at[g],
            out_ref.at[:, jnp.bitwise_xor(g, xor_ref[0]), offset:offset + step],
            sems.at[g],
        )
        for g in range(irreps)
    ]
    for copy in copies:
        copy.start()
    for copy in copies:
        copy.wait()


def place_irreps(part, pair_xor, rows, offset, result):
    irreps, js, step, cols = part.shape
    operands = [pair_xor.reshape(1), part]
    aliases = {}
    if result is not None:
        operands.append(result)
        aliases = {2: 0}
    return pl.pallas_call(
        functools.partial(place_body, offset),
        out_shape=jax.ShapeDtypeStruct((js, irreps, rows, cols), part.dtype),
        grid_spec=pltpu.PrefetchScalarGridSpec(
            num_scalar_prefetch=1,
            grid=(1,),
            in_specs=[pl.BlockSpec(memory_space=pl.ANY)] * (len(operands) - 1),
            out_specs=pl.BlockSpec(memory_space=pl.ANY),
            scratch_shapes=[pltpu.SemaphoreType.DMA((irreps,))],
        ),
        input_output_aliases=aliases,
        compiler_params=params(16),
        cost_estimate=cost(0, 2 * part.size * 2),
        name="place_irreps",
    )(*operands)


def after(values, *earlier):
    return lax.optimization_barrier((values, earlier))[0]


def per_device(amplitudes, integrals, pair_irreps):
    pair_xor = jnp.bitwise_xor(pair_irreps[0], pair_irreps[1])
    quarters = lax.axis_size("ten") // IRREPS
    groups = [
        [g * quarters + (q ^ (g % 2 * quarters // 2)) for g in range(IRREPS)] for q in range(quarters)
    ]
    ranks = lax.axis_size("rep")
    column = lax.axis_index("rep")
    quarter = lax.axis_index("ten") % quarters
    nk, rows = amplitudes.shape[1], amplitudes.shape[3]
    half = IRREPS // 2

    by_j = integrals_by_j(integrals, ranks)
    amplitudes, by_j = lax.optimization_barrier((amplitudes, by_j))
    by_group = order_amps(amplitudes.reshape(nk, IRREPS, rows, rows), pair_xor, STEPS)

    def for_rank(distance):
        return lax.dynamic_index_in_dim(by_j, (column + distance) % ranks, 0, keepdims=False)

    near = for_rank(0)
    arrived = [near, shift_rep(for_rank(1), 1), shift_rep(for_rank(3), -1), shift_rep(for_rank(2), 2)]
    zl = [flip_ten(part, 2) for part in arrived]
    core = [flip_ten(part, 1) for part in arrived]
    both = [flip_ten(part, 1) for part in zl]

    first = exchange_irreps(by_group[0], groups)
    first, core[1], core[2], arrived[3], both[0] = lax.optimization_barrier(
        (first, core[1], core[2], arrived[3], both[0])
    )
    second = exchange_irreps(after(by_group[1], first), groups)

    left, right = shift_rep(first, 1), shift_rep(first, -1)
    left2, right2 = shift_rep(second, 1), shift_rep(second, -1)
    left, right, zl[1], zl[2] = lax.optimization_barrier((left, right, zl[1], zl[2]))
    low, high = shift_rep(left[:half], 1), shift_rep(right[half:], -1)
    left2, right2, zl[3], both[1], both[2] = lax.optimization_barrier((left2, right2, zl[3], both[1], both[2]))
    low, high, left2, right2 = lax.optimization_barrier((low, high, left2, right2))
    low2, high2 = shift_rep(left2[:half], 1), shift_rep(right2[half:], -1)
    chosen = [(arrived[n], core[n], zl[n], both[n]) for n in range(ranks)]

    halves = ((0, 3), (half, 3))
    wholes = ((0, 0), (0, 1), (0, 2))
    out = product((first, left, right, low, high), wholes + halves, chosen, (0, 1, 2, 3), quarter)
    sums = product((second, left2, right2), wholes, chosen, (0, 1, 2), quarter, last=False)
    low2, high2, sums, out = lax.optimization_barrier((low2, high2, sums, out))
    back = exchange_irreps(out, groups)
    out2 = product((low2, high2), halves, chosen, (3,), quarter, sums=sums)
    back, out2 = lax.optimization_barrier((back, out2))
    back2 = exchange_irreps(out2, groups)
    result = place_irreps(back, pair_xor, rows, 0, None)
    result = place_irreps(back2, pair_xor, rows, STEPS[0], result)
    return result.reshape(amplitudes.shape)


def solution(mesh):
    in_specs = (P("ten", "rep", None, None), P("rep", "ten", None, None), P())
    return jax.shard_map(
        per_device, mesh=mesh, in_specs=in_specs, out_specs=in_specs[0], check_vma=False
    )
```

time: 279 us -> 159 us (0.57)
  blocking collectives: 49.5 us -> 0 us
  Pallas kernels: 0 us -> 27.3 us
  local copies, waits for them, and re-layouts: 34.7 us -> 9.84 us
  matrix products: 23.9 us -> 0 us
  other arithmetic: 22.8 us -> 0 us
  waiting for transfers between devices: 96.6 us -> 77.1 us
  starting transfers between devices: 48.6 us -> 42.7 us
    all_to_all x2 -> x0, blocking collectives: 49.5 us -> none  [exchange_irreps(): lax.all_to_all(array, 'ten', split_axis=0, concat_axis=0, axis_index_grou...]
    ppermute x2 -> x12, waiting for transfers between devices: 45.1 us -> 14 us  [flip_ten(): lax.ppermute(array, 'ten', [(s, s ^ mask) for s in range(lax.axis_size('t...]
    pallas_call x0 -> x7, Pallas kernels: none -> 27.3 us  [the longest x3 20.8 us: product(): pl.pallas_call(functools.partial(product_body, plan, blocks, ni, sums is...]
    dot_general x4 -> x0, matrix products: 23.9 us -> none  [per_device(): jnp.einsum('ikac,jkcb->ijab', part, chosen, preferred_element_type=jnp.fl...]
    all_to_all x3 -> x4, waiting for transfers between devices: 6.18 us -> 28.2 us  [exchange_irreps(): lax.all_to_all(array, 'ten', split_axis=0, concat_axis=0, axis_index_grou...]
    ppermute x19 -> x11, starting transfers between devices: 31.5 us -> 14.9 us  [shift_rep(): lax.ppermute(array, 'rep', [(s, (s + distance) % n) for s in range(n)])]
    another operation x4 -> x0, other arithmetic: 16 us -> none  [the longest x2 10.7 us: per_device(): jnp.stack([jnp.where(odd, across, pair), jnp.where(odd, pair, across)], a...]
    ppermute x19 -> x11, waiting for transfers between devices: 45.4 us -> 34.9 us  [shift_rep(): lax.ppermute(array, 'rep', [(s, (s + distance) % n) for s in range(n)])]
  transfers between devices with their start and end apart: 24 -> 27, of which waited for: 10 -> 12; matrix products, arithmetic and copies ran while one was open for 23% -> 3% of each run, Pallas kernels for 0% -> 16%
where the time goes in v2:
time: 159 us
  waiting for transfers between devices  77.1 us (48%)
  starting transfers between devices  42.7 us (27%)
  Pallas kernels  27.3 us (17%)
  local copies, waits for them, and re-layouts  9.84 us (6%)
  between operations  1.68 us (1%)
    ppermute x11, waiting for transfers between devices, shift_rep(): lax.ppermute(array, 'rep', [(s, (s + distance) % n) for s in range(n)])  34.9 us
    all_to_all x4, waiting for transfers between devices, exchange_irreps(): lax.all_to_all(array, 'ten', split_axis=0, concat_axis=0, axis_index_grou...  28.2 us
    all_to_all x4, starting transfers between devices, exchange_irreps(): lax.all_to_all(array, 'ten', split_axis=0, concat_axis=0, axis_index_grou...  23.1 us
    pallas_call x3, Pallas kernels, product(): pl.pallas_call(functools.partial(product_body, plan, blocks, ni, sums is...  20.8 us
    ppermute x11, starting transfers between devices, shift_rep(): lax.ppermute(array, 'rep', [(s, (s + distance) % n) for s in range(n)])  14.9 us
    ppermute x12, waiting for transfers between devices, flip_ten(): lax.ppermute(array, 'ten', [(s, s ^ mask) for s in range(lax.axis_size('t...  14 us
    ppermute x12, starting transfers between devices, flip_ten(): lax.ppermute(array, 'ten', [(s, s ^ mask) for s in range(lax.axis_size('t...  4.71 us
    unnamed x34, local copies, waits for them, and re-layouts  4.15 us
  transfers between devices with their start and end apart: 27, of which 12 were waited for; matrix products, arithmetic and copies ran while one was open for 3% of the time, Pallas kernels for 16%

profile of v2, /device:TPU:0, one launch (start us, length us, event | category | flops | bytes accessed | tf_op | source)
XLA Modules:
  0.0 158.6 jit_solution(11091570266437480540)
XLA Ops:
  4.2 2.8 %collective-permute-start.2 = (bf16[8,32,1024]{2,1,0:T(8,128)(2,1)}, bf16[8,32,1024]{2,1,0:T(8,128)(2,1)S(1)}, u32[]{:S(2)}, u32[]{:S(2)}) collective-permute-start(bf16[8,32,1024]{2,1,0:T(8,128)(2,1)} %get-tuple-element.65), channel_id=1, source_target_pairs={{0,96},{32,0},{64,32},{96,64},{1,97},{33,1},{65,33},{97,65},{2,98}... | collective-permute-start | bytes 1572872 | tf_op jit(solution)/shard_map/ppermute | solution.py:18
  10.8 3.1 %order_amps.1 = (bf16[8,8,64,128]{3,2,1,0:T(8,128)(2,1)}, bf16[8,8,64,128]{3,2,1,0:T(8,128)(2,1)}) custom-call(s32[1]{0:T(128)S(6)} %xor.4.xor_ref, bf16[8,8,128,128]{3,2,1,0:T(8,128)(2,1)S(1)} %bitcast.11), custom_call_target="tpu_custom_call" | custom-call | tf_op jit(solution)/shard_map/order_amps/pallas_call | solution.py:49
  13.9 6.4 %all-to-all-start = ((bf16[8,8,64,128]{3,2,1,0:T(8,128)(2,1)}), bf16[8,8,64,128]{3,2,1,0:T(8,128)(2,1)S(1)}, u32[]{:S(2)}, u32[]{:S(2)}) async-start(bf16[8,8,64,128]{3,2,1,0:T(8,128)(2,1)} %get-tuple-element.35), calls=%async_computation | async-start | bytes 2097152 | tf_op jit(solution)/shard_map/all_to_all | solution.py:26
  20.3 2.3 %collective-permute-start.4 = (bf16[8,32,1024]{2,1,0:T(8,128)(2,1)}, bf16[8,32,1024]{2,1,0:T(8,128)(2,1)S(1)}, u32[]{:S(2)}, u32[]{:S(2)}) collective-permute-start(bf16[8,32,1024]{2,1,0:T(8,128)(2,1)} %get-tuple-element.64), channel_id=1, source_target_pairs={{0,64},{32,96},{64,0},{96,32},{1,65},{33,97},{65,1},{97,33},{2,66}... | collective-permute-start | bytes 1572872 | tf_op jit(solution)/shard_map/ppermute | solution.py:18
  23.2 11.6 %collective-permute-done.4.refs_17_.refs_2_ = bf16[8,32,1024]{2,1,0:T(8,128)(2,1)S(1)} collective-permute-done((bf16[8,32,1024]{2,1,0:T(8,128)(2,1)}, bf16[8,32,1024]{2,1,0:T(8,128)(2,1)S(1)}, u32[]{:S(2)}, u32[]{:S(2)}) %collective-permute-start.4) | collective-permute-done | bytes 524320 | tf_op jit(solution)/shard_map/ppermute | solution.py:18
  35.3 3.1 %collective-permute-start.8 = (bf16[8,8,64,128]{3,2,1,0:T(8,128)(2,1)S(1)}, bf16[8,8,64,128]{3,2,1,0:T(8,128)(2,1)}, u32[]{:S(2)}, u32[]{:S(2)}) collective-permute-start(bf16[8,8,64,128]{3,2,1,0:T(8,128)(2,1)S(1)} %all-to-all-done.refs_0_), channel_id=1, source_target_pairs={{0,96},{32,0},{64,32},{96,64},{1,97},{33,1},{65,33},{97,65},{2,98}... | collective-permute-start | bytes 3145736 | tf_op jit(solution)/shard_map/ppermute | solution.py:18
  38.4 6.1 %all-to-all-start.1 = ((bf16[8,8,64,128]{3,2,1,0:T(8,128)(2,1)}), bf16[8,8,64,128]{3,2,1,0:T(8,128)(2,1)S(1)}, u32[]{:S(2)}, u32[]{:S(2)}) async-start(bf16[8,8,64,128]{3,2,1,0:T(8,128)(2,1)} %get-tuple-element.41), calls=%async_computation.1 | async-start | bytes 2097152 | tf_op jit(solution)/shard_map/all_to_all | solution.py:26
  44.6 2.0 %collective-permute-start.9 = (bf16[8,32,1024]{2,1,0:T(8,128)(2,1)}, bf16[8,32,1024]{2,1,0:T(8,128)(2,1)}, u32[]{:S(2)}, u32[]{:S(2)}) collective-permute-start(bf16[8,32,1024]{2,1,0:T(8,128)(2,1)} %copy-done.9), channel_id=1, source_target_pairs={{0,2},{1,3},{2,0},{3,1},{4,6},{5,7},{6,4},{7,5},{8,10},{9,11},{10,... | collective-permute-start | bytes 1572872 | tf_op jit(solution)/shard_map/ppermute | solution.py:22
  46.6 11.2 %all-to-all-done.1.refs_0_ = bf16[8,8,64,128]{3,2,1,0:T(8,128)(2,1)S(1)} async-done(((bf16[8,8,64,128]{3,2,1,0:T(8,128)(2,1)}), bf16[8,8,64,128]{3,2,1,0:T(8,128)(2,1)S(1)}, u32[]{:S(2)}, u32[]{:S(2)}) %all-to-all-start.1) | async-done | bytes 1048608 | tf_op jit(solution)/shard_map/all_to_all | solution.py:26
  59.9 8.3 %collective-permute-done.9.refs_9_.refs_11_ = bf16[8,32,1024]{2,1,0:T(8,128)(2,1)} collective-permute-done((bf16[8,32,1024]{2,1,0:T(8,128)(2,1)}, bf16[8,32,1024]{2,1,0:T(8,128)(2,1)}, u32[]{:S(2)}, u32[]{:S(2)}) %collective-permute-start.9) | collective-permute-done | bytes 524320 | tf_op jit(solution)/shard_map/ppermute | solution.py:22
  68.2 3.8 %collective-permute-done.7.refs_1_ = bf16[8,8,64,128]{3,2,1,0:T(8,128)(2,1)} collective-permute-done((bf16[8,8,64,128]{3,2,1,0:T(8,128)(2,1)S(1)}, bf16[8,8,64,128]{3,2,1,0:T(8,128)(2,1)}, u32[]{:S(2)}, u32[]{:S(2)}) %collective-permute-start.7) | collective-permute-done | bytes 1048608 | tf_op jit(solution)/shard_map/ppermute | solution.py:18
  74.1 4.1 %collective-permute-done.15.refs_19_.refs_4_ = bf16[8,32,1024]{2,1,0:T(8,128)(2,1)} collective-permute-done((bf16[8,32,1024]{2,1,0:T(8,128)(2,1)S(1)}, bf16[8,32,1024]{2,1,0:T(8,128)(2,1)}, u32[]{:S(2)}, u32[]{:S(2)}) %collective-permute-start.15) | collective-permute-done | bytes 524320 | tf_op jit(solution)/shard_map/ppermute | solution.py:22
  78.2 2.9 %collective-permute-start.12 = (bf16[4,8,64,128]{3,2,1,0:T(8,128)(2,1)S(1)}, bf16[4,8,64,128]{3,2,1,0:T(8,128)(2,1)S(1)}, u32[]{:S(2)}, u32[]{:S(2)}) collective-permute-start(bf16[4,8,64,128]{3,2,1,0:T(8,128)(2,1)S(1)} %slice.21), channel_id=1, source_target_pairs={{0,96},{32,0},{64,32},{96,64},{1,97},{33,1},{65,33},{97,65},{2,98}... | collective-permute-start | bytes 1572872 | tf_op jit(solution)/shard_map/ppermute | solution.py:18
  81.2 3.3 %collective-permute-done.14.refs_2_ = bf16[8,8,64,128]{3,2,1,0:T(8,128)(2,1)S(1)} collective-permute-done((bf16[8,8,64,128]{3,2,1,0:T(8,128)(2,1)S(1)}, bf16[8,8,64,128]{3,2,1,0:T(8,128)(2,1)S(1)}, u32[]{:S(2)}, u32[]{:S(2)}) %collective-permute-start.14) | collective-permute-done | bytes 1048608 | tf_op jit(solution)/shard_map/ppermute | solution.py:18
  84.5 9.8 %collective-permute-done.13.refs_1_ = bf16[8,8,64,128]{3,2,1,0:T(8,128)(2,1)S(1)} collective-permute-done((bf16[8,8,64,128]{3,2,1,0:T(8,128)(2,1)S(1)}, bf16[8,8,64,128]{3,2,1,0:T(8,128)(2,1)S(1)}, u32[]{:S(2)}, u32[]{:S(2)}) %collective-permute-start.13) | collective-permute-done | bytes 1048608 | tf_op jit(solution)/shard_map/ppermute | solution.py:18
  95.2 6.3 %collective-permute-done.11.refs_3_ = bf16[4,8,64,128]{3,2,1,0:T(8,128)(2,1)} collective-permute-done((bf16[4,8,64,128]{3,2,1,0:T(8,128)(2,1)S(1)}, bf16[4,8,64,128]{3,2,1,0:T(8,128)(2,1)}, u32[]{:S(2)}, u32[]{:S(2)}) %collective-permute-start.11) | collective-permute-done | bytes 524320 | tf_op jit(solution)/shard_map/ppermute | solution.py:18
  103.3 3.5 %collective-permute-start.19 = (bf16[4,8,64,128]{3,2,1,0:T(8,128)(2,1)}, bf16[4,8,64,128]{3,2,1,0:T(8,128)(2,1)S(1)}, u32[]{:S(2)}, u32[]{:S(2)}) collective-permute-start(bf16[4,8,64,128]{3,2,1,0:T(8,128)(2,1)} %slice.23), channel_id=1, source_target_pairs={{0,96},{32,0},{64,32},{96,64},{1,97},{33,1},{65,33},{97,65},{2,98}... | collective-permute-start | bytes 1572872 | tf_op jit(solution)/shard_map/ppermute | solution.py:18
  106.8 7.0 %product.3.refs_6_ = f32[512,1024]{1,0:T(8,128)} custom-call(s32[1]{0:T(128)} %bitcast.5.quarter_ref, bf16[8,8,64,128]{3,2,1,0:T(8,128)(2,1)} %copy-done.3, bf16[8,8,64,128]{3,2,1,0:T(8,128)(2,1)} %copy-done.6, bf16[8,8,64,128]{3,2,1,0:T(8,128)(2,1)} %copy-done.5, bf16[8,32,1024]{2,1,0:T(8,128)(2,1)} %copy-done.2, ...), custom_call_target="tpu_custom_call" | custom-call | tf_op jit(solution)/shard_map/product/pallas_call | solution.py:160
  115.5 8.0 %product.4 = bf16[8,8,64,128]{3,2,1,0:T(8,128)(2,1)} custom-call(s32[1]{0:T(128)} %bitcast.5.quarter_ref, bf16[8,8,64,128]{3,2,1,0:T(8,128)(2,1)} %copy-done.4, bf16[8,8,64,128]{3,2,1,0:T(8,128)(2,1)} %collective-permute-done.7.refs_1_, bf16[8,8,64,128]{3,2,1,0:T(8,128)(2,1)} %collective-permute-done.8.refs_2_, ...), custom_call_target="tpu_custom_call" | custom-call | tf_op jit(solution)/shard_map/product/pallas_call | solution.py:160
  123.5 6.6 %all-to-all-start.2 = ((bf16[8,8,64,128]{3,2,1,0:T(8,128)(2,1)}), bf16[8,8,64,128]{3,2,1,0:T(8,128)(2,1)S(1)}, u32[]{:S(2)}, u32[]{:S(2)}) async-start(bf16[8,8,64,128]{3,2,1,0:T(8,128)(2,1)} %product.4), calls=%async_computation.2 | async-start | bytes 2097152 | tf_op jit(solution)/shard_map/all_to_all | solution.py:26
  130.2 5.8 %product.5 = bf16[8,8,64,128]{3,2,1,0:T(8,128)(2,1)} custom-call(s32[1]{0:T(128)} %bitcast.5.quarter_ref, bf16[4,8,64,128]{3,2,1,0:T(8,128)(2,1)} %collective-permute-done.18.refs_0_, bf16[4,8,64,128]{3,2,1,0:T(8,128)(2,1)} %copy-done.14, bf16[8,32,1024]{2,1,0:T(8,128)(2,1)} %copy-done.7, bf16[8,32,1024]{2,1,0:T(8,128)(2,1)} %copy-done.12, ...), custom_call_target="tpu_custom_call" | custom-call | tf_op jit(solution)/shard_map/product/pallas_call | solution.py:160
  135.9 5.9 %all-to-all-done.2.part_ref = bf16[8,8,64,128]{3,2,1,0:T(8,128)(2,1)S(1)} async-done(((bf16[8,8,64,128]{3,2,1,0:T(8,128)(2,1)}), bf16[8,8,64,128]{3,2,1,0:T(8,128)(2,1)S(1)}, u32[]{:S(2)}, u32[]{:S(2)}) %all-to-all-start.2) | async-done | bytes 1048608 | tf_op jit(solution)/shard_map/all_to_all | solution.py:26
  141.8 3.9 %all-to-all-start.3 = ((bf16[8,8,64,128]{3,2,1,0:T(8,128)(2,1)}), bf16[8,8,64,128]{3,2,1,0:T(8,128)(2,1)S(1)}, u32[]{:S(2)}, u32[]{:S(2)}) async-start(bf16[8,8,64,128]{3,2,1,0:T(8,128)(2,1)} %product.5), calls=%async_computation.3 | async-start | bytes 2097152 | tf_op jit(solution)/shard_map/all_to_all | solution.py:26
  146.8 10.7 %all-to-all-done.3.part_ref = bf16[8,8,64,128]{3,2,1,0:T(8,128)(2,1)S(1)} async-done(((bf16[8,8,64,128]{3,2,1,0:T(8,128)(2,1)}), bf16[8,8,64,128]{3,2,1,0:T(8,128)(2,1)S(1)}, u32[]{:S(2)}, u32[]{:S(2)}) %all-to-all-start.3) | async-done | bytes 1048608 | tf_op jit(solution)/shard_map/all_to_all | solution.py:26
  (77 shorter events, 18.5 us)
Async XLA Ops:
  4.2 18.4 %collective-permute-start.2 = (bf16[8,32,1024]{2,1,0:T(8,128)(2,1)}, bf16[8,32,1024]{2,1,0:T(8,128)(2,1)S(1)}, u32[]{:S(2)}, u32[]{:S(2)}) collective-permute-start(bf16[8,32,1024]{2,1,0:T(8,128)(2,1)} %get-tuple-element.65), channel_id=1, source_target_pairs={{0,96},{32,0},{64,32},{96,64},{1,97},{33,1},{65,33},{97,65},{2,98}... | collective-permute-start | bytes 1572872 | tf_op jit(solution)/shard_map/ppermute | solution.py:18
  7.1 15.5 %collective-permute-start = (bf16[8,32,1024]{2,1,0:T(8,128)(2,1)}, bf16[8,32,1024]{2,1,0:T(8,128)(2,1)S(1)}, u32[]{:S(2)}, u32[]{:S(2)}) collective-permute-start(bf16[8,32,1024]{2,1,0:T(8,128)(2,1)} %get-tuple-element.66), channel_id=1, source_target_pairs={{0,32},{32,64},{64,96},{96,0},{1,33},{33,65},{65,97},{97,1},{2,34}... | collective-permute-start | bytes 1572872 | tf_op jit(solution)/shard_map/ppermute | solution.py:18
  7.1 16.0 %collective-permute-start.5 = (bf16[8,32,1024]{2,1,0:T(8,128)(2,1)S(1)}, bf16[8,32,1024]{2,1,0:T(8,128)(2,1)}, u32[]{:S(2)}, u32[]{:S(2)}) collective-permute-start(bf16[8,32,1024]{2,1,0:T(8,128)(2,1)S(1)} %get-tuple-element.63.refs_3_.refs_5_), channel_id=1, source_target_pairs={{0,2},{1,3},{2,0},{3,1},{4,6},{5,7},{6,4},{7,5},{8,10},{9,11},{10,... | collective-permute-start | bytes 1572872 | tf_op jit(solution)/shard_map/ppermute | solution.py:22
  13.9 21.5 %all-to-all-start = ((bf16[8,8,64,128]{3,2,1,0:T(8,128)(2,1)}), bf16[8,8,64,128]{3,2,1,0:T(8,128)(2,1)S(1)}, u32[]{:S(2)}, u32[]{:S(2)}) async-start(bf16[8,8,64,128]{3,2,1,0:T(8,128)(2,1)} %get-tuple-element.35), calls=%async_computation | async-start | bytes 2097152 | tf_op jit(solution)/shard_map/all_to_all | solution.py:26
  20.3 14.5 %collective-permute-start.4 = (bf16[8,32,1024]{2,1,0:T(8,128)(2,1)}, bf16[8,32,1024]{2,1,0:T(8,128)(2,1)S(1)}, u32[]{:S(2)}, u32[]{:S(2)}) collective-permute-start(bf16[8,32,1024]{2,1,0:T(8,128)(2,1)} %get-tuple-element.64), channel_id=1, source_target_pairs={{0,64},{32,96},{64,0},{96,32},{1,65},{33,97},{65,1},{97,33},{2,66}... | collective-permute-start | bytes 1572872 | tf_op jit(solution)/shard_map/ppermute | solution.py:18
  22.6 12.7 %collective-permute-start.3 = (bf16[8,32,1024]{2,1,0:T(8,128)(2,1)S(1)}, bf16[8,32,1024]{2,1,0:T(8,128)(2,1)}, u32[]{:S(2)}, u32[]{:S(2)}) collective-permute-start(bf16[8,32,1024]{2,1,0:T(8,128)(2,1)S(1)} %collective-permute-done.2.refs_11_.refs_13_), channel_id=1, source_target_pairs={{0,1},{1,0},{2,3},{3,2},{4,5},{5,4},{6,7},{7,6},{8,9},{9,8},{10,11... | collective-permute-start | bytes 1572872 | tf_op jit(solution)/shard_map/ppermute | solution.py:22
  22.6 12.7 %collective-permute-start.1 = (bf16[8,32,1024]{2,1,0:T(8,128)(2,1)S(1)}, bf16[8,32,1024]{2,1,0:T(8,128)(2,1)}, u32[]{:S(2)}, u32[]{:S(2)}) collective-permute-start(bf16[8,32,1024]{2,1,0:T(8,128)(2,1)S(1)} %collective-permute-done.refs_7_.refs_9_), channel_id=1, source_target_pairs={{0,1},{1,0},{2,3},{3,2},{4,5},{5,4},{6,7},{7,6},{8,9},{9,8},{10,11... | collective-permute-start | bytes 1572872 | tf_op jit(solution)/shard_map/ppermute | solution.py:22
  35.3 32.8 %collective-permute-start.8 = (bf16[8,8,64,128]{3,2,1,0:T(8,128)(2,1)S(1)}, bf16[8,8,64,128]{3,2,1,0:T(8,128)(2,1)}, u32[]{:S(2)}, u32[]{:S(2)}) collective-permute-start(bf16[8,8,64,128]{3,2,1,0:T(8,128)(2,1)S(1)} %all-to-all-done.refs_0_), channel_id=1, source_target_pairs={{0,96},{32,0},{64,32},{96,64},{1,97},{33,1},{65,33},{97,65},{2,98}... | collective-permute-start | bytes 3145736 | tf_op jit(solution)/shard_map/ppermute | solution.py:18
  38.4 19.4 %all-to-all-start.1 = ((bf16[8,8,64,128]{3,2,1,0:T(8,128)(2,1)}), bf16[8,8,64,128]{3,2,1,0:T(8,128)(2,1)S(1)}, u32[]{:S(2)}, u32[]{:S(2)}) async-start(bf16[8,8,64,128]{3,2,1,0:T(8,128)(2,1)} %get-tuple-element.41), calls=%async_computation.1 | async-start | bytes 2097152 | tf_op jit(solution)/shard_map/all_to_all | solution.py:26
  44.5 27.4 %collective-permute-start.7 = (bf16[8,8,64,128]{3,2,1,0:T(8,128)(2,1)S(1)}, bf16[8,8,64,128]{3,2,1,0:T(8,128)(2,1)}, u32[]{:S(2)}, u32[]{:S(2)}) collective-permute-start(bf16[8,8,64,128]{3,2,1,0:T(8,128)(2,1)S(1)} %all-to-all-done.refs_0_), channel_id=1, source_target_pairs={{0,32},{32,64},{64,96},{96,0},{1,33},{33,65},{65,97},{97,1},{2,34}... | collective-permute-start | bytes 3145736 | tf_op jit(solution)/shard_map/ppermute | solution.py:18
  44.5 15.3 %collective-permute-start.10 = (bf16[8,32,1024]{2,1,0:T(8,128)(2,1)}, bf16[8,32,1024]{2,1,0:T(8,128)(2,1)}, u32[]{:S(2)}, u32[]{:S(2)}) collective-permute-start(bf16[8,32,1024]{2,1,0:T(8,128)(2,1)} %copy-done.8), channel_id=1, source_target_pairs={{0,2},{1,3},{2,0},{3,1},{4,6},{5,7},{6,4},{7,5},{8,10},{9,11},{10,... | collective-permute-start | bytes 1572872 | tf_op jit(solution)/shard_map/ppermute | solution.py:22
  44.6 23.5 %collective-permute-start.9 = (bf16[8,32,1024]{2,1,0:T(8,128)(2,1)}, bf16[8,32,1024]{2,1,0:T(8,128)(2,1)}, u32[]{:S(2)}, u32[]{:S(2)}) collective-permute-start(bf16[8,32,1024]{2,1,0:T(8,128)(2,1)} %copy-done.9), channel_id=1, source_target_pairs={{0,2},{1,3},{2,0},{3,1},{4,6},{5,7},{6,4},{7,5},{8,10},{9,11},{10,... | collective-permute-start | bytes 1572872 | tf_op jit(solution)/shard_map/ppermute | solution.py:22
  57.8 26.7 %collective-permute-start.14 = (bf16[8,8,64,128]{3,2,1,0:T(8,128)(2,1)S(1)}, bf16[8,8,64,128]{3,2,1,0:T(8,128)(2,1)S(1)}, u32[]{:S(2)}, u32[]{:S(2)}) collective-permute-start(bf16[8,8,64,128]{3,2,1,0:T(8,128)(2,1)S(1)} %all-to-all-done.1.refs_0_), channel_id=1, source_target_pairs={{0,96},{32,0},{64,32},{96,64},{1,97},{33,1},{65,33},{97,65},{2,98}... | collective-permute-start | bytes 3145736 | tf_op jit(solution)/shard_map/ppermute | solution.py:18
  59.8 34.5 %collective-permute-start.13 = (bf16[8,8,64,128]{3,2,1,0:T(8,128)(2,1)S(1)}, bf16[8,8,64,128]{3,2,1,0:T(8,128)(2,1)S(1)}, u32[]{:S(2)}, u32[]{:S(2)}) collective-permute-start(bf16[8,8,64,128]{3,2,1,0:T(8,128)(2,1)S(1)} %all-to-all-done.1.refs_0_), channel_id=1, source_target_pairs={{0,32},{32,64},{64,96},{96,0},{1,33},{33,65},{65,97},{97,1},{2,34}... | collective-permute-start | bytes 3145736 | tf_op jit(solution)/shard_map/ppermute | solution.py:18
  68.2 12.9 %collective-permute-start.17 = (bf16[8,32,1024]{2,1,0:T(8,128)(2,1)}, bf16[8,32,1024]{2,1,0:T(8,128)(2,1)S(1)}, u32[]{:S(2)}, u32[]{:S(2)}) collective-permute-start(bf16[8,32,1024]{2,1,0:T(8,128)(2,1)} %collective-permute-done.10.refs_13_.refs_15_), channel_id=1, source_target_pairs={{0,1},{1,0},{2,3},{3,2},{4,5},{5,4},{6,7},{7,6},{8,9},{9,8},{10,11... | collective-permute-start | bytes 1572872 | tf_op jit(solution)/shard_map/ppermute | solution.py:22
  78.2 16.1 %collective-permute-start.12 = (bf16[4,8,64,128]{3,2,1,0:T(8,128)(2,1)S(1)}, bf16[4,8,64,128]{3,2,1,0:T(8,128)(2,1)S(1)}, u32[]{:S(2)}, u32[]{:S(2)}) collective-permute-start(bf16[4,8,64,128]{3,2,1,0:T(8,128)(2,1)S(1)} %slice.21), channel_id=1, source_target_pairs={{0,96},{32,0},{64,32},{96,64},{1,97},{33,1},{65,33},{97,65},{2,98}... | collective-permute-start | bytes 1572872 | tf_op jit(solution)/shard_map/ppermute | solution.py:18
  81.1 20.5 %collective-permute-start.11 = (bf16[4,8,64,128]{3,2,1,0:T(8,128)(2,1)S(1)}, bf16[4,8,64,128]{3,2,1,0:T(8,128)(2,1)}, u32[]{:S(2)}, u32[]{:S(2)}) collective-permute-start(bf16[4,8,64,128]{3,2,1,0:T(8,128)(2,1)S(1)} %slice.20), channel_id=1, source_target_pairs={{0,32},{32,64},{64,96},{96,0},{1,33},{33,65},{65,97},{97,1},{2,34}... | collective-permute-start | bytes 1572872 | tf_op jit(solution)/shard_map/ppermute | solution.py:18
  81.1 25.7 %collective-permute-start.20 = (bf16[8,32,1024]{2,1,0:T(8,128)(2,1)S(1)}, bf16[8,32,1024]{2,1,0:T(8,128)(2,1)}, u32[]{:S(2)}, u32[]{:S(2)}) collective-permute-start(bf16[8,32,1024]{2,1,0:T(8,128)(2,1)S(1)} %get-tuple-element.63.refs_3_.refs_5_), channel_id=1, source_target_pairs={{0,1},{1,0},{2,3},{3,2},{4,5},{5,4},{6,7},{7,6},{8,9},{9,8},{10,11... | collective-permute-start | bytes 1572872 | tf_op jit(solution)/shard_map/ppermute | solution.py:22
  84.5 29.3 %collective-permute-start.21 = (bf16[8,32,1024]{2,1,0:T(8,128)(2,1)S(1)}, bf16[8,32,1024]{2,1,0:T(8,128)(2,1)S(1)}, u32[]{:S(2)}, u32[]{:S(2)}) collective-permute-start(bf16[8,32,1024]{2,1,0:T(8,128)(2,1)S(1)} %collective-permute-done.4.refs_17_.refs_2_), channel_id=1, source_target_pairs={{0,1},{1,0},{2,3},{3,2},{4,5},{5,4},{6,7},{7,6},{8,9},{9,8},{10,11... | collective-permute-start | bytes 1572872 | tf_op jit(solution)/shard_map/ppermute | solution.py:22
  94.3 19.5 %collective-permute-start.22 = (bf16[8,32,1024]{2,1,0:T(8,128)(2,1)}, bf16[8,32,1024]{2,1,0:T(8,128)(2,1)S(1)}, u32[]{:S(2)}, u32[]{:S(2)}) collective-permute-start(bf16[8,32,1024]{2,1,0:T(8,128)(2,1)} %collective-permute-done.15.refs_19_.refs_4_), channel_id=1, source_target_pairs={{0,1},{1,0},{2,3},{3,2},{4,5},{5,4},{6,7},{7,6},{8,9},{9,8},{10,11... | collective-permute-start | bytes 1572872 | tf_op jit(solution)/shard_map/ppermute | solution.py:22
  103.3 20.2 %collective-permute-start.18 = (bf16[4,8,64,128]{3,2,1,0:T(8,128)(2,1)}, bf16[4,8,64,128]{3,2,1,0:T(8,128)(2,1)}, u32[]{:S(2)}, u32[]{:S(2)}) collective-permute-start(bf16[4,8,64,128]{3,2,1,0:T(8,128)(2,1)} %slice.22), channel_id=1, source_target_pairs={{0,32},{32,64},{64,96},{96,0},{1,33},{33,65},{65,97},{97,1},{2,34}... | collective-permute-start | bytes 1572872 | tf_op jit(solution)/shard_map/ppermute | solution.py:18
  103.3 20.2 %collective-permute-start.19 = (bf16[4,8,64,128]{3,2,1,0:T(8,128)(2,1)}, bf16[4,8,64,128]{3,2,1,0:T(8,128)(2,1)S(1)}, u32[]{:S(2)}, u32[]{:S(2)}) collective-permute-start(bf16[4,8,64,128]{3,2,1,0:T(8,128)(2,1)} %slice.23), channel_id=1, source_target_pairs={{0,96},{32,0},{64,32},{96,64},{1,97},{33,1},{65,33},{97,65},{2,98}... | collective-permute-start | bytes 1572872 | tf_op jit(solution)/shard_map/ppermute | solution.py:18
  123.5 18.3 %all-to-all-start.2 = ((bf16[8,8,64,128]{3,2,1,0:T(8,128)(2,1)}), bf16[8,8,64,128]{3,2,1,0:T(8,128)(2,1)S(1)}, u32[]{:S(2)}, u32[]{:S(2)}) async-start(bf16[8,8,64,128]{3,2,1,0:T(8,128)(2,1)} %product.4), calls=%async_computation.2 | async-start | bytes 2097152 | tf_op jit(solution)/shard_map/all_to_all | solution.py:26
  141.8 15.6 %all-to-all-start.3 = ((bf16[8,8,64,128]{3,2,1,0:T(8,128)(2,1)}), bf16[8,8,64,128]{3,2,1,0:T(8,128)(2,1)S(1)}, u32[]{:S(2)}, u32[]{:S(2)}) async-start(bf16[8,8,64,128]{3,2,1,0:T(8,128)(2,1)} %product.5), calls=%async_computation.3 | async-start | bytes 2097152 | tf_op jit(solution)/shard_map/all_to_all | solution.py:26
  (20 other events, 370.7 us)

commit v3 on v2

v3 whole, which is shorter than its diff:
```python
import functools

import jax
import jax.numpy as jnp
from jax import lax
from jax.experimental import pallas as pl
from jax.experimental.pallas import tpu as pltpu
from jax.sharding import PartitionSpec as P

IRREPS = 8
STEPS = (64, 64)
VMEM_PRODUCT = 44
AHEAD = 2
MIB = 1 << 20


def shift_rep(array, distance):
    n = lax.axis_size("rep")
    return lax.ppermute(array, "rep", [(s, (s + distance) % n) for s in range(n)])


def flip_ten(array, mask):
    return lax.ppermute(array, "ten", [(s, s ^ mask) for s in range(lax.axis_size("ten"))])


def exchange_irreps(array, groups):
    return lax.all_to_all(
        array, "ten", split_axis=0, concat_axis=0, axis_index_groups=groups, tiled=True
    )


def params(limit):
    return pltpu.CompilerParams(vmem_limit_bytes=limit * MIB)


def cost(flops, moved):
    return pl.CostEstimate(flops=0, bytes_accessed=0, transcendentals=0)


def order_body(offset, pair_ref, amps_ref, out_ref, sems):
    irreps, _, step, _ = out_ref.shape
    pair_xor = jnp.bitwise_xor(pair_ref[0], pair_ref[1])
    copies = [
        pltpu.make_async_copy(
            amps_ref.at[:, jnp.bitwise_xor(g, pair_xor), offset:offset + step],
            out_ref.at[g],
            sems.at[g],
        )
        for g in range(irreps)
    ]
    for copy in copies:
        copy.start()
    for copy in copies:
        copy.wait()


def order_amps(amps, pair_irreps, offset, step):
    nk, irreps, _, cols = amps.shape
    return pl.pallas_call(
        functools.partial(order_body, offset),
        out_shape=pltpu.VMEM((irreps, nk, step, cols), amps.dtype),
        in_specs=[pl.BlockSpec(memory_space=pltpu.SMEM), pl.BlockSpec(memory_space=pl.ANY)],
        out_specs=pl.BlockSpec(memory_space=pltpu.VMEM),
        scratch_shapes=[pltpu.SemaphoreType.DMA((irreps,))],
        compiler_params=params(16),
        cost_estimate=cost(0, 0),
        name="order_amps",
    )(pair_irreps, pltpu.with_memory_space_constraint(amps, pltpu.HBM))


def by_j_body(ranks, w_ref, *refs):
    out_refs, moved = refs[:-1], refs[-1]
    rows, js, cols = w_ref.shape[1:]
    share = js // ranks
    moved[...] = jnp.swapaxes(w_ref[0].astype(jnp.float32), 0, 1).astype(w_ref.dtype)
    for distance, ref in enumerate(out_refs):
        first = lax.rem(lax.axis_index("rep") + distance, ranks) * share
        for j in range(share):
            ref[0, :, j * cols:(j + 1) * cols] = moved[first + j]


def integrals_by_j(integrals, ranks):
    nk, rows, js, cols = integrals.shape
    wide = js // ranks * cols
    return pl.pallas_call(
        functools.partial(by_j_body, ranks),
        out_shape=[jax.ShapeDtypeStruct((nk, rows, wide), integrals.dtype)] * ranks,
        grid=(nk,),
        in_specs=[pl.BlockSpec((1, rows, js, cols), lambda k: (k, 0, 0, 0))],
        out_specs=[pl.BlockSpec((1, rows, wide), lambda k: (k, 0, 0))] * ranks,
        scratch_shapes=[pltpu.VMEM((js, rows, cols), integrals.dtype)],
        compiler_params=params(16),
        cost_estimate=cost(0, 0),
        name="integrals_by_j",
    )(integrals)


def product_body(plan, blocks, has_sum, quarter_ref, *refs):
    count = len(plan)
    pieces, w_refs = refs[:count], refs[count:count + 4 * len(blocks)]
    sum_refs = refs[count + 4 * len(blocks):][:1] if has_sum else ()
    out_ref, lhs, chosen, total, piece_sems, w_sems = refs[-6:]
    nk, rows, width = w_refs[0].shape
    ni, _, step, cols = pieces[0].shape
    quarter = quarter_ref[0]

    def copies(slot):
        found = []
        for d in range(4):
            place = pl.multiple_of(jnp.bitwise_xor(quarter, d) * rows, rows)
            found.append(
                pltpu.make_async_copy(
                    w_refs[4 * slot + d],
                    chosen.at[pl.ds(slot * nk, nk), pl.ds(place, rows), :],
                    w_sems.at[4 * slot + d],
                )
            )
        n = plan.index(blocks[slot])
        found.append(
            pltpu.make_async_copy(pieces[n], lhs.at[pl.ds(slot * ni, ni)], piece_sems.at[slot])
        )
        return found

    waiting = [copies(slot) for slot in range(len(blocks))]
    for slot in range(min(AHEAD, len(blocks))):
        for copy in waiting[slot]:
            copy.start()
    for slot in range(len(blocks)):
        for copy in waiting[slot]:
            copy.wait()
        if slot + AHEAD < len(blocks):
            for copy in waiting[slot + AHEAD]:
                copy.start()
        left = jnp.concatenate(
            [lhs[slot * ni:(slot + 1) * ni, k].reshape(ni * step, cols) for k in range(nk)], axis=1
        )
        right = chosen[slot * nk:(slot + 1) * nk].reshape(nk * 4 * rows, width)
        sums = jnp.dot(left, right, preferred_element_type=jnp.float32)
        if slot == 0:
            if has_sum:
                sums = sums + sum_refs[0][...]
        else:
            sums = sums + total[...]
        if slot < len(blocks) - 1:
            total[...] = sums
        elif out_ref.dtype == jnp.float32:
            out_ref[...] = sums
        else:
            for j in range(width // cols):
                out_ref[:, j] = sums[:, j * cols:(j + 1) * cols].astype(out_ref.dtype).reshape(ni, step, cols)


def product(pieces, plan, chosen, blocks, quarter, sums=None, last=True):
    nk, step, cols = pieces[0].shape[1:]
    ni = IRREPS
    rows, width = chosen[0][0].shape[1:]
    js = width // cols
    w_parts = [part for block in blocks for part in chosen[block]]
    if sums is None:
        pieces = [pltpu.with_memory_space_constraint(piece, pltpu.HBM) for piece in pieces]
        w_parts = [pltpu.with_memory_space_constraint(part, pltpu.HBM) for part in w_parts]
    operands = [quarter.reshape(1), *pieces, *w_parts]
    in_specs = [pl.BlockSpec(memory_space=pltpu.SMEM)]
    in_specs += [pl.BlockSpec(memory_space=pl.ANY)] * (len(operands) - 1)
    if sums is not None:
        in_specs.append(pl.BlockSpec(memory_space=pltpu.VMEM))
        operands.append(sums)
    if last:
        out_shape = [jax.ShapeDtypeStruct((ni, js, step, cols), chosen[0][0].dtype)]
    else:
        out_shape = [jax.ShapeDtypeStruct((ni * step, width), jnp.float32)]
    depth = nk * 4 * rows * len(blocks)
    return pl.pallas_call(
        functools.partial(product_body, plan, blocks, sums is not None),
        out_shape=out_shape,
        in_specs=in_specs,
        out_specs=[pl.BlockSpec(memory_space=pltpu.VMEM)],
        scratch_shapes=[
            pltpu.VMEM((ni * len(blocks), nk, step, cols), chosen[0][0].dtype),
            pltpu.VMEM((nk * len(blocks), 4 * rows, width), chosen[0][0].dtype),
            pltpu.VMEM((ni * step, width), jnp.float32),
            pltpu.SemaphoreType.DMA((len(pieces),)),
            pltpu.SemaphoreType.DMA((len(w_parts),)),
        ],
        compiler_params=params(VMEM_PRODUCT),
        cost_estimate=cost(2 * ni * step * depth * width, 2 * depth * width + 2 * ni * step * depth),
        name="product",
    )(*operands)


def place_body(offset, xor_ref, part_ref, *refs):
    out_ref, sems = refs[-2:]
    irreps, _, step, _ = part_ref.shape
    copies = [
        pltpu.make_async_copy(
            part_ref.at[g],
            out_ref.at[:, jnp.bitwise_xor(g, xor_ref[0]), offset:offset + step],
            sems.at[g],
        )
        for g in range(irreps)
    ]
    for copy in copies:
        copy.start()
    for copy in copies:
        copy.wait()


def place_irreps(part, pair_xor, rows, offset, result):
    irreps, js, step, cols = part.shape
    operands = [pair_xor.reshape(1), part]
    aliases = {}
    if result is not None:
        aliases = {len(operands): 0}
        operands.append(result)
    return pl.pallas_call(
        functools.partial(place_body, offset),
        out_shape=jax.ShapeDtypeStruct((js, irreps, rows, cols), part.dtype),
        in_specs=[pl.BlockSpec(memory_space=pltpu.SMEM)]
        + [pl.BlockSpec(memory_space=pl.ANY)] * (len(operands) - 1),
        out_specs=pl.BlockSpec(memory_space=pl.ANY),
        scratch_shapes=[pltpu.SemaphoreType.DMA((irreps,))],
        input_output_aliases=aliases,
        compiler_params=params(16),
        cost_estimate=cost(0, 0),
        name="place_irreps",
    )(*operands)


def after(values, *earlier):
    return lax.optimization_barrier((values, earlier))[0]


def per_device(amplitudes, integrals, pair_irreps):
    quarters = lax.axis_size("ten") // IRREPS
    groups = [
        [g * quarters + (q ^ (g % 2 * quarters // 2)) for g in range(IRREPS)] for q in range(quarters)
    ]
    ranks = lax.axis_size("rep")
    quarter = lax.axis_index("ten") % quarters
    nk, rows = amplitudes.shape[1], amplitudes.shape[3]

    by_j = integrals_by_j(integrals, ranks)
    amplitudes, by_j = lax.optimization_barrier((amplitudes, by_j))
    amps = amplitudes.reshape(nk, IRREPS, rows, rows)
    by_group = order_amps(amps, pair_irreps, 0, STEPS[0])

    near = by_j[0]
    arrived = [near, shift_rep(by_j[1], 1), shift_rep(by_j[3], -1), shift_rep(by_j[2], 2)]
    zl = [flip_ten(part, 2) for part in arrived]
    core = [flip_ten(part, 1) for part in arrived]
    both = [flip_ten(part, 1) for part in zl]

    first = exchange_irreps(by_group, groups)
    by_group2 = order_amps(after(amps, core[1]), pair_irreps, STEPS[0], STEPS[1])
    first, core[1], core[2], arrived[3], zl[0], by_group2 = lax.optimization_barrier(
        (first, core[1], core[2], arrived[3], zl[0], by_group2)
    )
    core[3], zl[3] = flip_ten(arrived[3], 1), flip_ten(arrived[3], 2)
    both[0] = flip_ten(zl[0], 1)
    by_group2, core[3] = lax.optimization_barrier((by_group2, core[3]))
    second = exchange_irreps(by_group2, groups)

    left, right = shift_rep(first, 1), shift_rep(first, -1)
    right2 = shift_rep(second, -1)
    left, right, zl[1] = lax.optimization_barrier((left, right, zl[1]))
    far = shift_rep(left, 1)
    both[1] = flip_ten(zl[1], 1)
    left2 = shift_rep(after(second, both[1]), 1)
    far2 = shift_rep(right2, -1)
    both[2], both[3] = flip_ten(zl[2], 1), flip_ten(zl[3], 1)
    chosen = [(arrived[n], core[n], zl[n], both[n]) for n in range(ranks)]

    (sums,) = product((first, left, right), (0, 1, 2), chosen, (0, 1, 2), quarter, last=False)
    far, sums = lax.optimization_barrier((far, sums))
    (out,) = product((far,), (3,), chosen, (3,), quarter, sums=sums)
    back = exchange_irreps(out, groups)
    (sums,) = product((second, right2), (0, 2), chosen, (0, 2), quarter, last=False)
    left2, far2, sums = lax.optimization_barrier((left2, far2, sums))
    (out2,) = product((left2, far2), (1, 3), chosen, (1, 3), quarter, sums=sums)
    pair_xor = jnp.bitwise_xor(pair_irreps[0], pair_irreps[1])
    back, out2 = lax.optimization_barrier((back, out2))
    back2 = exchange_irreps(out2, groups)
    result = place_irreps(back, pair_xor, rows, 0, None)
    result = place_irreps(back2, pair_xor, rows, STEPS[0], result)
    return result.reshape(amplitudes.shape)


def solution(mesh):
    in_specs = (P("ten", "rep", None, None), P("rep", "ten", None, None), P())
    return jax.shard_map(
        per_device, mesh=mesh, in_specs=in_specs, out_specs=in_specs[0], check_vma=False
    )
```

time: 159 us -> 140 us (0.88)
  waiting for transfers between devices: 77.1 us -> 62.8 us
  local copies, waits for them, and re-layouts: 9.84 us -> 2.23 us
    ppermute x11 -> x9, waiting for transfers between devices: 34.9 us -> 15.8 us  [shift_rep(): lax.ppermute(array, 'rep', [(s, (s + distance) % n) for s in range(n)])]
    ppermute x12, waiting for transfers between devices: 14 us -> 31.2 us  [flip_ten(): lax.ppermute(array, 'ten', [(s, s ^ mask) for s in range(lax.axis_size('t...]
    all_to_all x4, waiting for transfers between devices: 28.2 us -> 15.8 us  [exchange_irreps(): lax.all_to_all(array, 'ten', split_axis=0, concat_axis=0, axis_index_grou...]
    all_to_all x4, starting transfers between devices: 23.1 us -> 27.1 us  [exchange_irreps(): lax.all_to_all(array, 'ten', split_axis=0, concat_axis=0, axis_index_grou...]
    slice x4 -> x0, local copies, waits for them, and re-layouts: 3.87 us -> none  [the longest x2 2.15 us: per_device(): low, high = (shift_rep(left[:half], 1), shift_rep(right[half:], -1))]
    ppermute x11 -> x9, starting transfers between devices: 14.9 us -> 11.1 us  [shift_rep(): lax.ppermute(array, 'rep', [(s, (s + distance) % n) for s in range(n)])]
    unnamed x34 -> x32, local copies, waits for them, and re-layouts: 4.15 us -> 1.65 us
    pallas_call x5 -> x7, Pallas kernels: 25.2 us -> 26.7 us  [the longest x4 19.4 us: product(): pl.pallas_call(functools.partial(product_body, plan, blocks, sums is not...]
  transfers between devices with their start and end apart: 27 -> 25, of which waited for: 12 -> 11; matrix products, arithmetic and copies ran while one was open for 3% -> 0% of each run, Pallas kernels for 16% -> 19%
where the time goes in v3:
time: 140 us
  waiting for transfers between devices  62.8 us (45%)
  starting transfers between devices  44.2 us (32%)
  Pallas kernels  28.8 us (21%)
  local copies, waits for them, and re-layouts  2.23 us (2%)
  between operations  1.67 us (1%)
    ppermute x12, waiting for transfers between devices, flip_ten(): lax.ppermute(array, 'ten', [(s, s ^ mask) for s in range(lax.axis_size('t...  31.2 us
    all_to_all x4, starting transfers between devices, exchange_irreps(): lax.all_to_all(array, 'ten', split_axis=0, concat_axis=0, axis_index_grou...  27.1 us
    pallas_call x4, Pallas kernels, product(): pl.pallas_call(functools.partial(product_body, plan, blocks, sums is not...  19.4 us
    ppermute x9, waiting for transfers between devices, shift_rep(): lax.ppermute(array, 'rep', [(s, (s + distance) % n) for s in range(n)])  15.8 us
    all_to_all x4, waiting for transfers between devices, exchange_irreps(): lax.all_to_all(array, 'ten', split_axis=0, concat_axis=0, axis_index_grou...  15.8 us
    ppermute x9, starting transfers between devices, shift_rep(): lax.ppermute(array, 'rep', [(s, (s + distance) % n) for s in range(n)])  11.1 us
    ppermute x12, starting transfers between devices, flip_ten(): lax.ppermute(array, 'ten', [(s, s ^ mask) for s in range(lax.axis_size('t...  5.97 us
    pallas_call x2, Pallas kernels, order_amps(): pl.pallas_call(functools.partial(order_body, offset), out_shape=pltpu.VME...  5.78 us
  transfers between devices with their start and end apart: 25, of which 11 were waited for; matrix products, arithmetic and copies ran while one was open for 0% of the time, Pallas kernels for 19%

profile of v3, /device:TPU:0, one launch (start us, length us, event | category | flops | bytes accessed | tf_op | source)
XLA Modules:
  0.0 139.6 jit_solution(11980156608840053519)
XLA Ops:
  4.9 1.7 %collective-permute-start.2 = (bf16[8,32,1024]{2,1,0:T(8,128)(2,1)S(1)}, bf16[8,32,1024]{2,1,0:T(8,128)(2,1)}, u32[]{:S(2)}, u32[]{:S(2)}) collective-permute-start(bf16[8,32,1024]{2,1,0:T(8,128)(2,1)S(1)} %get-tuple-element.40), channel_id=1, source_target_pairs={{0,96},{32,0},{64,32},{96,64},{1,97},{33,1},{65,33},{97,65},{2,98}... | collective-permute-start | bytes 1572872 | tf_op jit(solution)/shard_map/ppermute | solution.py:19
  6.5 2.9 %order_amps.2 = bf16[8,8,64,128]{3,2,1,0:T(8,128)(2,1)} custom-call(s32[2]{0:T(128)S(1)} %copy-done.14, bf16[8,8,128,128]{3,2,1,0:T(8,128)(2,1)} %bitcast.3), custom_call_target="tpu_custom_call" | custom-call | tf_op jit(solution)/shard_map/order_amps/pallas_call | solution.py:59
  9.4 8.0 %all-to-all-start = ((bf16[8,8,64,128]{3,2,1,0:T(8,128)(2,1)}), bf16[8,8,64,128]{3,2,1,0:T(8,128)(2,1)}, u32[]{:S(2)}, u32[]{:S(2)}) async-start(bf16[8,8,64,128]{3,2,1,0:T(8,128)(2,1)} %order_amps.2), calls=%async_computation | async-start | bytes 2097152 | tf_op jit(solution)/shard_map/all_to_all | solution.py:27
  18.1 2.0 %collective-permute-start.4 = (bf16[8,32,1024]{2,1,0:T(8,128)(2,1)S(1)}, bf16[8,32,1024]{2,1,0:T(8,128)(2,1)S(1)}, u32[]{:S(2)}, u32[]{:S(2)}) collective-permute-start(bf16[8,32,1024]{2,1,0:T(8,128)(2,1)S(1)} %get-tuple-element.41), channel_id=1, source_target_pairs={{0,64},{32,96},{64,0},{96,32},{1,65},{33,97},{65,1},{97,33},{2,66}... | collective-permute-start | bytes 1572872 | tf_op jit(solution)/shard_map/ppermute | solution.py:19
  20.1 1.9 %collective-permute-start.5 = (bf16[8,32,1024]{2,1,0:T(8,128)(2,1)S(1)}, bf16[8,32,1024]{2,1,0:T(8,128)(2,1)}, u32[]{:S(2)}, u32[]{:S(2)}) collective-permute-start(bf16[8,32,1024]{2,1,0:T(8,128)(2,1)S(1)} %get-tuple-element.42.refs_3_.refs_2_), channel_id=1, source_target_pairs={{0,2},{1,3},{2,0},{3,1},{4,6},{5,7},{6,4},{7,5},{8,10},{9,11},{10,... | collective-permute-start | bytes 1572872 | tf_op jit(solution)/shard_map/ppermute | solution.py:23
  22.0 2.9 %order_amps.3 = bf16[8,8,64,128]{3,2,1,0:T(8,128)(2,1)} custom-call(s32[2]{0:T(128)S(1)} %copy-done.14, bf16[8,8,128,128]{3,2,1,0:T(8,128)(2,1)} %bitcast.4), custom_call_target="tpu_custom_call" | custom-call | tf_op jit(solution)/shard_map/order_amps/pallas_call | solution.py:59
  24.9 9.0 %collective-permute-done.4.refs_1_.refs_6_ = bf16[8,32,1024]{2,1,0:T(8,128)(2,1)S(1)} collective-permute-done((bf16[8,32,1024]{2,1,0:T(8,128)(2,1)S(1)}, bf16[8,32,1024]{2,1,0:T(8,128)(2,1)S(1)}, u32[]{:S(2)}, u32[]{:S(2)}) %collective-permute-start.4) | collective-permute-done | bytes 524320 | tf_op jit(solution)/shard_map/ppermute | solution.py:19
  35.2 2.6 %collective-permute-start.7 = (bf16[8,8,64,128]{3,2,1,0:T(8,128)(2,1)}, bf16[8,8,64,128]{3,2,1,0:T(8,128)(2,1)}, u32[]{:S(2)}, u32[]{:S(2)}) collective-permute-start(bf16[8,8,64,128]{3,2,1,0:T(8,128)(2,1)} %all-to-all-done.refs_0_), channel_id=1, source_target_pairs={{0,96},{32,0},{64,32},{96,64},{1,97},{33,1},{65,33},{97,65},{2,98}... | collective-permute-start | bytes 3145736 | tf_op jit(solution)/shard_map/ppermute | solution.py:19
  37.8 7.8 %all-to-all-start.2 = ((bf16[8,8,64,128]{3,2,1,0:T(8,128)(2,1)}), bf16[8,8,64,128]{3,2,1,0:T(8,128)(2,1)}, u32[]{:S(2)}, u32[]{:S(2)}) async-start(bf16[8,8,64,128]{3,2,1,0:T(8,128)(2,1)} %order_amps.3), calls=%async_computation.2 | async-start | bytes 2097152 | tf_op jit(solution)/shard_map/all_to_all | solution.py:27
  45.8 1.9 %collective-permute-start.13 = (bf16[8,32,1024]{2,1,0:T(8,128)(2,1)}, bf16[8,32,1024]{2,1,0:T(8,128)(2,1)}, u32[]{:S(2)}, u32[]{:S(2)}) collective-permute-start(bf16[8,32,1024]{2,1,0:T(8,128)(2,1)} %collective-permute-done.2.refs_11_.refs_6_), channel_id=1, source_target_pairs={{0,2},{1,3},{2,0},{3,1},{4,6},{5,7},{6,4},{7,5},{8,10},{9,11},{10,... | collective-permute-start | bytes 1572872 | tf_op jit(solution)/shard_map/ppermute | solution.py:23
  47.7 12.8 %collective-permute-done.8.refs_9_.refs_4_ = bf16[8,32,1024]{2,1,0:T(8,128)(2,1)S(1)} collective-permute-done((bf16[8,32,1024]{2,1,0:T(8,128)(2,1)S(1)}, bf16[8,32,1024]{2,1,0:T(8,128)(2,1)S(1)}, u32[]{:S(2)}, u32[]{:S(2)}) %collective-permute-start.8) | collective-permute-done | bytes 524320 | tf_op jit(solution)/shard_map/ppermute | solution.py:23
  63.8 8.1 %collective-permute-done.13.refs_13_.refs_8_ = bf16[8,32,1024]{2,1,0:T(8,128)(2,1)} collective-permute-done((bf16[8,32,1024]{2,1,0:T(8,128)(2,1)}, bf16[8,32,1024]{2,1,0:T(8,128)(2,1)}, u32[]{:S(2)}, u32[]{:S(2)}) %collective-permute-start.13) | collective-permute-done | bytes 524320 | tf_op jit(solution)/shard_map/ppermute | solution.py:23
  71.9 9.7 %collective-permute-done.16.refs_3_.refs_8_ = bf16[8,32,1024]{2,1,0:T(8,128)(2,1)S(1)} collective-permute-done((bf16[8,32,1024]{2,1,0:T(8,128)(2,1)S(1)}, bf16[8,32,1024]{2,1,0:T(8,128)(2,1)S(1)}, u32[]{:S(2)}, u32[]{:S(2)}) %collective-permute-start.16) | collective-permute-done | bytes 524320 | tf_op jit(solution)/shard_map/ppermute | solution.py:23
  82.2 3.7 %collective-permute-done.19.refs_1_ = bf16[8,8,64,128]{3,2,1,0:T(8,128)(2,1)} collective-permute-done((bf16[8,8,64,128]{3,2,1,0:T(8,128)(2,1)}, bf16[8,8,64,128]{3,2,1,0:T(8,128)(2,1)}, u32[]{:S(2)}, u32[]{:S(2)}) %collective-permute-start.19) | collective-permute-done | bytes 1048608 | tf_op jit(solution)/shard_map/ppermute | solution.py:19
  85.9 1.7 %collective-permute-start.20 = (bf16[8,8,64,128]{3,2,1,0:T(8,128)(2,1)}, bf16[8,8,64,128]{3,2,1,0:T(8,128)(2,1)}, u32[]{:S(2)}, u32[]{:S(2)}) collective-permute-start(bf16[8,8,64,128]{3,2,1,0:T(8,128)(2,1)} %collective-permute-done.19.refs_1_), channel_id=1, source_target_pairs={{0,96},{32,0},{64,32},{96,64},{1,97},{33,1},{65,33},{97,65},{2,98}... | collective-permute-start | bytes 3145736 | tf_op jit(solution)/shard_map/ppermute | solution.py:19
  87.6 5.9 %product.4.refs_5_ = f32[512,1024]{1,0:T(8,128)S(1)} custom-call(s32[1]{0:T(128)} %bitcast.quarter_ref, bf16[8,8,64,128]{3,2,1,0:T(8,128)(2,1)} %all-to-all-done.refs_0_, bf16[8,8,64,128]{3,2,1,0:T(8,128)(2,1)} %collective-permute-done.6.refs_1_, bf16[8,8,64,128]{3,2,1,0:T(8,128)(2,1)} %collective-permute-done.7.refs_2_, bf16[8,32,1024]{2,1,0:T(8,128)(2,1)} %copy-done.2, ...), custom_call_target="tpu_custom_call" | custom-call | tf_op jit(solution)/shard_map/product/pallas_call | solution.py:173
  93.5 3.7 %product.5 = bf16[8,8,64,128]{3,2,1,0:T(8,128)(2,1)} custom-call(s32[1]{0:T(128)} %bitcast.quarter_ref, bf16[8,8,64,128]{3,2,1,0:T(8,128)(2,1)} %collective-permute-done.9.refs_0_, bf16[8,32,1024]{2,1,0:T(8,128)(2,1)S(1)} %collective-permute-done.4.refs_1_.refs_6_, bf16[8,32,1024]{2,1,0:T(8,128)(2,1)S(1)} %collective-permute-done.15.refs_2_.refs_7_, ...), custom_call_target="tpu_custom_call" | custom-call | tf_op jit(solution)/shard_map/product/pallas_call | solution.py:173
  97.2 7.2 %all-to-all-start.1 = ((bf16[8,8,64,128]{3,2,1,0:T(8,128)(2,1)}), bf16[8,8,64,128]{3,2,1,0:T(8,128)(2,1)S(1)}, u32[]{:S(2)}, u32[]{:S(2)}) async-start(bf16[8,8,64,128]{3,2,1,0:T(8,128)(2,1)} %product.5), calls=%async_computation.1 | async-start | bytes 2097152 | tf_op jit(solution)/shard_map/all_to_all | solution.py:27
  104.5 4.8 %product.6.refs_10_ = f32[512,1024]{1,0:T(8,128)S(1)} custom-call(s32[1]{0:T(128)} %bitcast.quarter_ref, bf16[8,8,64,128]{3,2,1,0:T(8,128)(2,1)} %all-to-all-done.2.refs_0_, bf16[8,8,64,128]{3,2,1,0:T(8,128)(2,1)} %collective-permute-done.19.refs_1_, bf16[8,32,1024]{2,1,0:T(8,128)(2,1)} %copy-done.2, ...), custom_call_target="tpu_custom_call" | custom-call | tf_op jit(solution)/shard_map/product/pallas_call | solution.py:173
  109.3 2.5 %collective-permute-done.18.refs_0_ = bf16[8,8,64,128]{3,2,1,0:T(8,128)(2,1)} collective-permute-done((bf16[8,8,64,128]{3,2,1,0:T(8,128)(2,1)}, bf16[8,8,64,128]{3,2,1,0:T(8,128)(2,1)}, u32[]{:S(2)}, u32[]{:S(2)}) %collective-permute-start.18) | collective-permute-done | bytes 1048608 | tf_op jit(solution)/shard_map/ppermute | solution.py:19
  111.8 5.0 %product.7 = bf16[8,8,64,128]{3,2,1,0:T(8,128)(2,1)} custom-call(s32[1]{0:T(128)} %bitcast.quarter_ref, bf16[8,8,64,128]{3,2,1,0:T(8,128)(2,1)} %collective-permute-done.18.refs_0_, bf16[8,8,64,128]{3,2,1,0:T(8,128)(2,1)} %collective-permute-done.20.refs_1_, bf16[8,32,1024]{2,1,0:T(8,128)(2,1)S(1)} %copy-done.1, bf16[8,32,1024]{2,1,0:T(8,128)(2,1)S(1)} %copy-done.4, ...), custom_call_target="tpu_custom_call" | custom-call | tf_op jit(solution)/shard_map/product/pallas_call | solution.py:173
  116.8 2.4 %all-to-all-done.1.part_ref = bf16[8,8,64,128]{3,2,1,0:T(8,128)(2,1)S(1)} async-done(((bf16[8,8,64,128]{3,2,1,0:T(8,128)(2,1)}), bf16[8,8,64,128]{3,2,1,0:T(8,128)(2,1)S(1)}, u32[]{:S(2)}, u32[]{:S(2)}) %all-to-all-start.1) | async-done | bytes 1048608 | tf_op jit(solution)/shard_map/all_to_all | solution.py:27
  119.2 4.1 %all-to-all-start.3 = ((bf16[8,8,64,128]{3,2,1,0:T(8,128)(2,1)}), bf16[8,8,64,128]{3,2,1,0:T(8,128)(2,1)S(1)}, u32[]{:S(2)}, u32[]{:S(2)}) async-start(bf16[8,8,64,128]{3,2,1,0:T(8,128)(2,1)} %product.7), calls=%async_computation.3 | async-start | bytes 2097152 | tf_op jit(solution)/shard_map/all_to_all | solution.py:27
  126.2 12.3 %all-to-all-done.3.part_ref = bf16[8,8,64,128]{3,2,1,0:T(8,128)(2,1)S(1)} async-done(((bf16[8,8,64,128]{3,2,1,0:T(8,128)(2,1)}), bf16[8,8,64,128]{3,2,1,0:T(8,128)(2,1)S(1)}, u32[]{:S(2)}, u32[]{:S(2)}) %all-to-all-start.3) | async-done | bytes 1048608 | tf_op jit(solution)/shard_map/all_to_all | solution.py:27
  (68 shorter events, 13.4 us)
Async XLA Ops:
  3.2 14.8 %collective-permute-start = (bf16[8,32,1024]{2,1,0:T(8,128)(2,1)S(1)}, bf16[8,32,1024]{2,1,0:T(8,128)(2,1)S(1)}, u32[]{:S(2)}, u32[]{:S(2)}) collective-permute-start(bf16[8,32,1024]{2,1,0:T(8,128)(2,1)S(1)} %get-tuple-element.39), channel_id=1, source_target_pairs={{0,32},{32,64},{64,96},{96,0},{1,33},{33,65},{65,97},{97,1},{2,34}... | collective-permute-start | bytes 1572872 | tf_op jit(solution)/shard_map/ppermute | solution.py:19
  4.9 17.1 %collective-permute-start.2 = (bf16[8,32,1024]{2,1,0:T(8,128)(2,1)S(1)}, bf16[8,32,1024]{2,1,0:T(8,128)(2,1)}, u32[]{:S(2)}, u32[]{:S(2)}) collective-permute-start(bf16[8,32,1024]{2,1,0:T(8,128)(2,1)S(1)} %get-tuple-element.40), channel_id=1, source_target_pairs={{0,96},{32,0},{64,32},{96,64},{1,97},{33,1},{65,33},{97,65},{2,98}... | collective-permute-start | bytes 1572872 | tf_op jit(solution)/shard_map/ppermute | solution.py:19
  9.4 25.0 %all-to-all-start = ((bf16[8,8,64,128]{3,2,1,0:T(8,128)(2,1)}), bf16[8,8,64,128]{3,2,1,0:T(8,128)(2,1)}, u32[]{:S(2)}, u32[]{:S(2)}) async-start(bf16[8,8,64,128]{3,2,1,0:T(8,128)(2,1)} %order_amps.2), calls=%async_computation | async-start | bytes 2097152 | tf_op jit(solution)/shard_map/all_to_all | solution.py:27
  18.1 3.9 %collective-permute-start.1 = (bf16[8,32,1024]{2,1,0:T(8,128)(2,1)S(1)}, bf16[8,32,1024]{2,1,0:T(8,128)(2,1)S(1)}, u32[]{:S(2)}, u32[]{:S(2)}) collective-permute-start(bf16[8,32,1024]{2,1,0:T(8,128)(2,1)S(1)} %collective-permute-done.refs_7_.refs_2_), channel_id=1, source_target_pairs={{0,1},{1,0},{2,3},{3,2},{4,5},{5,4},{6,7},{7,6},{8,9},{9,8},{10,11... | collective-permute-start | bytes 1572872 | tf_op jit(solution)/shard_map/ppermute | solution.py:23
  18.1 15.8 %collective-permute-start.4 = (bf16[8,32,1024]{2,1,0:T(8,128)(2,1)S(1)}, bf16[8,32,1024]{2,1,0:T(8,128)(2,1)S(1)}, u32[]{:S(2)}, u32[]{:S(2)}) collective-permute-start(bf16[8,32,1024]{2,1,0:T(8,128)(2,1)S(1)} %get-tuple-element.41), channel_id=1, source_target_pairs={{0,64},{32,96},{64,0},{96,32},{1,65},{33,97},{65,1},{97,33},{2,66}... | collective-permute-start | bytes 1572872 | tf_op jit(solution)/shard_map/ppermute | solution.py:19
  20.1 14.3 %collective-permute-start.5 = (bf16[8,32,1024]{2,1,0:T(8,128)(2,1)S(1)}, bf16[8,32,1024]{2,1,0:T(8,128)(2,1)}, u32[]{:S(2)}, u32[]{:S(2)}) collective-permute-start(bf16[8,32,1024]{2,1,0:T(8,128)(2,1)S(1)} %get-tuple-element.42.refs_3_.refs_2_), channel_id=1, source_target_pairs={{0,2},{1,3},{2,0},{3,1},{4,6},{5,7},{6,4},{7,5},{8,10},{9,11},{10,... | collective-permute-start | bytes 1572872 | tf_op jit(solution)/shard_map/ppermute | solution.py:23
  22.0 12.4 %collective-permute-start.3 = (bf16[8,32,1024]{2,1,0:T(8,128)(2,1)}, bf16[8,32,1024]{2,1,0:T(8,128)(2,1)S(1)}, u32[]{:S(2)}, u32[]{:S(2)}) collective-permute-start(bf16[8,32,1024]{2,1,0:T(8,128)(2,1)} %collective-permute-done.2.refs_11_.refs_6_), channel_id=1, source_target_pairs={{0,1},{1,0},{2,3},{3,2},{4,5},{5,4},{6,7},{7,6},{8,9},{9,8},{10,11... | collective-permute-start | bytes 1572872 | tf_op jit(solution)/shard_map/ppermute | solution.py:23
  34.5 27.5 %collective-permute-start.6 = (bf16[8,8,64,128]{3,2,1,0:T(8,128)(2,1)}, bf16[8,8,64,128]{3,2,1,0:T(8,128)(2,1)}, u32[]{:S(2)}, u32[]{:S(2)}) collective-permute-start(bf16[8,8,64,128]{3,2,1,0:T(8,128)(2,1)} %all-to-all-done.refs_0_), channel_id=1, source_target_pairs={{0,32},{32,64},{64,96},{96,0},{1,33},{33,65},{65,97},{97,1},{2,34}... | collective-permute-start | bytes 3145736 | tf_op jit(solution)/shard_map/ppermute | solution.py:19
  35.2 28.2 %collective-permute-start.7 = (bf16[8,8,64,128]{3,2,1,0:T(8,128)(2,1)}, bf16[8,8,64,128]{3,2,1,0:T(8,128)(2,1)}, u32[]{:S(2)}, u32[]{:S(2)}) collective-permute-start(bf16[8,8,64,128]{3,2,1,0:T(8,128)(2,1)} %all-to-all-done.refs_0_), channel_id=1, source_target_pairs={{0,96},{32,0},{64,32},{96,64},{1,97},{33,1},{65,33},{97,65},{2,98}... | collective-permute-start | bytes 3145736 | tf_op jit(solution)/shard_map/ppermute | solution.py:19
  37.8 23.8 %all-to-all-start.2 = ((bf16[8,8,64,128]{3,2,1,0:T(8,128)(2,1)}), bf16[8,8,64,128]{3,2,1,0:T(8,128)(2,1)}, u32[]{:S(2)}, u32[]{:S(2)}) async-start(bf16[8,8,64,128]{3,2,1,0:T(8,128)(2,1)} %order_amps.3), calls=%async_computation.2 | async-start | bytes 2097152 | tf_op jit(solution)/shard_map/all_to_all | solution.py:27
  45.6 14.9 %collective-permute-start.8 = (bf16[8,32,1024]{2,1,0:T(8,128)(2,1)S(1)}, bf16[8,32,1024]{2,1,0:T(8,128)(2,1)S(1)}, u32[]{:S(2)}, u32[]{:S(2)}) collective-permute-start(bf16[8,32,1024]{2,1,0:T(8,128)(2,1)S(1)} %collective-permute-done.refs_7_.refs_2_), channel_id=1, source_target_pairs={{0,2},{1,3},{2,0},{3,1},{4,6},{5,7},{6,4},{7,5},{8,10},{9,11},{10,... | collective-permute-start | bytes 1572872 | tf_op jit(solution)/shard_map/ppermute | solution.py:23
  45.7 18.0 %collective-permute-start.10 = (bf16[8,32,1024]{2,1,0:T(8,128)(2,1)S(1)}, bf16[8,32,1024]{2,1,0:T(8,128)(2,1)}, u32[]{:S(2)}, u32[]{:S(2)}) collective-permute-start(bf16[8,32,1024]{2,1,0:T(8,128)(2,1)S(1)} %get-tuple-element.42.refs_3_.refs_2_), channel_id=1, source_target_pairs={{0,1},{1,0},{2,3},{3,2},{4,5},{5,4},{6,7},{7,6},{8,9},{9,8},{10,11... | collective-permute-start | bytes 1572872 | tf_op jit(solution)/shard_map/ppermute | solution.py:23
  45.8 26.1 %collective-permute-start.13 = (bf16[8,32,1024]{2,1,0:T(8,128)(2,1)}, bf16[8,32,1024]{2,1,0:T(8,128)(2,1)}, u32[]{:S(2)}, u32[]{:S(2)}) collective-permute-start(bf16[8,32,1024]{2,1,0:T(8,128)(2,1)} %collective-permute-done.2.refs_11_.refs_6_), channel_id=1, source_target_pairs={{0,2},{1,3},{2,0},{3,1},{4,6},{5,7},{6,4},{7,5},{8,10},{9,11},{10,... | collective-permute-start | bytes 1572872 | tf_op jit(solution)/shard_map/ppermute | solution.py:23
  61.6 24.3 %collective-permute-start.19 = (bf16[8,8,64,128]{3,2,1,0:T(8,128)(2,1)}, bf16[8,8,64,128]{3,2,1,0:T(8,128)(2,1)}, u32[]{:S(2)}, u32[]{:S(2)}) collective-permute-start(bf16[8,8,64,128]{3,2,1,0:T(8,128)(2,1)} %all-to-all-done.2.refs_0_), channel_id=1, source_target_pairs={{0,96},{32,0},{64,32},{96,64},{1,97},{33,1},{65,33},{97,65},{2,98}... | collective-permute-start | bytes 3145736 | tf_op jit(solution)/shard_map/ppermute | solution.py:19
  62.1 19.5 %collective-permute-start.16 = (bf16[8,32,1024]{2,1,0:T(8,128)(2,1)S(1)}, bf16[8,32,1024]{2,1,0:T(8,128)(2,1)S(1)}, u32[]{:S(2)}, u32[]{:S(2)}) collective-permute-start(bf16[8,32,1024]{2,1,0:T(8,128)(2,1)S(1)} %collective-permute-done.4.refs_1_.refs_6_), channel_id=1, source_target_pairs={{0,2},{1,3},{2,0},{3,1},{4,6},{5,7},{6,4},{7,5},{8,10},{9,11},{10,... | collective-permute-start | bytes 1572872 | tf_op jit(solution)/shard_map/ppermute | solution.py:23
  63.4 30.1 %collective-permute-start.9 = (bf16[8,8,64,128]{3,2,1,0:T(8,128)(2,1)}, bf16[8,8,64,128]{3,2,1,0:T(8,128)(2,1)}, u32[]{:S(2)}, u32[]{:S(2)}) collective-permute-start(bf16[8,8,64,128]{3,2,1,0:T(8,128)(2,1)} %collective-permute-done.6.refs_1_), channel_id=1, source_target_pairs={{0,32},{32,64},{64,96},{96,0},{1,33},{33,65},{65,97},{97,1},{2,34}... | collective-permute-start | bytes 3145736 | tf_op jit(solution)/shard_map/ppermute | solution.py:19
  63.8 17.8 %collective-permute-start.12 = (bf16[8,32,1024]{2,1,0:T(8,128)(2,1)S(1)}, bf16[8,32,1024]{2,1,0:T(8,128)(2,1)S(1)}, u32[]{:S(2)}, u32[]{:S(2)}) collective-permute-start(bf16[8,32,1024]{2,1,0:T(8,128)(2,1)S(1)} %collective-permute-done.8.refs_9_.refs_4_), channel_id=1, source_target_pairs={{0,1},{1,0},{2,3},{3,2},{4,5},{5,4},{6,7},{7,6},{8,9},{9,8},{10,11... | collective-permute-start | bytes 1572872 | tf_op jit(solution)/shard_map/ppermute | solution.py:23
  71.9 10.3 %collective-permute-start.11 = (bf16[8,32,1024]{2,1,0:T(8,128)(2,1)}, bf16[8,32,1024]{2,1,0:T(8,128)(2,1)}, u32[]{:S(2)}, u32[]{:S(2)}) collective-permute-start(bf16[8,32,1024]{2,1,0:T(8,128)(2,1)} %collective-permute-done.5.refs_5_.refs_4_), channel_id=1, source_target_pairs={{0,1},{1,0},{2,3},{3,2},{4,5},{5,4},{6,7},{7,6},{8,9},{9,8},{10,11... | collective-permute-start | bytes 1572872 | tf_op jit(solution)/shard_map/ppermute | solution.py:23
  81.6 6.0 %collective-permute-start.14 = (bf16[8,32,1024]{2,1,0:T(8,128)(2,1)}, bf16[8,32,1024]{2,1,0:T(8,128)(2,1)}, u32[]{:S(2)}, u32[]{:S(2)}) collective-permute-start(bf16[8,32,1024]{2,1,0:T(8,128)(2,1)} %collective-permute-done.13.refs_13_.refs_8_), channel_id=1, source_target_pairs={{0,1},{1,0},{2,3},{3,2},{4,5},{5,4},{6,7},{7,6},{8,9},{9,8},{10,11... | collective-permute-start | bytes 1572872 | tf_op jit(solution)/shard_map/ppermute | solution.py:23
  81.6 11.9 %collective-permute-start.17 = (bf16[8,32,1024]{2,1,0:T(8,128)(2,1)S(1)}, bf16[8,32,1024]{2,1,0:T(8,128)(2,1)S(1)}, u32[]{:S(2)}, u32[]{:S(2)}) collective-permute-start(bf16[8,32,1024]{2,1,0:T(8,128)(2,1)S(1)} %collective-permute-done.16.refs_3_.refs_8_), channel_id=1, source_target_pairs={{0,1},{1,0},{2,3},{3,2},{4,5},{5,4},{6,7},{7,6},{8,9},{9,8},{10,11... | collective-permute-start | bytes 1572872 | tf_op jit(solution)/shard_map/ppermute | solution.py:23
  82.2 29.6 %collective-permute-start.18 = (bf16[8,8,64,128]{3,2,1,0:T(8,128)(2,1)}, bf16[8,8,64,128]{3,2,1,0:T(8,128)(2,1)}, u32[]{:S(2)}, u32[]{:S(2)}) collective-permute-start(bf16[8,8,64,128]{3,2,1,0:T(8,128)(2,1)} %all-to-all-done.2.refs_0_), channel_id=1, source_target_pairs={{0,32},{32,64},{64,96},{96,0},{1,33},{33,65},{65,97},{97,1},{2,34}... | collective-permute-start | bytes 3145736 | tf_op jit(solution)/shard_map/ppermute | solution.py:19
  85.9 25.9 %collective-permute-start.20 = (bf16[8,8,64,128]{3,2,1,0:T(8,128)(2,1)}, bf16[8,8,64,128]{3,2,1,0:T(8,128)(2,1)}, u32[]{:S(2)}, u32[]{:S(2)}) collective-permute-start(bf16[8,8,64,128]{3,2,1,0:T(8,128)(2,1)} %collective-permute-done.19.refs_1_), channel_id=1, source_target_pairs={{0,96},{32,0},{64,32},{96,64},{1,97},{33,1},{65,33},{97,65},{2,98}... | collective-permute-start | bytes 3145736 | tf_op jit(solution)/shard_map/ppermute | solution.py:19
  97.2 22.0 %all-to-all-start.1 = ((bf16[8,8,64,128]{3,2,1,0:T(8,128)(2,1)}), bf16[8,8,64,128]{3,2,1,0:T(8,128)(2,1)S(1)}, u32[]{:S(2)}, u32[]{:S(2)}) async-start(bf16[8,8,64,128]{3,2,1,0:T(8,128)(2,1)} %product.5), calls=%async_computation.1 | async-start | bytes 2097152 | tf_op jit(solution)/shard_map/all_to_all | solution.py:27
  119.2 19.2 %all-to-all-start.3 = ((bf16[8,8,64,128]{3,2,1,0:T(8,128)(2,1)}), bf16[8,8,64,128]{3,2,1,0:T(8,128)(2,1)S(1)}, u32[]{:S(2)}, u32[]{:S(2)}) async-start(bf16[8,8,64,128]{3,2,1,0:T(8,128)(2,1)} %product.7), calls=%async_computation.3 | async-start | bytes 2097152 | tf_op jit(solution)/shard_map/all_to_all | solution.py:27
  (17 other events, 279.5 us)

commit v4 on v3

--- a/solution.py
+++ b/solution.py
@@ -9,7 +9,7 @@
 
 IRREPS = 8
 STEPS = (64, 64)
-VMEM_PRODUCT = 44
+VMEM_PRODUCT = 24
 AHEAD = 2
 MIB = 1 << 20
 
@@ -95,95 +95,118 @@
     )(integrals)
 
 
-def product_body(plan, blocks, has_sum, quarter_ref, *refs):
+def quarter_copies(refs, chosen, slot, quarter, sems):
+    nk, rows, _ = refs[0].shape
+    found = []
+    for d, ref in enumerate(refs):
+        place = pl.multiple_of(jnp.bitwise_xor(quarter, d) * rows, rows)
+        found.append(
+            pltpu.make_async_copy(
+                ref, chosen.at[pl.ds(slot * nk, nk), pl.ds(place, rows), :], sems.at[4 * slot + d]
+            )
+        )
+    return found
+
+
+def product_body(plan, held, has_sum, is_held, quarter_ref, *refs):
     count = len(plan)
-    pieces, w_refs = refs[:count], refs[count:count + 4 * len(blocks)]
-    sum_refs = refs[count + 4 * len(blocks):][:1] if has_sum else ()
-    out_ref, lhs, chosen, total, piece_sems, w_sems = refs[-6:]
-    nk, rows, width = w_refs[0].shape
-    ni, _, step, cols = pieces[0].shape
+    pieces, refs = refs[:count], refs[count:]
+    w_refs, refs = (refs[:1], refs[1:]) if is_held else (refs[:4 * (count + held)], refs[4 * (count + held):])
+    sum_refs, refs = (refs[:1], refs[1:]) if has_sum else ((), refs)
+    out_ref, refs = refs[0], refs[1:]
+    held_ref, refs = (refs[0], refs[1:]) if held else (None, refs)
+    lhs, total, piece_sems, *refs = refs
+    chosen, w_sems, *held_sems = (w_refs[0], None) if is_held else refs
+    width = w_refs[0].shape[2]
+    ni, nk, step, cols = pieces[0].shape
     quarter = quarter_ref[0]
 
     def copies(slot):
-        found = []
-        for d in range(4):
-            place = pl.multiple_of(jnp.bitwise_xor(quarter, d) * rows, rows)
-            found.append(
-                pltpu.make_async_copy(
-                    w_refs[4 * slot + d],
-                    chosen.at[pl.ds(slot * nk, nk), pl.ds(place, rows), :],
-                    w_sems.at[4 * slot + d],
-                )
-            )
-        n = plan.index(blocks[slot])
-        found.append(
-            pltpu.make_async_copy(pieces[n], lhs.at[pl.ds(slot * ni, ni)], piece_sems.at[slot])
-        )
+        found = [pltpu.make_async_copy(pieces[slot], lhs.at[pl.ds(slot * ni, ni)], piece_sems.at[slot])]
+        if not is_held:
+            found += quarter_copies(w_refs[4 * slot:4 * slot + 4], chosen, slot, quarter, w_sems)
         return found
 
-    waiting = [copies(slot) for slot in range(len(blocks))]
-    for slot in range(min(AHEAD, len(blocks))):
+    waiting = [copies(slot) for slot in range(count)]
+    later = []
+    for n in range(held):
+        first = 4 * (count + n)
+        later += quarter_copies(w_refs[first:first + 4], held_ref, n, quarter, held_sems[0])
+    for slot in range(min(AHEAD, count)):
         for copy in waiting[slot]:
             copy.start()
-    for slot in range(len(blocks)):
+    for slot in range(count):
         for copy in waiting[slot]:
             copy.wait()
-        if slot + AHEAD < len(blocks):
+        if slot + AHEAD < count:
             for copy in waiting[slot + AHEAD]:
+                copy.start()
+        if slot == 0:
+            for copy in later:
                 copy.start()
         left = jnp.concatenate(
             [lhs[slot * ni:(slot + 1) * ni, k].reshape(ni * step, cols) for k in range(nk)], axis=1
         )
-        right = chosen[slot * nk:(slot + 1) * nk].reshape(nk * 4 * rows, width)
+        right = chosen[slot * nk:(slot + 1) * nk].reshape(nk * cols, width)
         sums = jnp.dot(left, right, preferred_element_type=jnp.float32)
         if slot == 0:
             if has_sum:
                 sums = sums + sum_refs[0][...]
         else:
             sums = sums + total[...]
-        if slot < len(blocks) - 1:
+        if slot < count - 1:
             total[...] = sums
         elif out_ref.dtype == jnp.float32:
             out_ref[...] = sums
         else:
             for j in range(width // cols):
                 out_ref[:, j] = sums[:, j * cols:(j + 1) * cols].astype(out_ref.dtype).reshape(ni, step, cols)
-
-
-def product(pieces, plan, chosen, blocks, quarter, sums=None, last=True):
-    nk, step, cols = pieces[0].shape[1:]
-    ni = IRREPS
-    rows, width = chosen[0][0].shape[1:]
+    for copy in later:
+        copy.wait()
+
+
+def product(pieces, plan, chosen, quarter, sums=None, last=True, hold=()):
+    ni, nk, step, cols = pieces[0].shape
+    is_held = not isinstance(chosen, list)
+    width = chosen.shape[2] if is_held else chosen[0][0].shape[2]
     js = width // cols
-    w_parts = [part for block in blocks for part in chosen[block]]
+    w_parts = [chosen] if is_held else [part for block in (*plan, *hold) for part in chosen[block]]
     if sums is None:
         pieces = [pltpu.with_memory_space_constraint(piece, pltpu.HBM) for piece in pieces]
         w_parts = [pltpu.with_memory_space_constraint(part, pltpu.HBM) for part in w_parts]
     operands = [quarter.reshape(1), *pieces, *w_parts]
     in_specs = [pl.BlockSpec(memory_space=pltpu.SMEM)]
     in_specs += [pl.BlockSpec(memory_space=pl.ANY)] * (len(operands) - 1)
+    if is_held:
+        in_specs[-1] = pl.BlockSpec(memory_space=pltpu.VMEM)
+        operands[-1] = pltpu.with_memory_space_constraint(chosen, pltpu.VMEM)
     if sums is not None:
         in_specs.append(pl.BlockSpec(memory_space=pltpu.VMEM))
         operands.append(sums)
     if last:
-        out_shape = [jax.ShapeDtypeStruct((ni, js, step, cols), chosen[0][0].dtype)]
+        out_shape = [jax.ShapeDtypeStruct((ni, js, step, cols), pieces[0].dtype)]
     else:
         out_shape = [jax.ShapeDtypeStruct((ni * step, width), jnp.float32)]
-    depth = nk * 4 * rows * len(blocks)
+    if hold:
+        out_shape.append(pltpu.VMEM((nk * len(hold), cols, width), pieces[0].dtype))
+    count = len(plan)
+    scratch = [
+        pltpu.VMEM((ni * count, nk, step, cols), pieces[0].dtype),
+        pltpu.VMEM((ni * step, width), jnp.float32),
+        pltpu.SemaphoreType.DMA((count,)),
+    ]
+    if not is_held:
+        scratch += [pltpu.VMEM((nk * count, cols, width), pieces[0].dtype), pltpu.SemaphoreType.DMA((4 * count,))]
+    if hold:
+        scratch.append(pltpu.SemaphoreType.DMA((4 * len(hold),)))
     return pl.pallas_call(
-        functools.partial(product_body, plan, blocks, sums is not None),
+        functools.partial(product_body, plan, len(hold), sums is not None, is_held),
         out_shape=out_shape,
         in_specs=in_specs,
-        out_specs=[pl.BlockSpec(memory_space=pltpu.VMEM)],
-        scratch_shapes=[
-            pltpu.VMEM((ni * len(blocks), nk, step, cols), chosen[0][0].dtype),
-            pltpu.VMEM((nk * len(blocks), 4 * rows, width), chosen[0][0].dtype),
-            pltpu.VMEM((ni * step, width), jnp.float32),
-            pltpu.SemaphoreType.DMA((len(pieces),)),
-            pltpu.SemaphoreType.DMA((len(w_parts),)),
-        ],
+        out_specs=[pl.BlockSpec(memory_space=pltpu.VMEM)] * len(out_shape),
+        scratch_shapes=scratch,
         compiler_params=params(VMEM_PRODUCT),
-        cost_estimate=cost(2 * ni * step * depth * width, 2 * depth * width + 2 * ni * step * depth),
+        cost_estimate=cost(0, 0),
         name="product",
     )(*operands)
 
@@ -246,18 +269,18 @@
 
     near = by_j[0]
     arrived = [near, shift_rep(by_j[1], 1), shift_rep(by_j[3], -1), shift_rep(by_j[2], 2)]
+    by_group2 = order_amps(after(amps, arrived[1]), pair_irreps, STEPS[0], STEPS[1])
+    arrived[2], by_group2 = lax.optimization_barrier((arrived[2], by_group2))
     zl = [flip_ten(part, 2) for part in arrived]
     core = [flip_ten(part, 1) for part in arrived]
     both = [flip_ten(part, 1) for part in zl]
 
     first = exchange_irreps(by_group, groups)
-    by_group2 = order_amps(after(amps, core[1]), pair_irreps, STEPS[0], STEPS[1])
-    first, core[1], core[2], arrived[3], zl[0], by_group2 = lax.optimization_barrier(
-        (first, core[1], core[2], arrived[3], zl[0], by_group2)
+    first, near, core[1], core[2], zl[0], by_group2 = lax.optimization_barrier(
+        (first, near, core[1], core[2], zl[0], by_group2)
     )
-    core[3], zl[3] = flip_ten(arrived[3], 1), flip_ten(arrived[3], 2)
-    both[0] = flip_ten(zl[0], 1)
-    by_group2, core[3] = lax.optimization_barrier((by_group2, core[3]))
+    core[0], both[0] = flip_ten(near, 1), flip_ten(zl[0], 1)
+    by_group2, core[0], core[3] = lax.optimization_barrier((by_group2, core[0], core[3]))
     second = exchange_irreps(by_group2, groups)
 
     left, right = shift_rep(first, 1), shift_rep(first, -1)
@@ -270,13 +293,13 @@
     both[2], both[3] = flip_ten(zl[2], 1), flip_ten(zl[3], 1)
     chosen = [(arrived[n], core[n], zl[n], both[n]) for n in range(ranks)]
 
-    (sums,) = product((first, left, right), (0, 1, 2), chosen, (0, 1, 2), quarter, last=False)
+    (sums,) = product((first, left, right), (0, 1, 2), chosen, quarter, last=False)
     far, sums = lax.optimization_barrier((far, sums))
-    (out,) = product((far,), (3,), chosen, (3,), quarter, sums=sums)
+    (out,) = product((far,), (3,), chosen, quarter, sums=sums)
     back = exchange_irreps(out, groups)
-    (sums,) = product((second, right2), (0, 2), chosen, (0, 2), quarter, last=False)
-    left2, far2, sums = lax.optimization_barrier((left2, far2, sums))
-    (out2,) = product((left2, far2), (1, 3), chosen, (1, 3), quarter, sums=sums)
+    sums, held = product((second, right2), (0, 2), chosen, quarter, last=False, hold=(1, 3))
+    left2, far2, sums, held = lax.optimization_barrier((left2, far2, sums, held))
+    (out2,) = product((left2, far2), (1, 3), held, quarter, sums=sums)
     pair_xor = jnp.bitwise_xor(pair_irreps[0], pair_irreps[1])
     back, out2 = lax.optimization_barrier((back, out2))
     back2 = exchange_irreps(out2, groups)

time: 140 us -> 138 us (0.986)
  Pallas kernels: 28.8 us -> 27.3 us
  waiting for transfers between devices: 62.8 us -> 61.3 us
    ppermute x12, waiting for transfers between devices: 31.2 us -> 17.5 us  [flip_ten(): lax.ppermute(array, 'ten', [(s, s ^ mask) for s in range(lax.axis_size('t...]
    all_to_all x4, waiting for transfers between devices: 15.8 us -> 28 us  [exchange_irreps(): lax.all_to_all(array, 'ten', split_axis=0, concat_axis=0, axis_index_grou...]
    ppermute x9, starting transfers between devices: 11.1 us -> 14.5 us  [shift_rep(): lax.ppermute(array, 'rep', [(s, (s + distance) % n) for s in range(n)])]
    ppermute x12, starting transfers between devices: 5.97 us -> 3.32 us  [flip_ten(): lax.ppermute(array, 'ten', [(s, s ^ mask) for s in range(lax.axis_size('t...]
    pallas_call x4, Pallas kernels: 19.4 us -> 17.9 us  [product(): pl.pallas_call(functools.partial(product_body, plan, len(hold), sums is n...]
  transfers between devices with their start and end apart: 25 -> 25, of which waited for: 11 -> 9; matrix products, arithmetic and copies ran while one was open for 0% -> 0% of each run, Pallas kernels for 19% -> 18%
where the time goes in v4:
time: 138 us; the launch traced here: 137 us
  waiting for transfers between devices  61.3 us (44%)
  starting transfers between devices  44.2 us (32%)
  Pallas kernels  27.3 us (20%)
  local copies, waits for them, and re-layouts  3.04 us (2%)
  between operations  1.64 us (1%)
    all_to_all x4, waiting for transfers between devices, exchange_irreps(): lax.all_to_all(array, 'ten', split_axis=0, concat_axis=0, axis_index_grou...  28 us
    all_to_all x4, starting transfers between devices, exchange_irreps(): lax.all_to_all(array, 'ten', split_axis=0, concat_axis=0, axis_index_grou...  26.4 us
    pallas_call x4, Pallas kernels, product(): pl.pallas_call(functools.partial(product_body, plan, len(hold), sums is n...  17.9 us
    ppermute x12, waiting for transfers between devices, flip_ten(): lax.ppermute(array, 'ten', [(s, s ^ mask) for s in range(lax.axis_size('t...  17.5 us
    ppermute x9, waiting for transfers between devices, shift_rep(): lax.ppermute(array, 'rep', [(s, (s + distance) % n) for s in range(n)])  15.8 us
    ppermute x9, starting transfers between devices, shift_rep(): lax.ppermute(array, 'rep', [(s, (s + distance) % n) for s in range(n)])  14.5 us
    pallas_call x2, Pallas kernels, order_amps(): pl.pallas_call(functools.partial(order_body, offset), out_shape=pltpu.VME...  5.76 us
    ppermute x12, starting transfers between devices, flip_ten(): lax.ppermute(array, 'ten', [(s, s ^ mask) for s in range(lax.axis_size('t...  3.32 us
  transfers between devices with their start and end apart: 25, of which 9 were waited for; matrix products, arithmetic and copies ran while one was open for 0% of the time, Pallas kernels for 18%

profile of v4, /device:TPU:0, one launch (start us, length us, event | category | flops | bytes accessed | tf_op | source)
XLA Modules:
  0.0 137.4 jit_solution(6332998013493616617)
XLA Ops:
  3.2 1.6 %collective-permute-start = (bf16[8,32,1024]{2,1,0:T(8,128)(2,1)S(1)}, bf16[8,32,1024]{2,1,0:T(8,128)(2,1)S(1)}, u32[]{:S(2)}, u32[]{:S(2)}) collective-permute-start(bf16[8,32,1024]{2,1,0:T(8,128)(2,1)S(1)} %get-tuple-element.46), channel_id=1, source_target_pairs={{0,32},{32,64},{64,96},{96,0},{1,33},{33,65},{65,97},{97,1},{2,34}... | collective-permute-start | bytes 1572872 | tf_op jit(solution)/shard_map/ppermute | solution.py:19
  4.9 1.7 %collective-permute-start.2 = (bf16[8,32,1024]{2,1,0:T(8,128)(2,1)S(1)}, bf16[8,32,1024]{2,1,0:T(8,128)(2,1)}, u32[]{:S(2)}, u32[]{:S(2)}) collective-permute-start(bf16[8,32,1024]{2,1,0:T(8,128)(2,1)S(1)} %get-tuple-element.47), channel_id=1, source_target_pairs={{0,96},{32,0},{64,32},{96,64},{1,97},{33,1},{65,33},{97,65},{2,98}... | collective-permute-start | bytes 1572872 | tf_op jit(solution)/shard_map/ppermute | solution.py:19
  6.5 2.9 %order_amps.2 = bf16[8,8,64,128]{3,2,1,0:T(8,128)(2,1)} custom-call(s32[2]{0:T(128)S(1)} %copy-done.6, bf16[8,8,128,128]{3,2,1,0:T(8,128)(2,1)} %bitcast.3), custom_call_target="tpu_custom_call" | custom-call | tf_op jit(solution)/shard_map/order_amps/pallas_call | solution.py:59
  9.4 8.0 %all-to-all-start = ((bf16[8,8,64,128]{3,2,1,0:T(8,128)(2,1)}), bf16[8,8,64,128]{3,2,1,0:T(8,128)(2,1)}, u32[]{:S(2)}, u32[]{:S(2)}) async-start(bf16[8,8,64,128]{3,2,1,0:T(8,128)(2,1)} %order_amps.2), calls=%async_computation | async-start | bytes 2097152 | tf_op jit(solution)/shard_map/all_to_all | solution.py:27
  17.5 1.9 %collective-permute-start.10 = (bf16[8,32,1024]{2,1,0:T(8,128)(2,1)S(1)}, bf16[8,32,1024]{2,1,0:T(8,128)(2,1)S(1)}, u32[]{:S(2)}, u32[]{:S(2)}) collective-permute-start(bf16[8,32,1024]{2,1,0:T(8,128)(2,1)S(1)} %get-tuple-element.56), channel_id=1, source_target_pairs={{0,64},{32,96},{64,0},{96,32},{1,65},{33,97},{65,1},{97,33},{2,66}... | collective-permute-start | bytes 1572872 | tf_op jit(solution)/shard_map/ppermute | solution.py:19
  19.4 2.9 %order_amps.3 = bf16[8,8,64,128]{3,2,1,0:T(8,128)(2,1)} custom-call(s32[2]{0:T(128)S(1)} %copy-done.6, bf16[8,8,128,128]{3,2,1,0:T(8,128)(2,1)} %bitcast.4), custom_call_target="tpu_custom_call" | custom-call | tf_op jit(solution)/shard_map/order_amps/pallas_call | solution.py:59
  22.9 9.0 %collective-permute-done.10.refs_1_.refs_14_ = bf16[8,32,1024]{2,1,0:T(8,128)(2,1)S(1)} collective-permute-done((bf16[8,32,1024]{2,1,0:T(8,128)(2,1)S(1)}, bf16[8,32,1024]{2,1,0:T(8,128)(2,1)S(1)}, u32[]{:S(2)}, u32[]{:S(2)}) %collective-permute-start.10) | collective-permute-done | bytes 524320 | tf_op jit(solution)/shard_map/ppermute | solution.py:19
  33.1 3.0 %collective-permute-start.6 = (bf16[8,8,64,128]{3,2,1,0:T(8,128)(2,1)}, bf16[8,8,64,128]{3,2,1,0:T(8,128)(2,1)}, u32[]{:S(2)}, u32[]{:S(2)}) collective-permute-start(bf16[8,8,64,128]{3,2,1,0:T(8,128)(2,1)} %all-to-all-done.refs_0_), channel_id=1, source_target_pairs={{0,96},{32,0},{64,32},{96,64},{1,97},{33,1},{65,33},{97,65},{2,98}... | collective-permute-start | bytes 3145736 | tf_op jit(solution)/shard_map/ppermute | solution.py:19
  36.0 8.2 %all-to-all-start.2 = ((bf16[8,8,64,128]{3,2,1,0:T(8,128)(2,1)}), bf16[8,8,64,128]{3,2,1,0:T(8,128)(2,1)}, u32[]{:S(2)}, u32[]{:S(2)}) async-start(bf16[8,8,64,128]{3,2,1,0:T(8,128)(2,1)} %order_amps.3), calls=%async_computation.2 | async-start | bytes 2097152 | tf_op jit(solution)/shard_map/all_to_all | solution.py:27
  44.4 2.0 %collective-permute-start.14 = (bf16[8,32,1024]{2,1,0:T(8,128)(2,1)}, bf16[8,32,1024]{2,1,0:T(8,128)(2,1)}, u32[]{:S(2)}, u32[]{:S(2)}) collective-permute-start(bf16[8,32,1024]{2,1,0:T(8,128)(2,1)} %collective-permute-done.2.refs_11_.refs_6_), channel_id=1, source_target_pairs={{0,2},{1,3},{2,0},{3,1},{4,6},{5,7},{6,4},{7,5},{8,10},{9,11},{10,... | collective-permute-start | bytes 1572872 | tf_op jit(solution)/shard_map/ppermute | solution.py:23
  46.4 13.9 %all-to-all-done.2.refs_0_ = bf16[8,8,64,128]{3,2,1,0:T(8,128)(2,1)} async-done(((bf16[8,8,64,128]{3,2,1,0:T(8,128)(2,1)}), bf16[8,8,64,128]{3,2,1,0:T(8,128)(2,1)}, u32[]{:S(2)}, u32[]{:S(2)}) %all-to-all-start.2) | async-done | bytes 1048608 | tf_op jit(solution)/shard_map/all_to_all | solution.py:27
  60.3 2.3 %collective-permute-start.19 = (bf16[8,8,64,128]{3,2,1,0:T(8,128)(2,1)}, bf16[8,8,64,128]{3,2,1,0:T(8,128)(2,1)}, u32[]{:S(2)}, u32[]{:S(2)}) collective-permute-start(bf16[8,8,64,128]{3,2,1,0:T(8,128)(2,1)} %all-to-all-done.2.refs_0_), channel_id=1, source_target_pairs={{0,96},{32,0},{64,32},{96,64},{1,97},{33,1},{65,33},{97,65},{2,98}... | collective-permute-start | bytes 3145736 | tf_op jit(solution)/shard_map/ppermute | solution.py:19
  62.8 7.7 %collective-permute-done.14.refs_13_.refs_8_ = bf16[8,32,1024]{2,1,0:T(8,128)(2,1)} collective-permute-done((bf16[8,32,1024]{2,1,0:T(8,128)(2,1)}, bf16[8,32,1024]{2,1,0:T(8,128)(2,1)}, u32[]{:S(2)}, u32[]{:S(2)}) %collective-permute-start.14) | collective-permute-done | bytes 524320 | tf_op jit(solution)/shard_map/ppermute | solution.py:23
  70.6 9.7 %collective-permute-done.16.refs_3_.refs_16_ = bf16[8,32,1024]{2,1,0:T(8,128)(2,1)S(1)} collective-permute-done((bf16[8,32,1024]{2,1,0:T(8,128)(2,1)S(1)}, bf16[8,32,1024]{2,1,0:T(8,128)(2,1)S(1)}, u32[]{:S(2)}, u32[]{:S(2)}) %collective-permute-start.16) | collective-permute-done | bytes 524320 | tf_op jit(solution)/shard_map/ppermute | solution.py:23
  81.6 3.0 %collective-permute-done.19.refs_1_ = bf16[8,8,64,128]{3,2,1,0:T(8,128)(2,1)} collective-permute-done((bf16[8,8,64,128]{3,2,1,0:T(8,128)(2,1)}, bf16[8,8,64,128]{3,2,1,0:T(8,128)(2,1)}, u32[]{:S(2)}, u32[]{:S(2)}) %collective-permute-start.19) | collective-permute-done | bytes 1048608 | tf_op jit(solution)/shard_map/ppermute | solution.py:19
  84.6 3.6 %collective-permute-start.20 = (bf16[8,8,64,128]{3,2,1,0:T(8,128)(2,1)}, bf16[8,8,64,128]{3,2,1,0:T(8,128)(2,1)}, u32[]{:S(2)}, u32[]{:S(2)}) collective-permute-start(bf16[8,8,64,128]{3,2,1,0:T(8,128)(2,1)} %collective-permute-done.19.refs_1_), channel_id=1, source_target_pairs={{0,96},{32,0},{64,32},{96,64},{1,97},{33,1},{65,33},{97,65},{2,98}... | collective-permute-start | bytes 3145736 | tf_op jit(solution)/shard_map/ppermute | solution.py:19
  88.2 5.8 %product.4.refs_5_ = f32[512,1024]{1,0:T(8,128)S(1)} custom-call(s32[1]{0:T(128)} %bitcast.quarter_ref, bf16[8,8,64,128]{3,2,1,0:T(8,128)(2,1)} %all-to-all-done.refs_0_, bf16[8,8,64,128]{3,2,1,0:T(8,128)(2,1)} %collective-permute-done.5.refs_1_, bf16[8,8,64,128]{3,2,1,0:T(8,128)(2,1)} %collective-permute-done.6.refs_2_, bf16[8,32,1024]{2,1,0:T(8,128)(2,1)} %copy-done.1, ...), custom_call_target="tpu_custom_call" | custom-call | tf_op jit(solution)/shard_map/product/pallas_call | solution.py:202
  94.1 2.5 %product.5 = bf16[8,8,64,128]{3,2,1,0:T(8,128)(2,1)} custom-call(s32[1]{0:T(128)} %bitcast.quarter_ref, bf16[8,8,64,128]{3,2,1,0:T(8,128)(2,1)S(1)} %collective-permute-done.8.refs_0_, bf16[8,32,1024]{2,1,0:T(8,128)(2,1)S(1)} %collective-permute-done.10.refs_1_.refs_14_, bf16[8,32,1024]{2,1,0:T(8,128)(2,1)S(1)} %collective-permute-done.11.refs_2_.refs_15_, ...), custom_call_target="tpu_custom_call" | custom-call | tf_op jit(solution)/shard_map/product/pallas_call | solution.py:202
  96.6 5.3 %all-to-all-start.1 = ((bf16[8,8,64,128]{3,2,1,0:T(8,128)(2,1)}), bf16[8,8,64,128]{3,2,1,0:T(8,128)(2,1)S(1)}, u32[]{:S(2)}, u32[]{:S(2)}) async-start(bf16[8,8,64,128]{3,2,1,0:T(8,128)(2,1)} %product.5), calls=%async_computation.1 | async-start | bytes 2097152 | tf_op jit(solution)/shard_map/all_to_all | solution.py:27
  101.9 4.7 %product.6 = (f32[512,1024]{1,0:T(8,128)S(1)}, bf16[16,128,1024]{2,1,0:T(8,128)(2,1)S(1)}) custom-call(s32[1]{0:T(128)} %bitcast.quarter_ref, bf16[8,8,64,128]{3,2,1,0:T(8,128)(2,1)} %all-to-all-done.2.refs_0_, bf16[8,8,64,128]{3,2,1,0:T(8,128)(2,1)} %collective-permute-done.19.refs_1_, bf16[8,32,1024]{2,1,0:T(8,128)(2,1)} %copy-done.1, ...), custom_call_target="tpu_custom_call" | custom-call | tf_op jit(solution)/shard_map/product/pallas_call | solution.py:202
  106.7 3.8 %collective-permute-done.18.refs_0_ = bf16[8,8,64,128]{3,2,1,0:T(8,128)(2,1)} collective-permute-done((bf16[8,8,64,128]{3,2,1,0:T(8,128)(2,1)}, bf16[8,8,64,128]{3,2,1,0:T(8,128)(2,1)}, u32[]{:S(2)}, u32[]{:S(2)}) %collective-permute-start.18) | collective-permute-done | bytes 1048608 | tf_op jit(solution)/shard_map/ppermute | solution.py:19
  110.5 4.8 %product.7 = bf16[8,8,64,128]{3,2,1,0:T(8,128)(2,1)} custom-call(s32[1]{0:T(128)} %bitcast.quarter_ref, bf16[8,8,64,128]{3,2,1,0:T(8,128)(2,1)} %collective-permute-done.18.refs_0_, bf16[8,8,64,128]{3,2,1,0:T(8,128)(2,1)} %collective-permute-done.20.refs_1_, bf16[16,128,1024]{2,1,0:T(8,128)(2,1)S(1)} %get-tuple-element.71.refs_2_, ...), custom_call_target="tpu_custom_call" | custom-call | tf_op jit(solution)/shard_map/product/pallas_call | solution.py:202
  116.7 4.8 %all-to-all-start.3 = ((bf16[8,8,64,128]{3,2,1,0:T(8,128)(2,1)}), bf16[8,8,64,128]{3,2,1,0:T(8,128)(2,1)S(1)}, u32[]{:S(2)}, u32[]{:S(2)}) async-start(bf16[8,8,64,128]{3,2,1,0:T(8,128)(2,1)} %product.7), calls=%async_computation.3 | async-start | bytes 2097152 | tf_op jit(solution)/shard_map/all_to_all | solution.py:27
  124.3 11.9 %all-to-all-done.3.part_ref = bf16[8,8,64,128]{3,2,1,0:T(8,128)(2,1)S(1)} async-done(((bf16[8,8,64,128]{3,2,1,0:T(8,128)(2,1)}), bf16[8,8,64,128]{3,2,1,0:T(8,128)(2,1)S(1)}, u32[]{:S(2)}, u32[]{:S(2)}) %all-to-all-start.3) | async-done | bytes 1048608 | tf_op jit(solution)/shard_map/all_to_all | solution.py:27
  (58 shorter events, 10.7 us)
Async XLA Ops:
  3.2 16.2 %collective-permute-start = (bf16[8,32,1024]{2,1,0:T(8,128)(2,1)S(1)}, bf16[8,32,1024]{2,1,0:T(8,128)(2,1)S(1)}, u32[]{:S(2)}, u32[]{:S(2)}) collective-permute-start(bf16[8,32,1024]{2,1,0:T(8,128)(2,1)S(1)} %get-tuple-element.46), channel_id=1, source_target_pairs={{0,32},{32,64},{64,96},{96,0},{1,33},{33,65},{65,97},{97,1},{2,34}... | collective-permute-start | bytes 1572872 | tf_op jit(solution)/shard_map/ppermute | solution.py:19
  4.9 17.4 %collective-permute-start.2 = (bf16[8,32,1024]{2,1,0:T(8,128)(2,1)S(1)}, bf16[8,32,1024]{2,1,0:T(8,128)(2,1)}, u32[]{:S(2)}, u32[]{:S(2)}) collective-permute-start(bf16[8,32,1024]{2,1,0:T(8,128)(2,1)S(1)} %get-tuple-element.47), channel_id=1, source_target_pairs={{0,96},{32,0},{64,32},{96,64},{1,97},{33,1},{65,33},{97,65},{2,98}... | collective-permute-start | bytes 1572872 | tf_op jit(solution)/shard_map/ppermute | solution.py:19
  9.4 23.2 %all-to-all-start = ((bf16[8,8,64,128]{3,2,1,0:T(8,128)(2,1)}), bf16[8,8,64,128]{3,2,1,0:T(8,128)(2,1)}, u32[]{:S(2)}, u32[]{:S(2)}) async-start(bf16[8,8,64,128]{3,2,1,0:T(8,128)(2,1)} %order_amps.2), calls=%async_computation | async-start | bytes 2097152 | tf_op jit(solution)/shard_map/all_to_all | solution.py:27
  17.5 14.4 %collective-permute-start.4 = (bf16[8,32,1024]{2,1,0:T(8,128)(2,1)S(1)}, bf16[8,32,1024]{2,1,0:T(8,128)(2,1)}, u32[]{:S(2)}, u32[]{:S(2)}) collective-permute-start(bf16[8,32,1024]{2,1,0:T(8,128)(2,1)S(1)} %get-tuple-element.55.refs_3_.refs_2_), channel_id=1, source_target_pairs={{0,2},{1,3},{2,0},{3,1},{4,6},{5,7},{6,4},{7,5},{8,10},{9,11},{10,... | collective-permute-start | bytes 1572872 | tf_op jit(solution)/shard_map/ppermute | solution.py:23
  17.5 14.4 %collective-permute-start.10 = (bf16[8,32,1024]{2,1,0:T(8,128)(2,1)S(1)}, bf16[8,32,1024]{2,1,0:T(8,128)(2,1)S(1)}, u32[]{:S(2)}, u32[]{:S(2)}) collective-permute-start(bf16[8,32,1024]{2,1,0:T(8,128)(2,1)S(1)} %get-tuple-element.56), channel_id=1, source_target_pairs={{0,64},{32,96},{64,0},{96,32},{1,65},{33,97},{65,1},{97,33},{2,66}... | collective-permute-start | bytes 1572872 | tf_op jit(solution)/shard_map/ppermute | solution.py:19
  22.3 10.3 %collective-permute-start.1 = (bf16[8,32,1024]{2,1,0:T(8,128)(2,1)S(1)}, bf16[8,32,1024]{2,1,0:T(8,128)(2,1)S(1)}, u32[]{:S(2)}, u32[]{:S(2)}) collective-permute-start(bf16[8,32,1024]{2,1,0:T(8,128)(2,1)S(1)} %collective-permute-done.refs_7_.refs_10_), channel_id=1, source_target_pairs={{0,1},{1,0},{2,3},{3,2},{4,5},{5,4},{6,7},{7,6},{8,9},{9,8},{10,11... | collective-permute-start | bytes 1572872 | tf_op jit(solution)/shard_map/ppermute | solution.py:23
  22.4 10.2 %collective-permute-start.3 = (bf16[8,32,1024]{2,1,0:T(8,128)(2,1)}, bf16[8,32,1024]{2,1,0:T(8,128)(2,1)}, u32[]{:S(2)}, u32[]{:S(2)}) collective-permute-start(bf16[8,32,1024]{2,1,0:T(8,128)(2,1)} %collective-permute-done.2.refs_11_.refs_6_), channel_id=1, source_target_pairs={{0,1},{1,0},{2,3},{3,2},{4,5},{5,4},{6,7},{7,6},{8,9},{9,8},{10,11... | collective-permute-start | bytes 1572872 | tf_op jit(solution)/shard_map/ppermute | solution.py:23
  31.9 4.1 %collective-permute-start.11 = (bf16[8,32,1024]{2,1,0:T(8,128)(2,1)S(1)}, bf16[8,32,1024]{2,1,0:T(8,128)(2,1)S(1)}, u32[]{:S(2)}, u32[]{:S(2)}) collective-permute-start(bf16[8,32,1024]{2,1,0:T(8,128)(2,1)S(1)} %collective-permute-done.10.refs_1_.refs_14_), channel_id=1, source_target_pairs={{0,1},{1,0},{2,3},{3,2},{4,5},{5,4},{6,7},{7,6},{8,9},{9,8},{10,11... | collective-permute-start | bytes 1572872 | tf_op jit(solution)/shard_map/ppermute | solution.py:23
  32.7 29.9 %collective-permute-start.5 = (bf16[8,8,64,128]{3,2,1,0:T(8,128)(2,1)}, bf16[8,8,64,128]{3,2,1,0:T(8,128)(2,1)}, u32[]{:S(2)}, u32[]{:S(2)}) collective-permute-start(bf16[8,8,64,128]{3,2,1,0:T(8,128)(2,1)} %all-to-all-done.refs_0_), channel_id=1, source_target_pairs={{0,32},{32,64},{64,96},{96,0},{1,33},{33,65},{65,97},{97,1},{2,34}... | collective-permute-start | bytes 3145736 | tf_op jit(solution)/shard_map/ppermute | solution.py:19
  33.1 29.6 %collective-permute-start.6 = (bf16[8,8,64,128]{3,2,1,0:T(8,128)(2,1)}, bf16[8,8,64,128]{3,2,1,0:T(8,128)(2,1)}, u32[]{:S(2)}, u32[]{:S(2)}) collective-permute-start(bf16[8,8,64,128]{3,2,1,0:T(8,128)(2,1)} %all-to-all-done.refs_0_), channel_id=1, source_target_pairs={{0,96},{32,0},{64,32},{96,64},{1,97},{33,1},{65,33},{97,65},{2,98}... | collective-permute-start | bytes 3145736 | tf_op jit(solution)/shard_map/ppermute | solution.py:19
  36.0 24.2 %all-to-all-start.2 = ((bf16[8,8,64,128]{3,2,1,0:T(8,128)(2,1)}), bf16[8,8,64,128]{3,2,1,0:T(8,128)(2,1)}, u32[]{:S(2)}, u32[]{:S(2)}) async-start(bf16[8,8,64,128]{3,2,1,0:T(8,128)(2,1)} %order_amps.3), calls=%async_computation.2 | async-start | bytes 2097152 | tf_op jit(solution)/shard_map/all_to_all | solution.py:27
  44.3 18.3 %collective-permute-start.7 = (bf16[8,32,1024]{2,1,0:T(8,128)(2,1)S(1)}, bf16[8,32,1024]{2,1,0:T(8,128)(2,1)S(1)}, u32[]{:S(2)}, u32[]{:S(2)}) collective-permute-start(bf16[8,32,1024]{2,1,0:T(8,128)(2,1)S(1)} %collective-permute-done.refs_7_.refs_10_), channel_id=1, source_target_pairs={{0,2},{1,3},{2,0},{3,1},{4,6},{5,7},{6,4},{7,5},{8,10},{9,11},{10,... | collective-permute-start | bytes 1572872 | tf_op jit(solution)/shard_map/ppermute | solution.py:23
  44.4 26.2 %collective-permute-start.14 = (bf16[8,32,1024]{2,1,0:T(8,128)(2,1)}, bf16[8,32,1024]{2,1,0:T(8,128)(2,1)}, u32[]{:S(2)}, u32[]{:S(2)}) collective-permute-start(bf16[8,32,1024]{2,1,0:T(8,128)(2,1)} %collective-permute-done.2.refs_11_.refs_6_), channel_id=1, source_target_pairs={{0,2},{1,3},{2,0},{3,1},{4,6},{5,7},{6,4},{7,5},{8,10},{9,11},{10,... | collective-permute-start | bytes 1572872 | tf_op jit(solution)/shard_map/ppermute | solution.py:23
  60.3 24.3 %collective-permute-start.19 = (bf16[8,8,64,128]{3,2,1,0:T(8,128)(2,1)}, bf16[8,8,64,128]{3,2,1,0:T(8,128)(2,1)}, u32[]{:S(2)}, u32[]{:S(2)}) collective-permute-start(bf16[8,8,64,128]{3,2,1,0:T(8,128)(2,1)} %all-to-all-done.2.refs_0_), channel_id=1, source_target_pairs={{0,96},{32,0},{64,32},{96,64},{1,97},{33,1},{65,33},{97,65},{2,98}... | collective-permute-start | bytes 3145736 | tf_op jit(solution)/shard_map/ppermute | solution.py:19
  62.6 17.6 %collective-permute-start.16 = (bf16[8,32,1024]{2,1,0:T(8,128)(2,1)S(1)}, bf16[8,32,1024]{2,1,0:T(8,128)(2,1)S(1)}, u32[]{:S(2)}, u32[]{:S(2)}) collective-permute-start(bf16[8,32,1024]{2,1,0:T(8,128)(2,1)S(1)} %collective-permute-done.10.refs_1_.refs_14_), channel_id=1, source_target_pairs={{0,2},{1,3},{2,0},{3,1},{4,6},{5,7},{6,4},{7,5},{8,10},{9,11},{10,... | collective-permute-start | bytes 1572872 | tf_op jit(solution)/shard_map/ppermute | solution.py:23
  62.6 31.4 %collective-permute-start.8 = (bf16[8,8,64,128]{3,2,1,0:T(8,128)(2,1)}, bf16[8,8,64,128]{3,2,1,0:T(8,128)(2,1)S(1)}, u32[]{:S(2)}, u32[]{:S(2)}) collective-permute-start(bf16[8,8,64,128]{3,2,1,0:T(8,128)(2,1)} %collective-permute-done.5.refs_1_), channel_id=1, source_target_pairs={{0,32},{32,64},{64,96},{96,0},{1,33},{33,65},{65,97},{97,1},{2,34}... | collective-permute-start | bytes 3145736 | tf_op jit(solution)/shard_map/ppermute | solution.py:19
  62.7 17.5 %collective-permute-start.13 = (bf16[8,32,1024]{2,1,0:T(8,128)(2,1)S(1)}, bf16[8,32,1024]{2,1,0:T(8,128)(2,1)S(1)}, u32[]{:S(2)}, u32[]{:S(2)}) collective-permute-start(bf16[8,32,1024]{2,1,0:T(8,128)(2,1)S(1)} %collective-permute-done.7.refs_9_.refs_12_), channel_id=1, source_target_pairs={{0,1},{1,0},{2,3},{3,2},{4,5},{5,4},{6,7},{7,6},{8,9},{9,8},{10,11... | collective-permute-start | bytes 1572872 | tf_op jit(solution)/shard_map/ppermute | solution.py:23
  70.6 11.0 %collective-permute-start.12 = (bf16[8,32,1024]{2,1,0:T(8,128)(2,1)}, bf16[8,32,1024]{2,1,0:T(8,128)(2,1)}, u32[]{:S(2)}, u32[]{:S(2)}) collective-permute-start(bf16[8,32,1024]{2,1,0:T(8,128)(2,1)} %collective-permute-done.4.refs_5_.refs_4_), channel_id=1, source_target_pairs={{0,1},{1,0},{2,3},{3,2},{4,5},{5,4},{6,7},{7,6},{8,9},{9,8},{10,11... | collective-permute-start | bytes 1572872 | tf_op jit(solution)/shard_map/ppermute | solution.py:23
  80.2 7.9 %collective-permute-start.15 = (bf16[8,32,1024]{2,1,0:T(8,128)(2,1)}, bf16[8,32,1024]{2,1,0:T(8,128)(2,1)}, u32[]{:S(2)}, u32[]{:S(2)}) collective-permute-start(bf16[8,32,1024]{2,1,0:T(8,128)(2,1)} %collective-permute-done.14.refs_13_.refs_8_), channel_id=1, source_target_pairs={{0,1},{1,0},{2,3},{3,2},{4,5},{5,4},{6,7},{7,6},{8,9},{9,8},{10,11... | collective-permute-start | bytes 1572872 | tf_op jit(solution)/shard_map/ppermute | solution.py:23
  81.1 12.9 %collective-permute-start.17 = (bf16[8,32,1024]{2,1,0:T(8,128)(2,1)S(1)}, bf16[8,32,1024]{2,1,0:T(8,128)(2,1)S(1)}, u32[]{:S(2)}, u32[]{:S(2)}) collective-permute-start(bf16[8,32,1024]{2,1,0:T(8,128)(2,1)S(1)} %collective-permute-done.16.refs_3_.refs_16_), channel_id=1, source_target_pairs={{0,1},{1,0},{2,3},{3,2},{4,5},{5,4},{6,7},{7,6},{8,9},{9,8},{10,11... | collective-permute-start | bytes 1572872 | tf_op jit(solution)/shard_map/ppermute | solution.py:23
  81.6 28.9 %collective-permute-start.18 = (bf16[8,8,64,128]{3,2,1,0:T(8,128)(2,1)}, bf16[8,8,64,128]{3,2,1,0:T(8,128)(2,1)}, u32[]{:S(2)}, u32[]{:S(2)}) collective-permute-start(bf16[8,8,64,128]{3,2,1,0:T(8,128)(2,1)} %all-to-all-done.2.refs_0_), channel_id=1, source_target_pairs={{0,32},{32,64},{64,96},{96,0},{1,33},{33,65},{65,97},{97,1},{2,34}... | collective-permute-start | bytes 3145736 | tf_op jit(solution)/shard_map/ppermute | solution.py:19
  84.6 25.9 %collective-permute-start.20 = (bf16[8,8,64,128]{3,2,1,0:T(8,128)(2,1)}, bf16[8,8,64,128]{3,2,1,0:T(8,128)(2,1)}, u32[]{:S(2)}, u32[]{:S(2)}) collective-permute-start(bf16[8,8,64,128]{3,2,1,0:T(8,128)(2,1)} %collective-permute-done.19.refs_1_), channel_id=1, source_target_pairs={{0,96},{32,0},{64,32},{96,64},{1,97},{33,1},{65,33},{97,65},{2,98}... | collective-permute-start | bytes 3145736 | tf_op jit(solution)/shard_map/ppermute | solution.py:19
  96.6 20.1 %all-to-all-start.1 = ((bf16[8,8,64,128]{3,2,1,0:T(8,128)(2,1)}), bf16[8,8,64,128]{3,2,1,0:T(8,128)(2,1)S(1)}, u32[]{:S(2)}, u32[]{:S(2)}) async-start(bf16[8,8,64,128]{3,2,1,0:T(8,128)(2,1)} %product.5), calls=%async_computation.1 | async-start | bytes 2097152 | tf_op jit(solution)/shard_map/all_to_all | solution.py:27
  116.7 19.5 %all-to-all-start.3 = ((bf16[8,8,64,128]{3,2,1,0:T(8,128)(2,1)}), bf16[8,8,64,128]{3,2,1,0:T(8,128)(2,1)S(1)}, u32[]{:S(2)}, u32[]{:S(2)}) async-start(bf16[8,8,64,128]{3,2,1,0:T(8,128)(2,1)} %product.7), calls=%async_computation.3 | async-start | bytes 2097152 | tf_op jit(solution)/shard_map/all_to_all | solution.py:27
  (12 other events, 249.3 us)

commit v5 on v4

--- a/solution.py
+++ b/solution.py
@@ -69,10 +69,18 @@
 
 
 def by_j_body(ranks, w_ref, *refs):
-    out_refs, moved = refs[:-1], refs[-1]
-    rows, js, cols = w_ref.shape[1:]
+    out_refs, (held, moved, sems) = refs[:-3], refs[-3:]
+    nk, rows, js, cols = w_ref.shape
     share = js // ranks
-    moved[...] = jnp.swapaxes(w_ref[0].astype(jnp.float32), 0, 1).astype(w_ref.dtype)
+    step = pl.program_id(0)
+
+    @pl.when(step == 0)
+    def _():
+        for k in range(nk):
+            pltpu.make_async_copy(w_ref.at[k], held.at[k], sems.at[k]).start()
+
+    pltpu.make_async_copy(w_ref.at[step], held.at[step], sems.at[step]).wait()
+    moved[...] = jnp.swapaxes(held[step].astype(jnp.float32), 0, 1).astype(w_ref.dtype)
     for distance, ref in enumerate(out_refs):
         first = lax.rem(lax.axis_index("rep") + distance, ranks) * share
         for j in range(share):
@@ -86,13 +94,17 @@
         functools.partial(by_j_body, ranks),
         out_shape=[jax.ShapeDtypeStruct((nk, rows, wide), integrals.dtype)] * ranks,
         grid=(nk,),
-        in_specs=[pl.BlockSpec((1, rows, js, cols), lambda k: (k, 0, 0, 0))],
+        in_specs=[pl.BlockSpec(memory_space=pl.ANY)],
         out_specs=[pl.BlockSpec((1, rows, wide), lambda k: (k, 0, 0))] * ranks,
-        scratch_shapes=[pltpu.VMEM((js, rows, cols), integrals.dtype)],
+        scratch_shapes=[
+            pltpu.VMEM((nk, rows, js, cols), integrals.dtype),
+            pltpu.VMEM((js, rows, cols), integrals.dtype),
+            pltpu.SemaphoreType.DMA((nk,)),
+        ],
         compiler_params=params(16),
         cost_estimate=cost(0, 0),
         name="integrals_by_j",
-    )(integrals)
+    )(pltpu.with_memory_space_constraint(integrals, pltpu.HBM))
 
 
 def quarter_copies(refs, chosen, slot, quarter, sems):

time: 138 us -> 137 us (level)
  local copies, waits for them, and re-layouts: 3.04 us -> 1.44 us
    unnamed x22 -> x20, local copies, waits for them, and re-layouts: 2.46 us -> 0.86 us
where the time goes in v5:
time: 137 us
  waiting for transfers between devices  61.1 us (45%)
  starting transfers between devices  44.2 us (32%)
  Pallas kernels  28.2 us (21%)
  between operations  1.76 us (1%)
  local copies, waits for them, and re-layouts  1.44 us (1%)
    all_to_all x4, waiting for transfers between devices, exchange_irreps(): lax.all_to_all(array, 'ten', split_axis=0, concat_axis=0, axis_index_grou...  27.9 us
    all_to_all x4, starting transfers between devices, exchange_irreps(): lax.all_to_all(array, 'ten', split_axis=0, concat_axis=0, axis_index_grou...  26.4 us
    pallas_call x4, Pallas kernels, product(): pl.pallas_call(functools.partial(product_body, plan, len(hold), sums is n...  17.9 us
    ppermute x12, waiting for transfers between devices, flip_ten(): lax.ppermute(array, 'ten', [(s, s ^ mask) for s in range(lax.axis_size('t...  17.5 us
    ppermute x9, waiting for transfers between devices, shift_rep(): lax.ppermute(array, 'rep', [(s, (s + distance) % n) for s in range(n)])  15.8 us
    ppermute x9, starting transfers between devices, shift_rep(): lax.ppermute(array, 'rep', [(s, (s + distance) % n) for s in range(n)])  14.5 us
    pallas_call x2, Pallas kernels, order_amps(): pl.pallas_call(functools.partial(order_body, offset), out_shape=pltpu.VME...  5.76 us
    ppermute x12, starting transfers between devices, flip_ten(): lax.ppermute(array, 'ten', [(s, s ^ mask) for s in range(lax.axis_size('t...  3.34 us
  transfers between devices with their start and end apart: 25, of which 9 were waited for; matrix products, arithmetic and copies ran while one was open for 0% of the time, Pallas kernels for 18%

profile of v5, /device:TPU:0, one launch (start us, length us, event | category | flops | bytes accessed | tf_op | source)
XLA Modules:
  0.0 136.8 jit_solution(17571668595056361213)
XLA Ops:
  0.0 2.5 %integrals_by_j.1 = (bf16[8,32,1024]{2,1,0:T(8,128)(2,1)S(1)}, bf16[8,32,1024]{2,1,0:T(8,128)(2,1)S(1)}, bf16[8,32,1024]{2,1,0:T(8,128)(2,1)S(1)}, bf16[8,32,1024]{2,1,0:T(8,128)(2,1)S(1)}) custom-call(bf16[8,32,32,128]{3,2,1,0:T(8,128)(2,1)} %w_ref.1), custom_call_target="tpu_custom_call" | custom-call | tf_op jit(solution)/shard_map/integrals_by_j/pallas_call | solution.py:93
  4.2 1.7 %collective-permute-start.2 = (bf16[8,32,1024]{2,1,0:T(8,128)(2,1)S(1)}, bf16[8,32,1024]{2,1,0:T(8,128)(2,1)}, u32[]{:S(2)}, u32[]{:S(2)}) collective-permute-start(bf16[8,32,1024]{2,1,0:T(8,128)(2,1)S(1)} %get-tuple-element.47), channel_id=1, source_target_pairs={{0,96},{32,0},{64,32},{96,64},{1,97},{33,1},{65,33},{97,65},{2,98}... | collective-permute-start | bytes 1572872 | tf_op jit(solution)/shard_map/ppermute | solution.py:19
  5.9 2.9 %order_amps.2 = bf16[8,8,64,128]{3,2,1,0:T(8,128)(2,1)} custom-call(s32[2]{0:T(128)S(1)} %copy-done.5, bf16[8,8,128,128]{3,2,1,0:T(8,128)(2,1)} %bitcast.3), custom_call_target="tpu_custom_call" | custom-call | tf_op jit(solution)/shard_map/order_amps/pallas_call | solution.py:59
  8.8 8.0 %all-to-all-start = ((bf16[8,8,64,128]{3,2,1,0:T(8,128)(2,1)}), bf16[8,8,64,128]{3,2,1,0:T(8,128)(2,1)}, u32[]{:S(2)}, u32[]{:S(2)}) async-start(bf16[8,8,64,128]{3,2,1,0:T(8,128)(2,1)} %order_amps.2), calls=%async_computation | async-start | bytes 2097152 | tf_op jit(solution)/shard_map/all_to_all | solution.py:27
  16.8 1.9 %collective-permute-start.10 = (bf16[8,32,1024]{2,1,0:T(8,128)(2,1)S(1)}, bf16[8,32,1024]{2,1,0:T(8,128)(2,1)S(1)}, u32[]{:S(2)}, u32[]{:S(2)}) collective-permute-start(bf16[8,32,1024]{2,1,0:T(8,128)(2,1)S(1)} %get-tuple-element.56), channel_id=1, source_target_pairs={{0,64},{32,96},{64,0},{96,32},{1,65},{33,97},{65,1},{97,33},{2,66}... | collective-permute-start | bytes 1572872 | tf_op jit(solution)/shard_map/ppermute | solution.py:19
  18.7 2.9 %order_amps.3 = bf16[8,8,64,128]{3,2,1,0:T(8,128)(2,1)} custom-call(s32[2]{0:T(128)S(1)} %copy-done.5, bf16[8,8,128,128]{3,2,1,0:T(8,128)(2,1)} %bitcast.4), custom_call_target="tpu_custom_call" | custom-call | tf_op jit(solution)/shard_map/order_amps/pallas_call | solution.py:59
  22.2 9.0 %collective-permute-done.10.refs_1_.refs_14_ = bf16[8,32,1024]{2,1,0:T(8,128)(2,1)S(1)} collective-permute-done((bf16[8,32,1024]{2,1,0:T(8,128)(2,1)S(1)}, bf16[8,32,1024]{2,1,0:T(8,128)(2,1)S(1)}, u32[]{:S(2)}, u32[]{:S(2)}) %collective-permute-start.10) | collective-permute-done | bytes 524320 | tf_op jit(solution)/shard_map/ppermute | solution.py:19
  32.4 3.0 %collective-permute-start.6 = (bf16[8,8,64,128]{3,2,1,0:T(8,128)(2,1)}, bf16[8,8,64,128]{3,2,1,0:T(8,128)(2,1)}, u32[]{:S(2)}, u32[]{:S(2)}) collective-permute-start(bf16[8,8,64,128]{3,2,1,0:T(8,128)(2,1)} %all-to-all-done.refs_0_), channel_id=1, source_target_pairs={{0,96},{32,0},{64,32},{96,64},{1,97},{33,1},{65,33},{97,65},{2,98}... | collective-permute-start | bytes 3145736 | tf_op jit(solution)/shard_map/ppermute | solution.py:19
  35.4 8.3 %all-to-all-start.2 = ((bf16[8,8,64,128]{3,2,1,0:T(8,128)(2,1)}), bf16[8,8,64,128]{3,2,1,0:T(8,128)(2,1)}, u32[]{:S(2)}, u32[]{:S(2)}) async-start(bf16[8,8,64,128]{3,2,1,0:T(8,128)(2,1)} %order_amps.3), calls=%async_computation.2 | async-start | bytes 2097152 | tf_op jit(solution)/shard_map/all_to_all | solution.py:27
  43.7 2.0 %collective-permute-start.14 = (bf16[8,32,1024]{2,1,0:T(8,128)(2,1)}, bf16[8,32,1024]{2,1,0:T(8,128)(2,1)}, u32[]{:S(2)}, u32[]{:S(2)}) collective-permute-start(bf16[8,32,1024]{2,1,0:T(8,128)(2,1)} %collective-permute-done.2.refs_11_.refs_6_), channel_id=1, source_target_pairs={{0,2},{1,3},{2,0},{3,1},{4,6},{5,7},{6,4},{7,5},{8,10},{9,11},{10,... | collective-permute-start | bytes 1572872 | tf_op jit(solution)/shard_map/ppermute | solution.py:23
  45.7 13.9 %all-to-all-done.2.refs_0_ = bf16[8,8,64,128]{3,2,1,0:T(8,128)(2,1)} async-done(((bf16[8,8,64,128]{3,2,1,0:T(8,128)(2,1)}), bf16[8,8,64,128]{3,2,1,0:T(8,128)(2,1)}, u32[]{:S(2)}, u32[]{:S(2)}) %all-to-all-start.2) | async-done | bytes 1048608 | tf_op jit(solution)/shard_map/all_to_all | solution.py:27
  59.6 2.3 %collective-permute-start.19 = (bf16[8,8,64,128]{3,2,1,0:T(8,128)(2,1)}, bf16[8,8,64,128]{3,2,1,0:T(8,128)(2,1)}, u32[]{:S(2)}, u32[]{:S(2)}) collective-permute-start(bf16[8,8,64,128]{3,2,1,0:T(8,128)(2,1)} %all-to-all-done.2.refs_0_), channel_id=1, source_target_pairs={{0,96},{32,0},{64,32},{96,64},{1,97},{33,1},{65,33},{97,65},{2,98}... | collective-permute-start | bytes 3145736 | tf_op jit(solution)/shard_map/ppermute | solution.py:19
  62.1 7.7 %collective-permute-done.14.refs_13_.refs_8_ = bf16[8,32,1024]{2,1,0:T(8,128)(2,1)} collective-permute-done((bf16[8,32,1024]{2,1,0:T(8,128)(2,1)}, bf16[8,32,1024]{2,1,0:T(8,128)(2,1)}, u32[]{:S(2)}, u32[]{:S(2)}) %collective-permute-start.14) | collective-permute-done | bytes 524320 | tf_op jit(solution)/shard_map/ppermute | solution.py:23
  69.9 9.7 %collective-permute-done.16.refs_3_.refs_16_ = bf16[8,32,1024]{2,1,0:T(8,128)(2,1)S(1)} collective-permute-done((bf16[8,32,1024]{2,1,0:T(8,128)(2,1)S(1)}, bf16[8,32,1024]{2,1,0:T(8,128)(2,1)S(1)}, u32[]{:S(2)}, u32[]{:S(2)}) %collective-permute-start.16) | collective-permute-done | bytes 524320 | tf_op jit(solution)/shard_map/ppermute | solution.py:23
  80.9 3.0 %collective-permute-done.19.refs_1_ = bf16[8,8,64,128]{3,2,1,0:T(8,128)(2,1)} collective-permute-done((bf16[8,8,64,128]{3,2,1,0:T(8,128)(2,1)}, bf16[8,8,64,128]{3,2,1,0:T(8,128)(2,1)}, u32[]{:S(2)}, u32[]{:S(2)}) %collective-permute-start.19) | collective-permute-done | bytes 1048608 | tf_op jit(solution)/shard_map/ppermute | solution.py:19
  83.9 3.6 %collective-permute-start.20 = (bf16[8,8,64,128]{3,2,1,0:T(8,128)(2,1)}, bf16[8,8,64,128]{3,2,1,0:T(8,128)(2,1)}, u32[]{:S(2)}, u32[]{:S(2)}) collective-permute-start(bf16[8,8,64,128]{3,2,1,0:T(8,128)(2,1)} %collective-permute-done.19.refs_1_), channel_id=1, source_target_pairs={{0,96},{32,0},{64,32},{96,64},{1,97},{33,1},{65,33},{97,65},{2,98}... | collective-permute-start | bytes 3145736 | tf_op jit(solution)/shard_map/ppermute | solution.py:19
  87.5 5.8 %product.4.refs_5_ = f32[512,1024]{1,0:T(8,128)S(1)} custom-call(s32[1]{0:T(128)} %bitcast.quarter_ref, bf16[8,8,64,128]{3,2,1,0:T(8,128)(2,1)} %all-to-all-done.refs_0_, bf16[8,8,64,128]{3,2,1,0:T(8,128)(2,1)} %collective-permute-done.5.refs_1_, bf16[8,8,64,128]{3,2,1,0:T(8,128)(2,1)} %collective-permute-done.6.refs_2_, bf16[8,32,1024]{2,1,0:T(8,128)(2,1)} %copy-done, ...), custom_call_target="tpu_custom_call" | custom-call | tf_op jit(solution)/shard_map/product/pallas_call | solution.py:214
  93.4 2.5 %product.5 = bf16[8,8,64,128]{3,2,1,0:T(8,128)(2,1)} custom-call(s32[1]{0:T(128)} %bitcast.quarter_ref, bf16[8,8,64,128]{3,2,1,0:T(8,128)(2,1)S(1)} %collective-permute-done.8.refs_0_, bf16[8,32,1024]{2,1,0:T(8,128)(2,1)S(1)} %collective-permute-done.10.refs_1_.refs_14_, bf16[8,32,1024]{2,1,0:T(8,128)(2,1)S(1)} %collective-permute-done.11.refs_2_.refs_15_, ...), custom_call_target="tpu_custom_call" | custom-call | tf_op jit(solution)/shard_map/product/pallas_call | solution.py:214
  95.9 5.3 %all-to-all-start.1 = ((bf16[8,8,64,128]{3,2,1,0:T(8,128)(2,1)}), bf16[8,8,64,128]{3,2,1,0:T(8,128)(2,1)S(1)}, u32[]{:S(2)}, u32[]{:S(2)}) async-start(bf16[8,8,64,128]{3,2,1,0:T(8,128)(2,1)} %product.5), calls=%async_computation.1 | async-start | bytes 2097152 | tf_op jit(solution)/shard_map/all_to_all | solution.py:27
  101.3 4.7 %product.6 = (f32[512,1024]{1,0:T(8,128)S(1)}, bf16[16,128,1024]{2,1,0:T(8,128)(2,1)S(1)}) custom-call(s32[1]{0:T(128)} %bitcast.quarter_ref, bf16[8,8,64,128]{3,2,1,0:T(8,128)(2,1)} %all-to-all-done.2.refs_0_, bf16[8,8,64,128]{3,2,1,0:T(8,128)(2,1)} %collective-permute-done.19.refs_1_, bf16[8,32,1024]{2,1,0:T(8,128)(2,1)} %copy-done, ...), custom_call_target="tpu_custom_call" | custom-call | tf_op jit(solution)/shard_map/product/pallas_call | solution.py:214
  106.0 3.8 %collective-permute-done.18.refs_0_ = bf16[8,8,64,128]{3,2,1,0:T(8,128)(2,1)} collective-permute-done((bf16[8,8,64,128]{3,2,1,0:T(8,128)(2,1)}, bf16[8,8,64,128]{3,2,1,0:T(8,128)(2,1)}, u32[]{:S(2)}, u32[]{:S(2)}) %collective-permute-start.18) | collective-permute-done | bytes 1048608 | tf_op jit(solution)/shard_map/ppermute | solution.py:19
  109.8 4.8 %product.7 = bf16[8,8,64,128]{3,2,1,0:T(8,128)(2,1)} custom-call(s32[1]{0:T(128)} %bitcast.quarter_ref, bf16[8,8,64,128]{3,2,1,0:T(8,128)(2,1)} %collective-permute-done.18.refs_0_, bf16[8,8,64,128]{3,2,1,0:T(8,128)(2,1)} %collective-permute-done.20.refs_1_, bf16[16,128,1024]{2,1,0:T(8,128)(2,1)S(1)} %get-tuple-element.71.refs_2_, ...), custom_call_target="tpu_custom_call" | custom-call | tf_op jit(solution)/shard_map/product/pallas_call | solution.py:214
  116.1 4.8 %all-to-all-start.3 = ((bf16[8,8,64,128]{3,2,1,0:T(8,128)(2,1)}), bf16[8,8,64,128]{3,2,1,0:T(8,128)(2,1)S(1)}, u32[]{:S(2)}, u32[]{:S(2)}) async-start(bf16[8,8,64,128]{3,2,1,0:T(8,128)(2,1)} %product.7), calls=%async_computation.3 | async-start | bytes 2097152 | tf_op jit(solution)/shard_map/all_to_all | solution.py:27
  123.8 11.8 %all-to-all-done.3.part_ref = bf16[8,8,64,128]{3,2,1,0:T(8,128)(2,1)S(1)} async-done(((bf16[8,8,64,128]{3,2,1,0:T(8,128)(2,1)}), bf16[8,8,64,128]{3,2,1,0:T(8,128)(2,1)S(1)}, u32[]{:S(2)}, u32[]{:S(2)}) %all-to-all-start.3) | async-done | bytes 1048608 | tf_op jit(solution)/shard_map/all_to_all | solution.py:27
  (56 shorter events, 9.1 us)
Async XLA Ops:
  2.6 16.1 %collective-permute-start = (bf16[8,32,1024]{2,1,0:T(8,128)(2,1)S(1)}, bf16[8,32,1024]{2,1,0:T(8,128)(2,1)S(1)}, u32[]{:S(2)}, u32[]{:S(2)}) collective-permute-start(bf16[8,32,1024]{2,1,0:T(8,128)(2,1)S(1)} %get-tuple-element.46), channel_id=1, source_target_pairs={{0,32},{32,64},{64,96},{96,0},{1,33},{33,65},{65,97},{97,1},{2,34}... | collective-permute-start | bytes 1572872 | tf_op jit(solution)/shard_map/ppermute | solution.py:19
  4.2 17.4 %collective-permute-start.2 = (bf16[8,32,1024]{2,1,0:T(8,128)(2,1)S(1)}, bf16[8,32,1024]{2,1,0:T(8,128)(2,1)}, u32[]{:S(2)}, u32[]{:S(2)}) collective-permute-start(bf16[8,32,1024]{2,1,0:T(8,128)(2,1)S(1)} %get-tuple-element.47), channel_id=1, source_target_pairs={{0,96},{32,0},{64,32},{96,64},{1,97},{33,1},{65,33},{97,65},{2,98}... | collective-permute-start | bytes 1572872 | tf_op jit(solution)/shard_map/ppermute | solution.py:19
  8.8 23.2 %all-to-all-start = ((bf16[8,8,64,128]{3,2,1,0:T(8,128)(2,1)}), bf16[8,8,64,128]{3,2,1,0:T(8,128)(2,1)}, u32[]{:S(2)}, u32[]{:S(2)}) async-start(bf16[8,8,64,128]{3,2,1,0:T(8,128)(2,1)} %order_amps.2), calls=%async_computation | async-start | bytes 2097152 | tf_op jit(solution)/shard_map/all_to_all | solution.py:27
  16.8 14.4 %collective-permute-start.4 = (bf16[8,32,1024]{2,1,0:T(8,128)(2,1)S(1)}, bf16[8,32,1024]{2,1,0:T(8,128)(2,1)}, u32[]{:S(2)}, u32[]{:S(2)}) collective-permute-start(bf16[8,32,1024]{2,1,0:T(8,128)(2,1)S(1)} %get-tuple-element.55.refs_3_.refs_2_), channel_id=1, source_target_pairs={{0,2},{1,3},{2,0},{3,1},{4,6},{5,7},{6,4},{7,5},{8,10},{9,11},{10,... | collective-permute-start | bytes 1572872 | tf_op jit(solution)/shard_map/ppermute | solution.py:23
  16.8 14.4 %collective-permute-start.10 = (bf16[8,32,1024]{2,1,0:T(8,128)(2,1)S(1)}, bf16[8,32,1024]{2,1,0:T(8,128)(2,1)S(1)}, u32[]{:S(2)}, u32[]{:S(2)}) collective-permute-start(bf16[8,32,1024]{2,1,0:T(8,128)(2,1)S(1)} %get-tuple-element.56), channel_id=1, source_target_pairs={{0,64},{32,96},{64,0},{96,32},{1,65},{33,97},{65,1},{97,33},{2,66}... | collective-permute-start | bytes 1572872 | tf_op jit(solution)/shard_map/ppermute | solution.py:19
  21.6 10.3 %collective-permute-start.1 = (bf16[8,32,1024]{2,1,0:T(8,128)(2,1)S(1)}, bf16[8,32,1024]{2,1,0:T(8,128)(2,1)S(1)}, u32[]{:S(2)}, u32[]{:S(2)}) collective-permute-start(bf16[8,32,1024]{2,1,0:T(8,128)(2,1)S(1)} %collective-permute-done.refs_7_.refs_10_), channel_id=1, source_target_pairs={{0,1},{1,0},{2,3},{3,2},{4,5},{5,4},{6,7},{7,6},{8,9},{9,8},{10,11... | collective-permute-start | bytes 1572872 | tf_op jit(solution)/shard_map/ppermute | solution.py:23
  21.7 10.2 %collective-permute-start.3 = (bf16[8,32,1024]{2,1,0:T(8,128)(2,1)}, bf16[8,32,1024]{2,1,0:T(8,128)(2,1)}, u32[]{:S(2)}, u32[]{:S(2)}) collective-permute-start(bf16[8,32,1024]{2,1,0:T(8,128)(2,1)} %collective-permute-done.2.refs_11_.refs_6_), channel_id=1, source_target_pairs={{0,1},{1,0},{2,3},{3,2},{4,5},{5,4},{6,7},{7,6},{8,9},{9,8},{10,11... | collective-permute-start | bytes 1572872 | tf_op jit(solution)/shard_map/ppermute | solution.py:23
  31.2 4.1 %collective-permute-start.11 = (bf16[8,32,1024]{2,1,0:T(8,128)(2,1)S(1)}, bf16[8,32,1024]{2,1,0:T(8,128)(2,1)S(1)}, u32[]{:S(2)}, u32[]{:S(2)}) collective-permute-start(bf16[8,32,1024]{2,1,0:T(8,128)(2,1)S(1)} %collective-permute-done.10.refs_1_.refs_14_), channel_id=1, source_target_pairs={{0,1},{1,0},{2,3},{3,2},{4,5},{5,4},{6,7},{7,6},{8,9},{9,8},{10,11... | collective-permute-start | bytes 1572872 | tf_op jit(solution)/shard_map/ppermute | solution.py:23
  32.0 29.9 %collective-permute-start.5 = (bf16[8,8,64,128]{3,2,1,0:T(8,128)(2,1)}, bf16[8,8,64,128]{3,2,1,0:T(8,128)(2,1)}, u32[]{:S(2)}, u32[]{:S(2)}) collective-permute-start(bf16[8,8,64,128]{3,2,1,0:T(8,128)(2,1)} %all-to-all-done.refs_0_), channel_id=1, source_target_pairs={{0,32},{32,64},{64,96},{96,0},{1,33},{33,65},{65,97},{97,1},{2,34}... | collective-permute-start | bytes 3145736 | tf_op jit(solution)/shard_map/ppermute | solution.py:19
  32.4 29.6 %collective-permute-start.6 = (bf16[8,8,64,128]{3,2,1,0:T(8,128)(2,1)}, bf16[8,8,64,128]{3,2,1,0:T(8,128)(2,1)}, u32[]{:S(2)}, u32[]{:S(2)}) collective-permute-start(bf16[8,8,64,128]{3,2,1,0:T(8,128)(2,1)} %all-to-all-done.refs_0_), channel_id=1, source_target_pairs={{0,96},{32,0},{64,32},{96,64},{1,97},{33,1},{65,33},{97,65},{2,98}... | collective-permute-start | bytes 3145736 | tf_op jit(solution)/shard_map/ppermute | solution.py:19
  35.4 24.3 %all-to-all-start.2 = ((bf16[8,8,64,128]{3,2,1,0:T(8,128)(2,1)}), bf16[8,8,64,128]{3,2,1,0:T(8,128)(2,1)}, u32[]{:S(2)}, u32[]{:S(2)}) async-start(bf16[8,8,64,128]{3,2,1,0:T(8,128)(2,1)} %order_amps.3), calls=%async_computation.2 | async-start | bytes 2097152 | tf_op jit(solution)/shard_map/all_to_all | solution.py:27
  43.6 18.3 %collective-permute-start.7 = (bf16[8,32,1024]{2,1,0:T(8,128)(2,1)S(1)}, bf16[8,32,1024]{2,1,0:T(8,128)(2,1)S(1)}, u32[]{:S(2)}, u32[]{:S(2)}) collective-permute-start(bf16[8,32,1024]{2,1,0:T(8,128)(2,1)S(1)} %collective-permute-done.refs_7_.refs_10_), channel_id=1, source_target_pairs={{0,2},{1,3},{2,0},{3,1},{4,6},{5,7},{6,4},{7,5},{8,10},{9,11},{10,... | collective-permute-start | bytes 1572872 | tf_op jit(solution)/shard_map/ppermute | solution.py:23
  43.7 26.2 %collective-permute-start.14 = (bf16[8,32,1024]{2,1,0:T(8,128)(2,1)}, bf16[8,32,1024]{2,1,0:T(8,128)(2,1)}, u32[]{:S(2)}, u32[]{:S(2)}) collective-permute-start(bf16[8,32,1024]{2,1,0:T(8,128)(2,1)} %collective-permute-done.2.refs_11_.refs_6_), channel_id=1, source_target_pairs={{0,2},{1,3},{2,0},{3,1},{4,6},{5,7},{6,4},{7,5},{8,10},{9,11},{10,... | collective-permute-start | bytes 1572872 | tf_op jit(solution)/shard_map/ppermute | solution.py:23
  59.6 24.3 %collective-permute-start.19 = (bf16[8,8,64,128]{3,2,1,0:T(8,128)(2,1)}, bf16[8,8,64,128]{3,2,1,0:T(8,128)(2,1)}, u32[]{:S(2)}, u32[]{:S(2)}) collective-permute-start(bf16[8,8,64,128]{3,2,1,0:T(8,128)(2,1)} %all-to-all-done.2.refs_0_), channel_id=1, source_target_pairs={{0,96},{32,0},{64,32},{96,64},{1,97},{33,1},{65,33},{97,65},{2,98}... | collective-permute-start | bytes 3145736 | tf_op jit(solution)/shard_map/ppermute | solution.py:19
  61.9 17.6 %collective-permute-start.16 = (bf16[8,32,1024]{2,1,0:T(8,128)(2,1)S(1)}, bf16[8,32,1024]{2,1,0:T(8,128)(2,1)S(1)}, u32[]{:S(2)}, u32[]{:S(2)}) collective-permute-start(bf16[8,32,1024]{2,1,0:T(8,128)(2,1)S(1)} %collective-permute-done.10.refs_1_.refs_14_), channel_id=1, source_target_pairs={{0,2},{1,3},{2,0},{3,1},{4,6},{5,7},{6,4},{7,5},{8,10},{9,11},{10,... | collective-permute-start | bytes 1572872 | tf_op jit(solution)/shard_map/ppermute | solution.py:23
  62.0 31.4 %collective-permute-start.8 = (bf16[8,8,64,128]{3,2,1,0:T(8,128)(2,1)}, bf16[8,8,64,128]{3,2,1,0:T(8,128)(2,1)S(1)}, u32[]{:S(2)}, u32[]{:S(2)}) collective-permute-start(bf16[8,8,64,128]{3,2,1,0:T(8,128)(2,1)} %collective-permute-done.5.refs_1_), channel_id=1, source_target_pairs={{0,32},{32,64},{64,96},{96,0},{1,33},{33,65},{65,97},{97,1},{2,34}... | collective-permute-start | bytes 3145736 | tf_op jit(solution)/shard_map/ppermute | solution.py:19
  62.1 17.5 %collective-permute-start.13 = (bf16[8,32,1024]{2,1,0:T(8,128)(2,1)S(1)}, bf16[8,32,1024]{2,1,0:T(8,128)(2,1)S(1)}, u32[]{:S(2)}, u32[]{:S(2)}) collective-permute-start(bf16[8,32,1024]{2,1,0:T(8,128)(2,1)S(1)} %collective-permute-done.7.refs_9_.refs_12_), channel_id=1, source_target_pairs={{0,1},{1,0},{2,3},{3,2},{4,5},{5,4},{6,7},{7,6},{8,9},{9,8},{10,11... | collective-permute-start | bytes 1572872 | tf_op jit(solution)/shard_map/ppermute | solution.py:23
  69.9 11.0 %collective-permute-start.12 = (bf16[8,32,1024]{2,1,0:T(8,128)(2,1)}, bf16[8,32,1024]{2,1,0:T(8,128)(2,1)}, u32[]{:S(2)}, u32[]{:S(2)}) collective-permute-start(bf16[8,32,1024]{2,1,0:T(8,128)(2,1)} %collective-permute-done.4.refs_5_.refs_4_), channel_id=1, source_target_pairs={{0,1},{1,0},{2,3},{3,2},{4,5},{5,4},{6,7},{7,6},{8,9},{9,8},{10,11... | collective-permute-start | bytes 1572872 | tf_op jit(solution)/shard_map/ppermute | solution.py:23
  79.6 7.9 %collective-permute-start.15 = (bf16[8,32,1024]{2,1,0:T(8,128)(2,1)}, bf16[8,32,1024]{2,1,0:T(8,128)(2,1)}, u32[]{:S(2)}, u32[]{:S(2)}) collective-permute-start(bf16[8,32,1024]{2,1,0:T(8,128)(2,1)} %collective-permute-done.14.refs_13_.refs_8_), channel_id=1, source_target_pairs={{0,1},{1,0},{2,3},{3,2},{4,5},{5,4},{6,7},{7,6},{8,9},{9,8},{10,11... | collective-permute-start | bytes 1572872 | tf_op jit(solution)/shard_map/ppermute | solution.py:23
  80.4 12.9 %collective-permute-start.17 = (bf16[8,32,1024]{2,1,0:T(8,128)(2,1)S(1)}, bf16[8,32,1024]{2,1,0:T(8,128)(2,1)S(1)}, u32[]{:S(2)}, u32[]{:S(2)}) collective-permute-start(bf16[8,32,1024]{2,1,0:T(8,128)(2,1)S(1)} %collective-permute-done.16.refs_3_.refs_16_), channel_id=1, source_target_pairs={{0,1},{1,0},{2,3},{3,2},{4,5},{5,4},{6,7},{7,6},{8,9},{9,8},{10,11... | collective-permute-start | bytes 1572872 | tf_op jit(solution)/shard_map/ppermute | solution.py:23
  80.9 28.9 %collective-permute-start.18 = (bf16[8,8,64,128]{3,2,1,0:T(8,128)(2,1)}, bf16[8,8,64,128]{3,2,1,0:T(8,128)(2,1)}, u32[]{:S(2)}, u32[]{:S(2)}) collective-permute-start(bf16[8,8,64,128]{3,2,1,0:T(8,128)(2,1)} %all-to-all-done.2.refs_0_), channel_id=1, source_target_pairs={{0,32},{32,64},{64,96},{96,0},{1,33},{33,65},{65,97},{97,1},{2,34}... | collective-permute-start | bytes 3145736 | tf_op jit(solution)/shard_map/ppermute | solution.py:19
  83.9 25.9 %collective-permute-start.20 = (bf16[8,8,64,128]{3,2,1,0:T(8,128)(2,1)}, bf16[8,8,64,128]{3,2,1,0:T(8,128)(2,1)}, u32[]{:S(2)}, u32[]{:S(2)}) collective-permute-start(bf16[8,8,64,128]{3,2,1,0:T(8,128)(2,1)} %collective-permute-done.19.refs_1_), channel_id=1, source_target_pairs={{0,96},{32,0},{64,32},{96,64},{1,97},{33,1},{65,33},{97,65},{2,98}... | collective-permute-start | bytes 3145736 | tf_op jit(solution)/shard_map/ppermute | solution.py:19
  95.9 20.1 %all-to-all-start.1 = ((bf16[8,8,64,128]{3,2,1,0:T(8,128)(2,1)}), bf16[8,8,64,128]{3,2,1,0:T(8,128)(2,1)S(1)}, u32[]{:S(2)}, u32[]{:S(2)}) async-start(bf16[8,8,64,128]{3,2,1,0:T(8,128)(2,1)} %product.5), calls=%async_computation.1 | async-start | bytes 2097152 | tf_op jit(solution)/shard_map/all_to_all | solution.py:27
  116.1 19.5 %all-to-all-start.3 = ((bf16[8,8,64,128]{3,2,1,0:T(8,128)(2,1)}), bf16[8,8,64,128]{3,2,1,0:T(8,128)(2,1)S(1)}, u32[]{:S(2)}, u32[]{:S(2)}) async-start(bf16[8,8,64,128]{3,2,1,0:T(8,128)(2,1)} %product.7), calls=%async_computation.3 | async-start | bytes 2097152 | tf_op jit(solution)/shard_map/all_to_all | solution.py:27
  (11 other events, 248.6 us)

commit v6 on v5

--- a/solution.py
+++ b/solution.py
@@ -128,6 +128,8 @@
     out_ref, refs = refs[0], refs[1:]
     held_ref, refs = (refs[0], refs[1:]) if held else (None, refs)
     lhs, total, piece_sems, *refs = refs
+    if out_ref.dtype != jnp.float32:
+        *refs, staged, out_sems = refs
     chosen, w_sems, *held_sems = (w_refs[0], None) if is_held else refs
     width = w_refs[0].shape[2]
     ni, nk, step, cols = pieces[0].shape
@@ -160,6 +162,24 @@
             [lhs[slot * ni:(slot + 1) * ni, k].reshape(ni * step, cols) for k in range(nk)], axis=1
         )
         right = chosen[slot * nk:(slot + 1) * nk].reshape(nk * cols, width)
+        if slot == count - 1 and out_ref.dtype != jnp.float32:
+            js = out_ref.shape[1] // 2
+            leaving = []
+            for n in range(2):
+                here = slice(n * js * cols, (n + 1) * js * cols)
+                sums = jnp.dot(left, right[:, here], preferred_element_type=jnp.float32)
+                sums = sums + (sum_refs[0] if slot == 0 else total)[:, here]
+                for j in range(js):
+                    part = sums[:, j * cols:(j + 1) * cols].astype(out_ref.dtype)
+                    staged[:, n * js + j] = part.reshape(ni, step, cols)
+                place = pl.ds(n * js, js)
+                leaving.append(
+                    pltpu.make_async_copy(staged.at[:, place], out_ref.at[:, place], out_sems.at[n])
+                )
+                leaving[-1].start()
+            for copy in leaving:
+                copy.wait()
+            continue
         sums = jnp.dot(left, right, preferred_element_type=jnp.float32)
         if slot == 0:
             if has_sum:
@@ -168,11 +188,8 @@
             sums = sums + total[...]
         if slot < count - 1:
             total[...] = sums
-        elif out_ref.dtype == jnp.float32:
+        else:
             out_ref[...] = sums
-        else:
-            for j in range(width // cols):
-                out_ref[:, j] = sums[:, j * cols:(j + 1) * cols].astype(out_ref.dtype).reshape(ni, step, cols)
     for copy in later:
         copy.wait()
 
@@ -211,11 +228,13 @@
         scratch += [pltpu.VMEM((nk * count, cols, width), pieces[0].dtype), pltpu.SemaphoreType.DMA((4 * count,))]
     if hold:
         scratch.append(pltpu.SemaphoreType.DMA((4 * len(hold),)))
+    if last:
+        scratch += [pltpu.VMEM((ni, js, step, cols), pieces[0].dtype), pltpu.SemaphoreType.DMA((2,))]
     return pl.pallas_call(
         functools.partial(product_body, plan, len(hold), sums is not None, is_held),
         out_shape=out_shape,
         in_specs=in_specs,
-        out_specs=[pl.BlockSpec(memory_space=pltpu.VMEM)] * len(out_shape),
+        out_specs=[pl.BlockSpec(memory_space=pl.ANY if last else pltpu.VMEM)] * len(out_shape),
         scratch_shapes=scratch,
         compiler_params=params(VMEM_PRODUCT),
         cost_estimate=cost(0, 0),

time: 137 us -> 137 us (level)
  no operation moved by 1% of the time
where the time goes in v6:
time: 137 us
  waiting for transfers between devices  61.3 us (45%)
  starting transfers between devices  44.2 us (32%)
  Pallas kernels  27.9 us (20%)
  between operations  1.76 us (1%)
  local copies, waits for them, and re-layouts  1.44 us (1%)
    all_to_all x4, waiting for transfers between devices, exchange_irreps(): lax.all_to_all(array, 'ten', split_axis=0, concat_axis=0, axis_index_grou...  27.9 us
    all_to_all x4, starting transfers between devices, exchange_irreps(): lax.all_to_all(array, 'ten', split_axis=0, concat_axis=0, axis_index_grou...  26.4 us
    pallas_call x4, Pallas kernels, product(): pl.pallas_call(functools.partial(product_body, plan, len(hold), sums is n...  17.5 us
    ppermute x12, waiting for transfers between devices, flip_ten(): lax.ppermute(array, 'ten', [(s, s ^ mask) for s in range(lax.axis_size('t...  17.5 us
    ppermute x9, waiting for transfers between devices, shift_rep(): lax.ppermute(array, 'rep', [(s, (s + distance) % n) for s in range(n)])  16 us
    ppermute x9, starting transfers between devices, shift_rep(): lax.ppermute(array, 'rep', [(s, (s + distance) % n) for s in range(n)])  14.5 us
    pallas_call x2, Pallas kernels, order_amps(): pl.pallas_call(functools.partial(order_body, offset), out_shape=pltpu.VME...  5.76 us
    ppermute x12, starting transfers between devices, flip_ten(): lax.ppermute(array, 'ten', [(s, s ^ mask) for s in range(lax.axis_size('t...  3.34 us
  transfers between devices with their start and end apart: 25, of which 9 were waited for; matrix products, arithmetic and copies ran while one was open for 0% of the time, Pallas kernels for 18%

profile of v6, /device:TPU:0, one launch (start us, length us, event | category | flops | bytes accessed | tf_op | source)
XLA Modules:
  0.0 136.6 jit_solution(16890497623363557784)
XLA Ops:
  0.0 2.5 %integrals_by_j.1 = (bf16[8,32,1024]{2,1,0:T(8,128)(2,1)S(1)}, bf16[8,32,1024]{2,1,0:T(8,128)(2,1)S(1)}, bf16[8,32,1024]{2,1,0:T(8,128)(2,1)S(1)}, bf16[8,32,1024]{2,1,0:T(8,128)(2,1)S(1)}) custom-call(bf16[8,32,32,128]{3,2,1,0:T(8,128)(2,1)} %w_ref.1), custom_call_target="tpu_custom_call" | custom-call | tf_op jit(solution)/shard_map/integrals_by_j/pallas_call | solution.py:93
  4.2 1.7 %collective-permute-start.2 = (bf16[8,32,1024]{2,1,0:T(8,128)(2,1)S(1)}, bf16[8,32,1024]{2,1,0:T(8,128)(2,1)}, u32[]{:S(2)}, u32[]{:S(2)}) collective-permute-start(bf16[8,32,1024]{2,1,0:T(8,128)(2,1)S(1)} %get-tuple-element.47), channel_id=1, source_target_pairs={{0,96},{32,0},{64,32},{96,64},{1,97},{33,1},{65,33},{97,65},{2,98}... | collective-permute-start | bytes 1572872 | tf_op jit(solution)/shard_map/ppermute | solution.py:19
  5.9 2.9 %order_amps.2 = bf16[8,8,64,128]{3,2,1,0:T(8,128)(2,1)} custom-call(s32[2]{0:T(128)S(1)} %copy-done.5, bf16[8,8,128,128]{3,2,1,0:T(8,128)(2,1)} %bitcast.3), custom_call_target="tpu_custom_call" | custom-call | tf_op jit(solution)/shard_map/order_amps/pallas_call | solution.py:59
  8.8 8.0 %all-to-all-start = ((bf16[8,8,64,128]{3,2,1,0:T(8,128)(2,1)}), bf16[8,8,64,128]{3,2,1,0:T(8,128)(2,1)}, u32[]{:S(2)}, u32[]{:S(2)}) async-start(bf16[8,8,64,128]{3,2,1,0:T(8,128)(2,1)} %order_amps.2), calls=%async_computation | async-start | bytes 2097152 | tf_op jit(solution)/shard_map/all_to_all | solution.py:27
  16.8 1.9 %collective-permute-start.10 = (bf16[8,32,1024]{2,1,0:T(8,128)(2,1)S(1)}, bf16[8,32,1024]{2,1,0:T(8,128)(2,1)S(1)}, u32[]{:S(2)}, u32[]{:S(2)}) collective-permute-start(bf16[8,32,1024]{2,1,0:T(8,128)(2,1)S(1)} %get-tuple-element.56), channel_id=1, source_target_pairs={{0,64},{32,96},{64,0},{96,32},{1,65},{33,97},{65,1},{97,33},{2,66}... | collective-permute-start | bytes 1572872 | tf_op jit(solution)/shard_map/ppermute | solution.py:19
  18.7 2.9 %order_amps.3 = bf16[8,8,64,128]{3,2,1,0:T(8,128)(2,1)} custom-call(s32[2]{0:T(128)S(1)} %copy-done.5, bf16[8,8,128,128]{3,2,1,0:T(8,128)(2,1)} %bitcast.4), custom_call_target="tpu_custom_call" | custom-call | tf_op jit(solution)/shard_map/order_amps/pallas_call | solution.py:59
  22.2 9.0 %collective-permute-done.10.refs_1_.refs_14_ = bf16[8,32,1024]{2,1,0:T(8,128)(2,1)S(1)} collective-permute-done((bf16[8,32,1024]{2,1,0:T(8,128)(2,1)S(1)}, bf16[8,32,1024]{2,1,0:T(8,128)(2,1)S(1)}, u32[]{:S(2)}, u32[]{:S(2)}) %collective-permute-start.10) | collective-permute-done | bytes 524320 | tf_op jit(solution)/shard_map/ppermute | solution.py:19
  32.4 3.0 %collective-permute-start.6 = (bf16[8,8,64,128]{3,2,1,0:T(8,128)(2,1)}, bf16[8,8,64,128]{3,2,1,0:T(8,128)(2,1)}, u32[]{:S(2)}, u32[]{:S(2)}) collective-permute-start(bf16[8,8,64,128]{3,2,1,0:T(8,128)(2,1)} %all-to-all-done.refs_0_), channel_id=1, source_target_pairs={{0,96},{32,0},{64,32},{96,64},{1,97},{33,1},{65,33},{97,65},{2,98}... | collective-permute-start | bytes 3145736 | tf_op jit(solution)/shard_map/ppermute | solution.py:19
  35.4 8.3 %all-to-all-start.2 = ((bf16[8,8,64,128]{3,2,1,0:T(8,128)(2,1)}), bf16[8,8,64,128]{3,2,1,0:T(8,128)(2,1)}, u32[]{:S(2)}, u32[]{:S(2)}) async-start(bf16[8,8,64,128]{3,2,1,0:T(8,128)(2,1)} %order_amps.3), calls=%async_computation.2 | async-start | bytes 2097152 | tf_op jit(solution)/shard_map/all_to_all | solution.py:27
  43.7 2.0 %collective-permute-start.14 = (bf16[8,32,1024]{2,1,0:T(8,128)(2,1)}, bf16[8,32,1024]{2,1,0:T(8,128)(2,1)}, u32[]{:S(2)}, u32[]{:S(2)}) collective-permute-start(bf16[8,32,1024]{2,1,0:T(8,128)(2,1)} %collective-permute-done.2.refs_11_.refs_6_), channel_id=1, source_target_pairs={{0,2},{1,3},{2,0},{3,1},{4,6},{5,7},{6,4},{7,5},{8,10},{9,11},{10,... | collective-permute-start | bytes 1572872 | tf_op jit(solution)/shard_map/ppermute | solution.py:23
  45.7 13.9 %all-to-all-done.2.refs_0_ = bf16[8,8,64,128]{3,2,1,0:T(8,128)(2,1)} async-done(((bf16[8,8,64,128]{3,2,1,0:T(8,128)(2,1)}), bf16[8,8,64,128]{3,2,1,0:T(8,128)(2,1)}, u32[]{:S(2)}, u32[]{:S(2)}) %all-to-all-start.2) | async-done | bytes 1048608 | tf_op jit(solution)/shard_map/all_to_all | solution.py:27
  59.6 2.3 %collective-permute-start.19 = (bf16[8,8,64,128]{3,2,1,0:T(8,128)(2,1)}, bf16[8,8,64,128]{3,2,1,0:T(8,128)(2,1)}, u32[]{:S(2)}, u32[]{:S(2)}) collective-permute-start(bf16[8,8,64,128]{3,2,1,0:T(8,128)(2,1)} %all-to-all-done.2.refs_0_), channel_id=1, source_target_pairs={{0,96},{32,0},{64,32},{96,64},{1,97},{33,1},{65,33},{97,65},{2,98}... | collective-permute-start | bytes 3145736 | tf_op jit(solution)/shard_map/ppermute | solution.py:19
  62.1 7.7 %collective-permute-done.14.refs_13_.refs_8_ = bf16[8,32,1024]{2,1,0:T(8,128)(2,1)} collective-permute-done((bf16[8,32,1024]{2,1,0:T(8,128)(2,1)}, bf16[8,32,1024]{2,1,0:T(8,128)(2,1)}, u32[]{:S(2)}, u32[]{:S(2)}) %collective-permute-start.14) | collective-permute-done | bytes 524320 | tf_op jit(solution)/shard_map/ppermute | solution.py:23
  69.9 9.7 %collective-permute-done.16.refs_3_.refs_16_ = bf16[8,32,1024]{2,1,0:T(8,128)(2,1)S(1)} collective-permute-done((bf16[8,32,1024]{2,1,0:T(8,128)(2,1)S(1)}, bf16[8,32,1024]{2,1,0:T(8,128)(2,1)S(1)}, u32[]{:S(2)}, u32[]{:S(2)}) %collective-permute-start.16) | collective-permute-done | bytes 524320 | tf_op jit(solution)/shard_map/ppermute | solution.py:23
  80.9 3.0 %collective-permute-done.19.refs_1_ = bf16[8,8,64,128]{3,2,1,0:T(8,128)(2,1)} collective-permute-done((bf16[8,8,64,128]{3,2,1,0:T(8,128)(2,1)}, bf16[8,8,64,128]{3,2,1,0:T(8,128)(2,1)}, u32[]{:S(2)}, u32[]{:S(2)}) %collective-permute-start.19) | collective-permute-done | bytes 1048608 | tf_op jit(solution)/shard_map/ppermute | solution.py:19
  83.9 3.6 %collective-permute-start.20 = (bf16[8,8,64,128]{3,2,1,0:T(8,128)(2,1)}, bf16[8,8,64,128]{3,2,1,0:T(8,128)(2,1)}, u32[]{:S(2)}, u32[]{:S(2)}) collective-permute-start(bf16[8,8,64,128]{3,2,1,0:T(8,128)(2,1)} %collective-permute-done.19.refs_1_), channel_id=1, source_target_pairs={{0,96},{32,0},{64,32},{96,64},{1,97},{33,1},{65,33},{97,65},{2,98}... | collective-permute-start | bytes 3145736 | tf_op jit(solution)/shard_map/ppermute | solution.py:19
  87.5 5.8 %product.4.refs_5_ = f32[512,1024]{1,0:T(8,128)S(1)} custom-call(s32[1]{0:T(128)} %bitcast.quarter_ref, bf16[8,8,64,128]{3,2,1,0:T(8,128)(2,1)} %all-to-all-done.refs_0_, bf16[8,8,64,128]{3,2,1,0:T(8,128)(2,1)} %collective-permute-done.5.refs_1_, bf16[8,8,64,128]{3,2,1,0:T(8,128)(2,1)} %collective-permute-done.6.refs_2_, bf16[8,32,1024]{2,1,0:T(8,128)(2,1)} %copy-done, ...), custom_call_target="tpu_custom_call" | custom-call | tf_op jit(solution)/shard_map/product/pallas_call | solution.py:233
  93.4 2.4 %product.5 = bf16[8,8,64,128]{3,2,1,0:T(8,128)(2,1)} custom-call(s32[1]{0:T(128)} %bitcast.quarter_ref, bf16[8,8,64,128]{3,2,1,0:T(8,128)(2,1)S(1)} %collective-permute-done.8.refs_0_, bf16[8,32,1024]{2,1,0:T(8,128)(2,1)S(1)} %collective-permute-done.10.refs_1_.refs_14_, bf16[8,32,1024]{2,1,0:T(8,128)(2,1)S(1)} %collective-permute-done.11.refs_2_.refs_15_, ...), custom_call_target="tpu_custom_call" | custom-call | tf_op jit(solution)/shard_map/product/pallas_call | solution.py:233
  95.8 5.3 %all-to-all-start.1 = ((bf16[8,8,64,128]{3,2,1,0:T(8,128)(2,1)}), bf16[8,8,64,128]{3,2,1,0:T(8,128)(2,1)S(1)}, u32[]{:S(2)}, u32[]{:S(2)}) async-start(bf16[8,8,64,128]{3,2,1,0:T(8,128)(2,1)} %product.5), calls=%async_computation.1 | async-start | bytes 2097152 | tf_op jit(solution)/shard_map/all_to_all | solution.py:27
  101.1 4.7 %product.6 = (f32[512,1024]{1,0:T(8,128)S(1)}, bf16[16,128,1024]{2,1,0:T(8,128)(2,1)S(1)}) custom-call(s32[1]{0:T(128)} %bitcast.quarter_ref, bf16[8,8,64,128]{3,2,1,0:T(8,128)(2,1)} %all-to-all-done.2.refs_0_, bf16[8,8,64,128]{3,2,1,0:T(8,128)(2,1)} %collective-permute-done.19.refs_1_, bf16[8,32,1024]{2,1,0:T(8,128)(2,1)} %copy-done, ...), custom_call_target="tpu_custom_call" | custom-call | tf_op jit(solution)/shard_map/product/pallas_call | solution.py:233
  105.8 3.9 %collective-permute-done.18.refs_0_ = bf16[8,8,64,128]{3,2,1,0:T(8,128)(2,1)} collective-permute-done((bf16[8,8,64,128]{3,2,1,0:T(8,128)(2,1)}, bf16[8,8,64,128]{3,2,1,0:T(8,128)(2,1)}, u32[]{:S(2)}, u32[]{:S(2)}) %collective-permute-start.18) | collective-permute-done | bytes 1048608 | tf_op jit(solution)/shard_map/ppermute | solution.py:19
  109.8 4.6 %product.7 = bf16[8,8,64,128]{3,2,1,0:T(8,128)(2,1)} custom-call(s32[1]{0:T(128)} %bitcast.quarter_ref, bf16[8,8,64,128]{3,2,1,0:T(8,128)(2,1)} %collective-permute-done.18.refs_0_, bf16[8,8,64,128]{3,2,1,0:T(8,128)(2,1)} %collective-permute-done.20.refs_1_, bf16[16,128,1024]{2,1,0:T(8,128)(2,1)S(1)} %get-tuple-element.71.refs_2_, ...), custom_call_target="tpu_custom_call" | custom-call | tf_op jit(solution)/shard_map/product/pallas_call | solution.py:233
  115.9 4.8 %all-to-all-start.3 = ((bf16[8,8,64,128]{3,2,1,0:T(8,128)(2,1)}), bf16[8,8,64,128]{3,2,1,0:T(8,128)(2,1)S(1)}, u32[]{:S(2)}, u32[]{:S(2)}) async-start(bf16[8,8,64,128]{3,2,1,0:T(8,128)(2,1)} %product.7), calls=%async_computation.3 | async-start | bytes 2097152 | tf_op jit(solution)/shard_map/all_to_all | solution.py:27
  123.6 11.8 %all-to-all-done.3.part_ref = bf16[8,8,64,128]{3,2,1,0:T(8,128)(2,1)S(1)} async-done(((bf16[8,8,64,128]{3,2,1,0:T(8,128)(2,1)}), bf16[8,8,64,128]{3,2,1,0:T(8,128)(2,1)S(1)}, u32[]{:S(2)}, u32[]{:S(2)}) %all-to-all-start.3) | async-done | bytes 1048608 | tf_op jit(solution)/shard_map/all_to_all | solution.py:27
  (56 shorter events, 9.1 us)
Async XLA Ops:
  2.6 16.1 %collective-permute-start = (bf16[8,32,1024]{2,1,0:T(8,128)(2,1)S(1)}, bf16[8,32,1024]{2,1,0:T(8,128)(2,1)S(1)}, u32[]{:S(2)}, u32[]{:S(2)}) collective-permute-start(bf16[8,32,1024]{2,1,0:T(8,128)(2,1)S(1)} %get-tuple-element.46), channel_id=1, source_target_pairs={{0,32},{32,64},{64,96},{96,0},{1,33},{33,65},{65,97},{97,1},{2,34}... | collective-permute-start | bytes 1572872 | tf_op jit(solution)/shard_map/ppermute | solution.py:19
  4.2 17.4 %collective-permute-start.2 = (bf16[8,32,1024]{2,1,0:T(8,128)(2,1)S(1)}, bf16[8,32,1024]{2,1,0:T(8,128)(2,1)}, u32[]{:S(2)}, u32[]{:S(2)}) collective-permute-start(bf16[8,32,1024]{2,1,0:T(8,128)(2,1)S(1)} %get-tuple-element.47), channel_id=1, source_target_pairs={{0,96},{32,0},{64,32},{96,64},{1,97},{33,1},{65,33},{97,65},{2,98}... | collective-permute-start | bytes 1572872 | tf_op jit(solution)/shard_map/ppermute | solution.py:19
  8.8 23.2 %all-to-all-start = ((bf16[8,8,64,128]{3,2,1,0:T(8,128)(2,1)}), bf16[8,8,64,128]{3,2,1,0:T(8,128)(2,1)}, u32[]{:S(2)}, u32[]{:S(2)}) async-start(bf16[8,8,64,128]{3,2,1,0:T(8,128)(2,1)} %order_amps.2), calls=%async_computation | async-start | bytes 2097152 | tf_op jit(solution)/shard_map/all_to_all | solution.py:27
  16.8 14.4 %collective-permute-start.4 = (bf16[8,32,1024]{2,1,0:T(8,128)(2,1)S(1)}, bf16[8,32,1024]{2,1,0:T(8,128)(2,1)}, u32[]{:S(2)}, u32[]{:S(2)}) collective-permute-start(bf16[8,32,1024]{2,1,0:T(8,128)(2,1)S(1)} %get-tuple-element.55.refs_3_.refs_2_), channel_id=1, source_target_pairs={{0,2},{1,3},{2,0},{3,1},{4,6},{5,7},{6,4},{7,5},{8,10},{9,11},{10,... | collective-permute-start | bytes 1572872 | tf_op jit(solution)/shard_map/ppermute | solution.py:23
  16.8 14.4 %collective-permute-start.10 = (bf16[8,32,1024]{2,1,0:T(8,128)(2,1)S(1)}, bf16[8,32,1024]{2,1,0:T(8,128)(2,1)S(1)}, u32[]{:S(2)}, u32[]{:S(2)}) collective-permute-start(bf16[8,32,1024]{2,1,0:T(8,128)(2,1)S(1)} %get-tuple-element.56), channel_id=1, source_target_pairs={{0,64},{32,96},{64,0},{96,32},{1,65},{33,97},{65,1},{97,33},{2,66}... | collective-permute-start | bytes 1572872 | tf_op jit(solution)/shard_map/ppermute | solution.py:19
  21.6 10.3 %collective-permute-start.1 = (bf16[8,32,1024]{2,1,0:T(8,128)(2,1)S(1)}, bf16[8,32,1024]{2,1,0:T(8,128)(2,1)S(1)}, u32[]{:S(2)}, u32[]{:S(2)}) collective-permute-start(bf16[8,32,1024]{2,1,0:T(8,128)(2,1)S(1)} %collective-permute-done.refs_7_.refs_10_), channel_id=1, source_target_pairs={{0,1},{1,0},{2,3},{3,2},{4,5},{5,4},{6,7},{7,6},{8,9},{9,8},{10,11... | collective-permute-start | bytes 1572872 | tf_op jit(solution)/shard_map/ppermute | solution.py:23
  21.7 10.2 %collective-permute-start.3 = (bf16[8,32,1024]{2,1,0:T(8,128)(2,1)}, bf16[8,32,1024]{2,1,0:T(8,128)(2,1)}, u32[]{:S(2)}, u32[]{:S(2)}) collective-permute-start(bf16[8,32,1024]{2,1,0:T(8,128)(2,1)} %collective-permute-done.2.refs_11_.refs_6_), channel_id=1, source_target_pairs={{0,1},{1,0},{2,3},{3,2},{4,5},{5,4},{6,7},{7,6},{8,9},{9,8},{10,11... | collective-permute-start | bytes 1572872 | tf_op jit(solution)/shard_map/ppermute | solution.py:23
  31.2 4.1 %collective-permute-start.11 = (bf16[8,32,1024]{2,1,0:T(8,128)(2,1)S(1)}, bf16[8,32,1024]{2,1,0:T(8,128)(2,1)S(1)}, u32[]{:S(2)}, u32[]{:S(2)}) collective-permute-start(bf16[8,32,1024]{2,1,0:T(8,128)(2,1)S(1)} %collective-permute-done.10.refs_1_.refs_14_), channel_id=1, source_target_pairs={{0,1},{1,0},{2,3},{3,2},{4,5},{5,4},{6,7},{7,6},{8,9},{9,8},{10,11... | collective-permute-start | bytes 1572872 | tf_op jit(solution)/shard_map/ppermute | solution.py:23
  32.0 29.9 %collective-permute-start.5 = (bf16[8,8,64,128]{3,2,1,0:T(8,128)(2,1)}, bf16[8,8,64,128]{3,2,1,0:T(8,128)(2,1)}, u32[]{:S(2)}, u32[]{:S(2)}) collective-permute-start(bf16[8,8,64,128]{3,2,1,0:T(8,128)(2,1)} %all-to-all-done.refs_0_), channel_id=1, source_target_pairs={{0,32},{32,64},{64,96},{96,0},{1,33},{33,65},{65,97},{97,1},{2,34}... | collective-permute-start | bytes 3145736 | tf_op jit(solution)/shard_map/ppermute | solution.py:19
  32.4 29.6 %collective-permute-start.6 = (bf16[8,8,64,128]{3,2,1,0:T(8,128)(2,1)}, bf16[8,8,64,128]{3,2,1,0:T(8,128)(2,1)}, u32[]{:S(2)}, u32[]{:S(2)}) collective-permute-start(bf16[8,8,64,128]{3,2,1,0:T(8,128)(2,1)} %all-to-all-done.refs_0_), channel_id=1, source_target_pairs={{0,96},{32,0},{64,32},{96,64},{1,97},{33,1},{65,33},{97,65},{2,98}... | collective-permute-start | bytes 3145736 | tf_op jit(solution)/shard_map/ppermute | solution.py:19
  35.4 24.3 %all-to-all-start.2 = ((bf16[8,8,64,128]{3,2,1,0:T(8,128)(2,1)}), bf16[8,8,64,128]{3,2,1,0:T(8,128)(2,1)}, u32[]{:S(2)}, u32[]{:S(2)}) async-start(bf16[8,8,64,128]{3,2,1,0:T(8,128)(2,1)} %order_amps.3), calls=%async_computation.2 | async-start | bytes 2097152 | tf_op jit(solution)/shard_map/all_to_all | solution.py:27
  43.6 18.3 %collective-permute-start.7 = (bf16[8,32,1024]{2,1,0:T(8,128)(2,1)S(1)}, bf16[8,32,1024]{2,1,0:T(8,128)(2,1)S(1)}, u32[]{:S(2)}, u32[]{:S(2)}) collective-permute-start(bf16[8,32,1024]{2,1,0:T(8,128)(2,1)S(1)} %collective-permute-done.refs_7_.refs_10_), channel_id=1, source_target_pairs={{0,2},{1,3},{2,0},{3,1},{4,6},{5,7},{6,4},{7,5},{8,10},{9,11},{10,... | collective-permute-start | bytes 1572872 | tf_op jit(solution)/shard_map/ppermute | solution.py:23
  43.7 26.2 %collective-permute-start.14 = (bf16[8,32,1024]{2,1,0:T(8,128)(2,1)}, bf16[8,32,1024]{2,1,0:T(8,128)(2,1)}, u32[]{:S(2)}, u32[]{:S(2)}) collective-permute-start(bf16[8,32,1024]{2,1,0:T(8,128)(2,1)} %collective-permute-done.2.refs_11_.refs_6_), channel_id=1, source_target_pairs={{0,2},{1,3},{2,0},{3,1},{4,6},{5,7},{6,4},{7,5},{8,10},{9,11},{10,... | collective-permute-start | bytes 1572872 | tf_op jit(solution)/shard_map/ppermute | solution.py:23
  59.6 24.3 %collective-permute-start.19 = (bf16[8,8,64,128]{3,2,1,0:T(8,128)(2,1)}, bf16[8,8,64,128]{3,2,1,0:T(8,128)(2,1)}, u32[]{:S(2)}, u32[]{:S(2)}) collective-permute-start(bf16[8,8,64,128]{3,2,1,0:T(8,128)(2,1)} %all-to-all-done.2.refs_0_), channel_id=1, source_target_pairs={{0,96},{32,0},{64,32},{96,64},{1,97},{33,1},{65,33},{97,65},{2,98}... | collective-permute-start | bytes 3145736 | tf_op jit(solution)/shard_map/ppermute | solution.py:19
  61.9 17.6 %collective-permute-start.16 = (bf16[8,32,1024]{2,1,0:T(8,128)(2,1)S(1)}, bf16[8,32,1024]{2,1,0:T(8,128)(2,1)S(1)}, u32[]{:S(2)}, u32[]{:S(2)}) collective-permute-start(bf16[8,32,1024]{2,1,0:T(8,128)(2,1)S(1)} %collective-permute-done.10.refs_1_.refs_14_), channel_id=1, source_target_pairs={{0,2},{1,3},{2,0},{3,1},{4,6},{5,7},{6,4},{7,5},{8,10},{9,11},{10,... | collective-permute-start | bytes 1572872 | tf_op jit(solution)/shard_map/ppermute | solution.py:23
  62.0 31.4 %collective-permute-start.8 = (bf16[8,8,64,128]{3,2,1,0:T(8,128)(2,1)}, bf16[8,8,64,128]{3,2,1,0:T(8,128)(2,1)S(1)}, u32[]{:S(2)}, u32[]{:S(2)}) collective-permute-start(bf16[8,8,64,128]{3,2,1,0:T(8,128)(2,1)} %collective-permute-done.5.refs_1_), channel_id=1, source_target_pairs={{0,32},{32,64},{64,96},{96,0},{1,33},{33,65},{65,97},{97,1},{2,34}... | collective-permute-start | bytes 3145736 | tf_op jit(solution)/shard_map/ppermute | solution.py:19
  62.1 17.5 %collective-permute-start.13 = (bf16[8,32,1024]{2,1,0:T(8,128)(2,1)S(1)}, bf16[8,32,1024]{2,1,0:T(8,128)(2,1)S(1)}, u32[]{:S(2)}, u32[]{:S(2)}) collective-permute-start(bf16[8,32,1024]{2,1,0:T(8,128)(2,1)S(1)} %collective-permute-done.7.refs_9_.refs_12_), channel_id=1, source_target_pairs={{0,1},{1,0},{2,3},{3,2},{4,5},{5,4},{6,7},{7,6},{8,9},{9,8},{10,11... | collective-permute-start | bytes 1572872 | tf_op jit(solution)/shard_map/ppermute | solution.py:23
  69.9 11.0 %collective-permute-start.12 = (bf16[8,32,1024]{2,1,0:T(8,128)(2,1)}, bf16[8,32,1024]{2,1,0:T(8,128)(2,1)}, u32[]{:S(2)}, u32[]{:S(2)}) collective-permute-start(bf16[8,32,1024]{2,1,0:T(8,128)(2,1)} %collective-permute-done.4.refs_5_.refs_4_), channel_id=1, source_target_pairs={{0,1},{1,0},{2,3},{3,2},{4,5},{5,4},{6,7},{7,6},{8,9},{9,8},{10,11... | collective-permute-start | bytes 1572872 | tf_op jit(solution)/shard_map/ppermute | solution.py:23
  79.6 7.9 %collective-permute-start.15 = (bf16[8,32,1024]{2,1,0:T(8,128)(2,1)}, bf16[8,32,1024]{2,1,0:T(8,128)(2,1)}, u32[]{:S(2)}, u32[]{:S(2)}) collective-permute-start(bf16[8,32,1024]{2,1,0:T(8,128)(2,1)} %collective-permute-done.14.refs_13_.refs_8_), channel_id=1, source_target_pairs={{0,1},{1,0},{2,3},{3,2},{4,5},{5,4},{6,7},{7,6},{8,9},{9,8},{10,11... | collective-permute-start | bytes 1572872 | tf_op jit(solution)/shard_map/ppermute | solution.py:23
  80.4 12.9 %collective-permute-start.17 = (bf16[8,32,1024]{2,1,0:T(8,128)(2,1)S(1)}, bf16[8,32,1024]{2,1,0:T(8,128)(2,1)S(1)}, u32[]{:S(2)}, u32[]{:S(2)}) collective-permute-start(bf16[8,32,1024]{2,1,0:T(8,128)(2,1)S(1)} %collective-permute-done.16.refs_3_.refs_16_), channel_id=1, source_target_pairs={{0,1},{1,0},{2,3},{3,2},{4,5},{5,4},{6,7},{7,6},{8,9},{9,8},{10,11... | collective-permute-start | bytes 1572872 | tf_op jit(solution)/shard_map/ppermute | solution.py:23
  80.9 28.9 %collective-permute-start.18 = (bf16[8,8,64,128]{3,2,1,0:T(8,128)(2,1)}, bf16[8,8,64,128]{3,2,1,0:T(8,128)(2,1)}, u32[]{:S(2)}, u32[]{:S(2)}) collective-permute-start(bf16[8,8,64,128]{3,2,1,0:T(8,128)(2,1)} %all-to-all-done.2.refs_0_), channel_id=1, source_target_pairs={{0,32},{32,64},{64,96},{96,0},{1,33},{33,65},{65,97},{97,1},{2,34}... | collective-permute-start | bytes 3145736 | tf_op jit(solution)/shard_map/ppermute | solution.py:19
  83.9 25.9 %collective-permute-start.20 = (bf16[8,8,64,128]{3,2,1,0:T(8,128)(2,1)}, bf16[8,8,64,128]{3,2,1,0:T(8,128)(2,1)}, u32[]{:S(2)}, u32[]{:S(2)}) collective-permute-start(bf16[8,8,64,128]{3,2,1,0:T(8,128)(2,1)} %collective-permute-done.19.refs_1_), channel_id=1, source_target_pairs={{0,96},{32,0},{64,32},{96,64},{1,97},{33,1},{65,33},{97,65},{2,98}... | collective-permute-start | bytes 3145736 | tf_op jit(solution)/shard_map/ppermute | solution.py:19
  95.8 20.1 %all-to-all-start.1 = ((bf16[8,8,64,128]{3,2,1,0:T(8,128)(2,1)}), bf16[8,8,64,128]{3,2,1,0:T(8,128)(2,1)S(1)}, u32[]{:S(2)}, u32[]{:S(2)}) async-start(bf16[8,8,64,128]{3,2,1,0:T(8,128)(2,1)} %product.5), calls=%async_computation.1 | async-start | bytes 2097152 | tf_op jit(solution)/shard_map/all_to_all | solution.py:27
  115.9 19.5 %all-to-all-start.3 = ((bf16[8,8,64,128]{3,2,1,0:T(8,128)(2,1)}), bf16[8,8,64,128]{3,2,1,0:T(8,128)(2,1)S(1)}, u32[]{:S(2)}, u32[]{:S(2)}) async-start(bf16[8,8,64,128]{3,2,1,0:T(8,128)(2,1)} %product.7), calls=%async_computation.3 | async-start | bytes 2097152 | tf_op jit(solution)/shard_map/all_to_all | solution.py:27
  (11 other events, 248.5 us)

commit v7 on v5

--- a/solution.py
+++ b/solution.py
@@ -37,20 +37,22 @@
     return pl.CostEstimate(flops=0, bytes_accessed=0, transcendentals=0)
 
 
-def order_body(offset, pair_ref, amps_ref, out_ref, sems):
-    irreps, _, step, _ = out_ref.shape
+def order_body(offset, pair_ref, amps_ref, out_ref, held, in_sems, out_sems):
+    irreps, _, step, _ = held.shape
     pair_xor = jnp.bitwise_xor(pair_ref[0], pair_ref[1])
-    copies = [
+    arriving = [
         pltpu.make_async_copy(
-            amps_ref.at[:, jnp.bitwise_xor(g, pair_xor), offset:offset + step],
-            out_ref.at[g],
-            sems.at[g],
+            amps_ref.at[:, jnp.bitwise_xor(g, pair_xor), offset:offset + step], held.at[g], in_sems.at[g]
         )
         for g in range(irreps)
     ]
-    for copy in copies:
+    leaving = [pltpu.make_async_copy(held.at[g], out_ref.at[g], out_sems.at[g]) for g in range(irreps)]
+    for copy in arriving:
         copy.start()
-    for copy in copies:
+    for g in range(irreps):
+        arriving[g].wait()
+        leaving[g].start()
+    for copy in leaving:
         copy.wait()
 
 
@@ -58,10 +60,14 @@
     nk, irreps, _, cols = amps.shape
     return pl.pallas_call(
         functools.partial(order_body, offset),
-        out_shape=pltpu.VMEM((irreps, nk, step, cols), amps.dtype),
+        out_shape=jax.ShapeDtypeStruct((irreps, nk, step, cols), amps.dtype),
         in_specs=[pl.BlockSpec(memory_space=pltpu.SMEM), pl.BlockSpec(memory_space=pl.ANY)],
-        out_specs=pl.BlockSpec(memory_space=pltpu.VMEM),
-        scratch_shapes=[pltpu.SemaphoreType.DMA((irreps,))],
+        out_specs=pl.BlockSpec(memory_space=pl.ANY),
+        scratch_shapes=[
+            pltpu.VMEM((irreps, nk, step, cols), amps.dtype),
+            pltpu.SemaphoreType.DMA((irreps,)),
+            pltpu.SemaphoreType.DMA((irreps,)),
+        ],
         compiler_params=params(16),
         cost_estimate=cost(0, 0),
         name="order_amps",

time: 137 us -> 137 us (level)
  no operation moved by 1% of the time
where the time goes in v7:
time: 137 us
  waiting for transfers between devices  61.4 us (45%)
  starting transfers between devices  44.4 us (32%)
  Pallas kernels  27.8 us (20%)
  between operations  1.76 us (1%)
  local copies, waits for them, and re-layouts  1.44 us (1%)
    all_to_all x4, waiting for transfers between devices, exchange_irreps(): lax.all_to_all(array, 'ten', split_axis=0, concat_axis=0, axis_index_grou...  27.9 us
    all_to_all x4, starting transfers between devices, exchange_irreps(): lax.all_to_all(array, 'ten', split_axis=0, concat_axis=0, axis_index_grou...  26.6 us
    pallas_call x4, Pallas kernels, product(): pl.pallas_call(functools.partial(product_body, plan, len(hold), sums is n...  17.9 us
    ppermute x12, waiting for transfers between devices, flip_ten(): lax.ppermute(array, 'ten', [(s, s ^ mask) for s in range(lax.axis_size('t...  17.5 us
    ppermute x9, waiting for transfers between devices, shift_rep(): lax.ppermute(array, 'rep', [(s, (s + distance) % n) for s in range(n)])  16.1 us
    ppermute x9, starting transfers between devices, shift_rep(): lax.ppermute(array, 'rep', [(s, (s + distance) % n) for s in range(n)])  14.5 us
    pallas_call x2, Pallas kernels, order_amps(): pl.pallas_call(functools.partial(order_body, offset), out_shape=jax.Shape...  5.3 us
    ppermute x12, starting transfers between devices, flip_ten(): lax.ppermute(array, 'ten', [(s, s ^ mask) for s in range(lax.axis_size('t...  3.34 us
  transfers between devices with their start and end apart: 25, of which 9 were waited for; matrix products, arithmetic and copies ran while one was open for 0% of the time, Pallas kernels for 18%

profile of v7, /device:TPU:0, one launch (start us, length us, event | category | flops | bytes accessed | tf_op | source)
XLA Modules:
  0.0 136.8 jit_solution(356187302595002984)
XLA Ops:
  0.0 2.5 %integrals_by_j.1 = (bf16[8,32,1024]{2,1,0:T(8,128)(2,1)S(1)}, bf16[8,32,1024]{2,1,0:T(8,128)(2,1)S(1)}, bf16[8,32,1024]{2,1,0:T(8,128)(2,1)S(1)}, bf16[8,32,1024]{2,1,0:T(8,128)(2,1)S(1)}) custom-call(bf16[8,32,32,128]{3,2,1,0:T(8,128)(2,1)} %w_ref.1), custom_call_target="tpu_custom_call" | custom-call | tf_op jit(solution)/shard_map/integrals_by_j/pallas_call | solution.py:99
  4.2 1.7 %collective-permute-start.2 = (bf16[8,32,1024]{2,1,0:T(8,128)(2,1)S(1)}, bf16[8,32,1024]{2,1,0:T(8,128)(2,1)}, u32[]{:S(2)}, u32[]{:S(2)}) collective-permute-start(bf16[8,32,1024]{2,1,0:T(8,128)(2,1)S(1)} %get-tuple-element.47), channel_id=1, source_target_pairs={{0,96},{32,0},{64,32},{96,64},{1,97},{33,1},{65,33},{97,65},{2,98}... | collective-permute-start | bytes 1572872 | tf_op jit(solution)/shard_map/ppermute | solution.py:19
  5.9 2.7 %order_amps.2 = bf16[8,8,64,128]{3,2,1,0:T(8,128)(2,1)} custom-call(s32[2]{0:T(128)S(1)} %copy-done.5, bf16[8,8,128,128]{3,2,1,0:T(8,128)(2,1)} %bitcast.3), custom_call_target="tpu_custom_call" | custom-call | tf_op jit(solution)/shard_map/order_amps/pallas_call | solution.py:61
  8.5 8.0 %all-to-all-start = ((bf16[8,8,64,128]{3,2,1,0:T(8,128)(2,1)}), bf16[8,8,64,128]{3,2,1,0:T(8,128)(2,1)}, u32[]{:S(2)}, u32[]{:S(2)}) async-start(bf16[8,8,64,128]{3,2,1,0:T(8,128)(2,1)} %order_amps.2), calls=%async_computation | async-start | bytes 2097152 | tf_op jit(solution)/shard_map/all_to_all | solution.py:27
  16.6 1.9 %collective-permute-start.10 = (bf16[8,32,1024]{2,1,0:T(8,128)(2,1)S(1)}, bf16[8,32,1024]{2,1,0:T(8,128)(2,1)S(1)}, u32[]{:S(2)}, u32[]{:S(2)}) collective-permute-start(bf16[8,32,1024]{2,1,0:T(8,128)(2,1)S(1)} %get-tuple-element.56), channel_id=1, source_target_pairs={{0,64},{32,96},{64,0},{96,32},{1,65},{33,97},{65,1},{97,33},{2,66}... | collective-permute-start | bytes 1572872 | tf_op jit(solution)/shard_map/ppermute | solution.py:19
  18.5 2.6 %order_amps.3 = bf16[8,8,64,128]{3,2,1,0:T(8,128)(2,1)} custom-call(s32[2]{0:T(128)S(1)} %copy-done.5, bf16[8,8,128,128]{3,2,1,0:T(8,128)(2,1)} %bitcast.4), custom_call_target="tpu_custom_call" | custom-call | tf_op jit(solution)/shard_map/order_amps/pallas_call | solution.py:61
  21.7 9.3 %collective-permute-done.10.refs_1_.refs_14_ = bf16[8,32,1024]{2,1,0:T(8,128)(2,1)S(1)} collective-permute-done((bf16[8,32,1024]{2,1,0:T(8,128)(2,1)S(1)}, bf16[8,32,1024]{2,1,0:T(8,128)(2,1)S(1)}, u32[]{:S(2)}, u32[]{:S(2)}) %collective-permute-start.10) | collective-permute-done | bytes 524320 | tf_op jit(solution)/shard_map/ppermute | solution.py:19
  32.2 3.0 %collective-permute-start.6 = (bf16[8,8,64,128]{3,2,1,0:T(8,128)(2,1)}, bf16[8,8,64,128]{3,2,1,0:T(8,128)(2,1)}, u32[]{:S(2)}, u32[]{:S(2)}) collective-permute-start(bf16[8,8,64,128]{3,2,1,0:T(8,128)(2,1)} %all-to-all-done.refs_0_), channel_id=1, source_target_pairs={{0,96},{32,0},{64,32},{96,64},{1,97},{33,1},{65,33},{97,65},{2,98}... | collective-permute-start | bytes 3145736 | tf_op jit(solution)/shard_map/ppermute | solution.py:19
  35.1 8.5 %all-to-all-start.2 = ((bf16[8,8,64,128]{3,2,1,0:T(8,128)(2,1)}), bf16[8,8,64,128]{3,2,1,0:T(8,128)(2,1)}, u32[]{:S(2)}, u32[]{:S(2)}) async-start(bf16[8,8,64,128]{3,2,1,0:T(8,128)(2,1)} %order_amps.3), calls=%async_computation.2 | async-start | bytes 2097152 | tf_op jit(solution)/shard_map/all_to_all | solution.py:27
  43.7 2.0 %collective-permute-start.14 = (bf16[8,32,1024]{2,1,0:T(8,128)(2,1)}, bf16[8,32,1024]{2,1,0:T(8,128)(2,1)}, u32[]{:S(2)}, u32[]{:S(2)}) collective-permute-start(bf16[8,32,1024]{2,1,0:T(8,128)(2,1)} %collective-permute-done.2.refs_11_.refs_6_), channel_id=1, source_target_pairs={{0,2},{1,3},{2,0},{3,1},{4,6},{5,7},{6,4},{7,5},{8,10},{9,11},{10,... | collective-permute-start | bytes 1572872 | tf_op jit(solution)/shard_map/ppermute | solution.py:23
  45.7 13.9 %all-to-all-done.2.refs_0_ = bf16[8,8,64,128]{3,2,1,0:T(8,128)(2,1)} async-done(((bf16[8,8,64,128]{3,2,1,0:T(8,128)(2,1)}), bf16[8,8,64,128]{3,2,1,0:T(8,128)(2,1)}, u32[]{:S(2)}, u32[]{:S(2)}) %all-to-all-start.2) | async-done | bytes 1048608 | tf_op jit(solution)/shard_map/all_to_all | solution.py:27
  59.6 2.3 %collective-permute-start.19 = (bf16[8,8,64,128]{3,2,1,0:T(8,128)(2,1)}, bf16[8,8,64,128]{3,2,1,0:T(8,128)(2,1)}, u32[]{:S(2)}, u32[]{:S(2)}) collective-permute-start(bf16[8,8,64,128]{3,2,1,0:T(8,128)(2,1)} %all-to-all-done.2.refs_0_), channel_id=1, source_target_pairs={{0,96},{32,0},{64,32},{96,64},{1,97},{33,1},{65,33},{97,65},{2,98}... | collective-permute-start | bytes 3145736 | tf_op jit(solution)/shard_map/ppermute | solution.py:19
  62.1 7.7 %collective-permute-done.14.refs_13_.refs_8_ = bf16[8,32,1024]{2,1,0:T(8,128)(2,1)} collective-permute-done((bf16[8,32,1024]{2,1,0:T(8,128)(2,1)}, bf16[8,32,1024]{2,1,0:T(8,128)(2,1)}, u32[]{:S(2)}, u32[]{:S(2)}) %collective-permute-start.14) | collective-permute-done | bytes 524320 | tf_op jit(solution)/shard_map/ppermute | solution.py:23
  69.9 9.7 %collective-permute-done.16.refs_3_.refs_16_ = bf16[8,32,1024]{2,1,0:T(8,128)(2,1)S(1)} collective-permute-done((bf16[8,32,1024]{2,1,0:T(8,128)(2,1)S(1)}, bf16[8,32,1024]{2,1,0:T(8,128)(2,1)S(1)}, u32[]{:S(2)}, u32[]{:S(2)}) %collective-permute-start.16) | collective-permute-done | bytes 524320 | tf_op jit(solution)/shard_map/ppermute | solution.py:23
  80.9 3.0 %collective-permute-done.19.refs_1_ = bf16[8,8,64,128]{3,2,1,0:T(8,128)(2,1)} collective-permute-done((bf16[8,8,64,128]{3,2,1,0:T(8,128)(2,1)}, bf16[8,8,64,128]{3,2,1,0:T(8,128)(2,1)}, u32[]{:S(2)}, u32[]{:S(2)}) %collective-permute-start.19) | collective-permute-done | bytes 1048608 | tf_op jit(solution)/shard_map/ppermute | solution.py:19
  83.9 3.6 %collective-permute-start.20 = (bf16[8,8,64,128]{3,2,1,0:T(8,128)(2,1)}, bf16[8,8,64,128]{3,2,1,0:T(8,128)(2,1)}, u32[]{:S(2)}, u32[]{:S(2)}) collective-permute-start(bf16[8,8,64,128]{3,2,1,0:T(8,128)(2,1)} %collective-permute-done.19.refs_1_), channel_id=1, source_target_pairs={{0,96},{32,0},{64,32},{96,64},{1,97},{33,1},{65,33},{97,65},{2,98}... | collective-permute-start | bytes 3145736 | tf_op jit(solution)/shard_map/ppermute | solution.py:19
  87.5 5.8 %product.4.refs_5_ = f32[512,1024]{1,0:T(8,128)S(1)} custom-call(s32[1]{0:T(128)} %bitcast.quarter_ref, bf16[8,8,64,128]{3,2,1,0:T(8,128)(2,1)} %all-to-all-done.refs_0_, bf16[8,8,64,128]{3,2,1,0:T(8,128)(2,1)} %collective-permute-done.5.refs_1_, bf16[8,8,64,128]{3,2,1,0:T(8,128)(2,1)} %collective-permute-done.6.refs_2_, bf16[8,32,1024]{2,1,0:T(8,128)(2,1)} %copy-done, ...), custom_call_target="tpu_custom_call" | custom-call | tf_op jit(solution)/shard_map/product/pallas_call | solution.py:220
  93.4 2.5 %product.5 = bf16[8,8,64,128]{3,2,1,0:T(8,128)(2,1)} custom-call(s32[1]{0:T(128)} %bitcast.quarter_ref, bf16[8,8,64,128]{3,2,1,0:T(8,128)(2,1)S(1)} %collective-permute-done.8.refs_0_, bf16[8,32,1024]{2,1,0:T(8,128)(2,1)S(1)} %collective-permute-done.10.refs_1_.refs_14_, bf16[8,32,1024]{2,1,0:T(8,128)(2,1)S(1)} %collective-permute-done.11.refs_2_.refs_15_, ...), custom_call_target="tpu_custom_call" | custom-call | tf_op jit(solution)/shard_map/product/pallas_call | solution.py:220
  95.9 5.3 %all-to-all-start.1 = ((bf16[8,8,64,128]{3,2,1,0:T(8,128)(2,1)}), bf16[8,8,64,128]{3,2,1,0:T(8,128)(2,1)S(1)}, u32[]{:S(2)}, u32[]{:S(2)}) async-start(bf16[8,8,64,128]{3,2,1,0:T(8,128)(2,1)} %product.5), calls=%async_computation.1 | async-start | bytes 2097152 | tf_op jit(solution)/shard_map/all_to_all | solution.py:27
  101.3 4.7 %product.6 = (f32[512,1024]{1,0:T(8,128)S(1)}, bf16[16,128,1024]{2,1,0:T(8,128)(2,1)S(1)}) custom-call(s32[1]{0:T(128)} %bitcast.quarter_ref, bf16[8,8,64,128]{3,2,1,0:T(8,128)(2,1)} %all-to-all-done.2.refs_0_, bf16[8,8,64,128]{3,2,1,0:T(8,128)(2,1)} %collective-permute-done.19.refs_1_, bf16[8,32,1024]{2,1,0:T(8,128)(2,1)} %copy-done, ...), custom_call_target="tpu_custom_call" | custom-call | tf_op jit(solution)/shard_map/product/pallas_call | solution.py:220
  106.0 3.8 %collective-permute-done.18.refs_0_ = bf16[8,8,64,128]{3,2,1,0:T(8,128)(2,1)} collective-permute-done((bf16[8,8,64,128]{3,2,1,0:T(8,128)(2,1)}, bf16[8,8,64,128]{3,2,1,0:T(8,128)(2,1)}, u32[]{:S(2)}, u32[]{:S(2)}) %collective-permute-start.18) | collective-permute-done | bytes 1048608 | tf_op jit(solution)/shard_map/ppermute | solution.py:19
  109.8 4.8 %product.7 = bf16[8,8,64,128]{3,2,1,0:T(8,128)(2,1)} custom-call(s32[1]{0:T(128)} %bitcast.quarter_ref, bf16[8,8,64,128]{3,2,1,0:T(8,128)(2,1)} %collective-permute-done.18.refs_0_, bf16[8,8,64,128]{3,2,1,0:T(8,128)(2,1)} %collective-permute-done.20.refs_1_, bf16[16,128,1024]{2,1,0:T(8,128)(2,1)S(1)} %get-tuple-element.71.refs_2_, ...), custom_call_target="tpu_custom_call" | custom-call | tf_op jit(solution)/shard_map/product/pallas_call | solution.py:220
  116.1 4.8 %all-to-all-start.3 = ((bf16[8,8,64,128]{3,2,1,0:T(8,128)(2,1)}), bf16[8,8,64,128]{3,2,1,0:T(8,128)(2,1)S(1)}, u32[]{:S(2)}, u32[]{:S(2)}) async-start(bf16[8,8,64,128]{3,2,1,0:T(8,128)(2,1)} %product.7), calls=%async_computation.3 | async-start | bytes 2097152 | tf_op jit(solution)/shard_map/all_to_all | solution.py:27
  123.8 11.8 %all-to-all-done.3.part_ref = bf16[8,8,64,128]{3,2,1,0:T(8,128)(2,1)S(1)} async-done(((bf16[8,8,64,128]{3,2,1,0:T(8,128)(2,1)}), bf16[8,8,64,128]{3,2,1,0:T(8,128)(2,1)S(1)}, u32[]{:S(2)}, u32[]{:S(2)}) %all-to-all-start.3) | async-done | bytes 1048608 | tf_op jit(solution)/shard_map/all_to_all | solution.py:27
  (56 shorter events, 9.1 us)
Async XLA Ops:
  2.6 15.9 %collective-permute-start = (bf16[8,32,1024]{2,1,0:T(8,128)(2,1)S(1)}, bf16[8,32,1024]{2,1,0:T(8,128)(2,1)S(1)}, u32[]{:S(2)}, u32[]{:S(2)}) collective-permute-start(bf16[8,32,1024]{2,1,0:T(8,128)(2,1)S(1)} %get-tuple-element.46), channel_id=1, source_target_pairs={{0,32},{32,64},{64,96},{96,0},{1,33},{33,65},{65,97},{97,1},{2,34}... | collective-permute-start | bytes 1572872 | tf_op jit(solution)/shard_map/ppermute | solution.py:19
  4.2 16.9 %collective-permute-start.2 = (bf16[8,32,1024]{2,1,0:T(8,128)(2,1)S(1)}, bf16[8,32,1024]{2,1,0:T(8,128)(2,1)}, u32[]{:S(2)}, u32[]{:S(2)}) collective-permute-start(bf16[8,32,1024]{2,1,0:T(8,128)(2,1)S(1)} %get-tuple-element.47), channel_id=1, source_target_pairs={{0,96},{32,0},{64,32},{96,64},{1,97},{33,1},{65,33},{97,65},{2,98}... | collective-permute-start | bytes 1572872 | tf_op jit(solution)/shard_map/ppermute | solution.py:19
  8.5 23.2 %all-to-all-start = ((bf16[8,8,64,128]{3,2,1,0:T(8,128)(2,1)}), bf16[8,8,64,128]{3,2,1,0:T(8,128)(2,1)}, u32[]{:S(2)}, u32[]{:S(2)}) async-start(bf16[8,8,64,128]{3,2,1,0:T(8,128)(2,1)} %order_amps.2), calls=%async_computation | async-start | bytes 2097152 | tf_op jit(solution)/shard_map/all_to_all | solution.py:27
  16.6 14.4 %collective-permute-start.4 = (bf16[8,32,1024]{2,1,0:T(8,128)(2,1)S(1)}, bf16[8,32,1024]{2,1,0:T(8,128)(2,1)}, u32[]{:S(2)}, u32[]{:S(2)}) collective-permute-start(bf16[8,32,1024]{2,1,0:T(8,128)(2,1)S(1)} %get-tuple-element.55.refs_3_.refs_2_), channel_id=1, source_target_pairs={{0,2},{1,3},{2,0},{3,1},{4,6},{5,7},{6,4},{7,5},{8,10},{9,11},{10,... | collective-permute-start | bytes 1572872 | tf_op jit(solution)/shard_map/ppermute | solution.py:23
  16.6 14.4 %collective-permute-start.10 = (bf16[8,32,1024]{2,1,0:T(8,128)(2,1)S(1)}, bf16[8,32,1024]{2,1,0:T(8,128)(2,1)S(1)}, u32[]{:S(2)}, u32[]{:S(2)}) collective-permute-start(bf16[8,32,1024]{2,1,0:T(8,128)(2,1)S(1)} %get-tuple-element.56), channel_id=1, source_target_pairs={{0,64},{32,96},{64,0},{96,32},{1,65},{33,97},{65,1},{97,33},{2,66}... | collective-permute-start | bytes 1572872 | tf_op jit(solution)/shard_map/ppermute | solution.py:19
  21.1 10.6 %collective-permute-start.1 = (bf16[8,32,1024]{2,1,0:T(8,128)(2,1)S(1)}, bf16[8,32,1024]{2,1,0:T(8,128)(2,1)S(1)}, u32[]{:S(2)}, u32[]{:S(2)}) collective-permute-start(bf16[8,32,1024]{2,1,0:T(8,128)(2,1)S(1)} %collective-permute-done.refs_7_.refs_10_), channel_id=1, source_target_pairs={{0,1},{1,0},{2,3},{3,2},{4,5},{5,4},{6,7},{7,6},{8,9},{9,8},{10,11... | collective-permute-start | bytes 1572872 | tf_op jit(solution)/shard_map/ppermute | solution.py:23
  21.2 10.5 %collective-permute-start.3 = (bf16[8,32,1024]{2,1,0:T(8,128)(2,1)}, bf16[8,32,1024]{2,1,0:T(8,128)(2,1)}, u32[]{:S(2)}, u32[]{:S(2)}) collective-permute-start(bf16[8,32,1024]{2,1,0:T(8,128)(2,1)} %collective-permute-done.2.refs_11_.refs_6_), channel_id=1, source_target_pairs={{0,1},{1,0},{2,3},{3,2},{4,5},{5,4},{6,7},{7,6},{8,9},{9,8},{10,11... | collective-permute-start | bytes 1572872 | tf_op jit(solution)/shard_map/ppermute | solution.py:23
  31.0 4.1 %collective-permute-start.11 = (bf16[8,32,1024]{2,1,0:T(8,128)(2,1)S(1)}, bf16[8,32,1024]{2,1,0:T(8,128)(2,1)S(1)}, u32[]{:S(2)}, u32[]{:S(2)}) collective-permute-start(bf16[8,32,1024]{2,1,0:T(8,128)(2,1)S(1)} %collective-permute-done.10.refs_1_.refs_14_), channel_id=1, source_target_pairs={{0,1},{1,0},{2,3},{3,2},{4,5},{5,4},{6,7},{7,6},{8,9},{9,8},{10,11... | collective-permute-start | bytes 1572872 | tf_op jit(solution)/shard_map/ppermute | solution.py:23
  31.8 30.1 %collective-permute-start.5 = (bf16[8,8,64,128]{3,2,1,0:T(8,128)(2,1)}, bf16[8,8,64,128]{3,2,1,0:T(8,128)(2,1)}, u32[]{:S(2)}, u32[]{:S(2)}) collective-permute-start(bf16[8,8,64,128]{3,2,1,0:T(8,128)(2,1)} %all-to-all-done.refs_0_), channel_id=1, source_target_pairs={{0,32},{32,64},{64,96},{96,0},{1,33},{33,65},{65,97},{97,1},{2,34}... | collective-permute-start | bytes 3145736 | tf_op jit(solution)/shard_map/ppermute | solution.py:19
  32.2 29.8 %collective-permute-start.6 = (bf16[8,8,64,128]{3,2,1,0:T(8,128)(2,1)}, bf16[8,8,64,128]{3,2,1,0:T(8,128)(2,1)}, u32[]{:S(2)}, u32[]{:S(2)}) collective-permute-start(bf16[8,8,64,128]{3,2,1,0:T(8,128)(2,1)} %all-to-all-done.refs_0_), channel_id=1, source_target_pairs={{0,96},{32,0},{64,32},{96,64},{1,97},{33,1},{65,33},{97,65},{2,98}... | collective-permute-start | bytes 3145736 | tf_op jit(solution)/shard_map/ppermute | solution.py:19
  35.1 24.5 %all-to-all-start.2 = ((bf16[8,8,64,128]{3,2,1,0:T(8,128)(2,1)}), bf16[8,8,64,128]{3,2,1,0:T(8,128)(2,1)}, u32[]{:S(2)}, u32[]{:S(2)}) async-start(bf16[8,8,64,128]{3,2,1,0:T(8,128)(2,1)} %order_amps.3), calls=%async_computation.2 | async-start | bytes 2097152 | tf_op jit(solution)/shard_map/all_to_all | solution.py:27
  43.6 18.3 %collective-permute-start.7 = (bf16[8,32,1024]{2,1,0:T(8,128)(2,1)S(1)}, bf16[8,32,1024]{2,1,0:T(8,128)(2,1)S(1)}, u32[]{:S(2)}, u32[]{:S(2)}) collective-permute-start(bf16[8,32,1024]{2,1,0:T(8,128)(2,1)S(1)} %collective-permute-done.refs_7_.refs_10_), channel_id=1, source_target_pairs={{0,2},{1,3},{2,0},{3,1},{4,6},{5,7},{6,4},{7,5},{8,10},{9,11},{10,... | collective-permute-start | bytes 1572872 | tf_op jit(solution)/shard_map/ppermute | solution.py:23
  43.7 26.2 %collective-permute-start.14 = (bf16[8,32,1024]{2,1,0:T(8,128)(2,1)}, bf16[8,32,1024]{2,1,0:T(8,128)(2,1)}, u32[]{:S(2)}, u32[]{:S(2)}) collective-permute-start(bf16[8,32,1024]{2,1,0:T(8,128)(2,1)} %collective-permute-done.2.refs_11_.refs_6_), channel_id=1, source_target_pairs={{0,2},{1,3},{2,0},{3,1},{4,6},{5,7},{6,4},{7,5},{8,10},{9,11},{10,... | collective-permute-start | bytes 1572872 | tf_op jit(solution)/shard_map/ppermute | solution.py:23
  59.6 24.3 %collective-permute-start.19 = (bf16[8,8,64,128]{3,2,1,0:T(8,128)(2,1)}, bf16[8,8,64,128]{3,2,1,0:T(8,128)(2,1)}, u32[]{:S(2)}, u32[]{:S(2)}) collective-permute-start(bf16[8,8,64,128]{3,2,1,0:T(8,128)(2,1)} %all-to-all-done.2.refs_0_), channel_id=1, source_target_pairs={{0,96},{32,0},{64,32},{96,64},{1,97},{33,1},{65,33},{97,65},{2,98}... | collective-permute-start | bytes 3145736 | tf_op jit(solution)/shard_map/ppermute | solution.py:19
  61.9 17.6 %collective-permute-start.16 = (bf16[8,32,1024]{2,1,0:T(8,128)(2,1)S(1)}, bf16[8,32,1024]{2,1,0:T(8,128)(2,1)S(1)}, u32[]{:S(2)}, u32[]{:S(2)}) collective-permute-start(bf16[8,32,1024]{2,1,0:T(8,128)(2,1)S(1)} %collective-permute-done.10.refs_1_.refs_14_), channel_id=1, source_target_pairs={{0,2},{1,3},{2,0},{3,1},{4,6},{5,7},{6,4},{7,5},{8,10},{9,11},{10,... | collective-permute-start | bytes 1572872 | tf_op jit(solution)/shard_map/ppermute | solution.py:23
  62.0 31.4 %collective-permute-start.8 = (bf16[8,8,64,128]{3,2,1,0:T(8,128)(2,1)}, bf16[8,8,64,128]{3,2,1,0:T(8,128)(2,1)S(1)}, u32[]{:S(2)}, u32[]{:S(2)}) collective-permute-start(bf16[8,8,64,128]{3,2,1,0:T(8,128)(2,1)} %collective-permute-done.5.refs_1_), channel_id=1, source_target_pairs={{0,32},{32,64},{64,96},{96,0},{1,33},{33,65},{65,97},{97,1},{2,34}... | collective-permute-start | bytes 3145736 | tf_op jit(solution)/shard_map/ppermute | solution.py:19
  62.1 17.5 %collective-permute-start.13 = (bf16[8,32,1024]{2,1,0:T(8,128)(2,1)S(1)}, bf16[8,32,1024]{2,1,0:T(8,128)(2,1)S(1)}, u32[]{:S(2)}, u32[]{:S(2)}) collective-permute-start(bf16[8,32,1024]{2,1,0:T(8,128)(2,1)S(1)} %collective-permute-done.7.refs_9_.refs_12_), channel_id=1, source_target_pairs={{0,1},{1,0},{2,3},{3,2},{4,5},{5,4},{6,7},{7,6},{8,9},{9,8},{10,11... | collective-permute-start | bytes 1572872 | tf_op jit(solution)/shard_map/ppermute | solution.py:23
  69.9 11.0 %collective-permute-start.12 = (bf16[8,32,1024]{2,1,0:T(8,128)(2,1)}, bf16[8,32,1024]{2,1,0:T(8,128)(2,1)}, u32[]{:S(2)}, u32[]{:S(2)}) collective-permute-start(bf16[8,32,1024]{2,1,0:T(8,128)(2,1)} %collective-permute-done.4.refs_5_.refs_4_), channel_id=1, source_target_pairs={{0,1},{1,0},{2,3},{3,2},{4,5},{5,4},{6,7},{7,6},{8,9},{9,8},{10,11... | collective-permute-start | bytes 1572872 | tf_op jit(solution)/shard_map/ppermute | solution.py:23
  79.6 7.9 %collective-permute-start.15 = (bf16[8,32,1024]{2,1,0:T(8,128)(2,1)}, bf16[8,32,1024]{2,1,0:T(8,128)(2,1)}, u32[]{:S(2)}, u32[]{:S(2)}) collective-permute-start(bf16[8,32,1024]{2,1,0:T(8,128)(2,1)} %collective-permute-done.14.refs_13_.refs_8_), channel_id=1, source_target_pairs={{0,1},{1,0},{2,3},{3,2},{4,5},{5,4},{6,7},{7,6},{8,9},{9,8},{10,11... | collective-permute-start | bytes 1572872 | tf_op jit(solution)/shard_map/ppermute | solution.py:23
  80.4 12.9 %collective-permute-start.17 = (bf16[8,32,1024]{2,1,0:T(8,128)(2,1)S(1)}, bf16[8,32,1024]{2,1,0:T(8,128)(2,1)S(1)}, u32[]{:S(2)}, u32[]{:S(2)}) collective-permute-start(bf16[8,32,1024]{2,1,0:T(8,128)(2,1)S(1)} %collective-permute-done.16.refs_3_.refs_16_), channel_id=1, source_target_pairs={{0,1},{1,0},{2,3},{3,2},{4,5},{5,4},{6,7},{7,6},{8,9},{9,8},{10,11... | collective-permute-start | bytes 1572872 | tf_op jit(solution)/shard_map/ppermute | solution.py:23
  80.9 28.9 %collective-permute-start.18 = (bf16[8,8,64,128]{3,2,1,0:T(8,128)(2,1)}, bf16[8,8,64,128]{3,2,1,0:T(8,128)(2,1)}, u32[]{:S(2)}, u32[]{:S(2)}) collective-permute-start(bf16[8,8,64,128]{3,2,1,0:T(8,128)(2,1)} %all-to-all-done.2.refs_0_), channel_id=1, source_target_pairs={{0,32},{32,64},{64,96},{96,0},{1,33},{33,65},{65,97},{97,1},{2,34}... | collective-permute-start | bytes 3145736 | tf_op jit(solution)/shard_map/ppermute | solution.py:19
  83.9 25.9 %collective-permute-start.20 = (bf16[8,8,64,128]{3,2,1,0:T(8,128)(2,1)}, bf16[8,8,64,128]{3,2,1,0:T(8,128)(2,1)}, u32[]{:S(2)}, u32[]{:S(2)}) collective-permute-start(bf16[8,8,64,128]{3,2,1,0:T(8,128)(2,1)} %collective-permute-done.19.refs_1_), channel_id=1, source_target_pairs={{0,96},{32,0},{64,32},{96,64},{1,97},{33,1},{65,33},{97,65},{2,98}... | collective-permute-start | bytes 3145736 | tf_op jit(solution)/shard_map/ppermute | solution.py:19
  95.9 20.1 %all-to-all-start.1 = ((bf16[8,8,64,128]{3,2,1,0:T(8,128)(2,1)}), bf16[8,8,64,128]{3,2,1,0:T(8,128)(2,1)S(1)}, u32[]{:S(2)}, u32[]{:S(2)}) async-start(bf16[8,8,64,128]{3,2,1,0:T(8,128)(2,1)} %product.5), calls=%async_computation.1 | async-start | bytes 2097152 | tf_op jit(solution)/shard_map/all_to_all | solution.py:27
  116.1 19.5 %all-to-all-start.3 = ((bf16[8,8,64,128]{3,2,1,0:T(8,128)(2,1)}), bf16[8,8,64,128]{3,2,1,0:T(8,128)(2,1)S(1)}, u32[]{:S(2)}, u32[]{:S(2)}) async-start(bf16[8,8,64,128]{3,2,1,0:T(8,128)(2,1)} %product.7), calls=%async_computation.3 | async-start | bytes 2097152 | tf_op jit(solution)/shard_map/all_to_all | solution.py:27
  (11 other events, 249.3 us)
